TPU v7x, 32 devices: a whole 2x2x4 slice. The times are simulated.
32 devices in a mesh: sec: 2 (over x), gy: 4 (over z), gz: 4 (over y, core).
Axes of the slice: x: 2, y: 2, z: 4, core: 2. Of those that a mesh axis runs over, the one named last changes fastest.
Arguments:
- inflow: float32 [5, 128, 1024], P(None, 'gy', 'gz'), may hold values from -6 to 6
- initial: float32 [2, 5, 128, 1024], P('sec', None, 'gy', 'gz'), may hold values from -6 to 6
- solid: int32 [2, 128, 1024], P('sec', 'gy', 'gz'), may hold values 0 or 1
- speed_y: float32 [5], replicated, may hold values from -1 to 1
- speed_z: float32 [5], replicated, may hold values from -1 to 1
- vigneron: float32 [5], replicated, may hold values from 0.2 to 0.9
- coupling: float32 [5, 5], replicated, may hold values from -2.5 to 2.5
Outputs:
- marched: float32 [2, 5, 128, 1024], P('sec', None, 'gy', 'gz')
Inputs may be any that keep to these rules, and one draw needn't show every extreme that they name: `solid`: 1 marks a cell inside the body, 0 a fluid cell.
All inputs are finite; a program needn't handle non-finite values. No bound on the sum of `solid` on one device may be relied on, other than what follows from the above.
Results may differ from a plain program's by a relative error of at most 0.00025.
Values sent between devices are 32-bit elements; how exact they have to be, the bound alone decides.
No kernel may reach another device: no remote copies, remote signals or barrier semaphores. Data moves between devices by JAX's collectives and lax.ppermute only.
A program may use at most 64 MiB of HBM per device.

v0:
```python
import jax
import jax.numpy as jnp
from jax import lax
from jax.sharding import PartitionSpec as P

ITERS = 4
CORRECTORS = 3
NEWTON = 2


STEP_RATIO = 0.25
WENO_EPS = 1e-06


def passed_along(value, axis, steps):
    count = lax.axis_size(axis)
    initial, last = (max(0, -steps), min(count, count - steps))
    return lax.ppermute(value, axis, [(source, source + steps) for source in range(initial, last)])


def extended(block, sides, width):
    for axis, dim in sides:
        count = lax.axis_size(axis)
        forward = [(i, i + 1) for i in range(count - 1)]
        backward = [(target, source) for source, target in forward]
        low = lax.ppermute(
            lax.slice_in_dim(block, block.shape[dim] - width, None, axis=dim), axis, forward
        )
        high = lax.ppermute(lax.slice_in_dim(block, 0, width, axis=dim), axis, backward)
        block = jnp.concatenate([low, block, high], axis=dim)
    return block


def weno_face(left_far, left_near, center, right_near, right_far):
    smooth_left = (
        13.0 / 12.0 * (left_far - 2.0 * left_near + center) ** 2
        + 0.25 * (left_far - 4.0 * left_near + 3.0 * center) ** 2
    )
    smooth_middle = (
        13.0 / 12.0 * (left_near - 2.0 * center + right_near) ** 2
        + 0.25 * (left_near - right_near) ** 2
    )
    smooth_right = (
        13.0 / 12.0 * (center - 2.0 * right_near + right_far) ** 2
        + 0.25 * (3.0 * center - 4.0 * right_near + right_far) ** 2
    )
    weight_left = 0.1 / (WENO_EPS + smooth_left) ** 2
    weight_middle = 0.6 / (WENO_EPS + smooth_middle) ** 2
    weight_right = 0.3 / (WENO_EPS + smooth_right) ** 2
    guess_left = (2.0 * left_far - 7.0 * left_near + 11.0 * center) / 6.0
    guess_middle = (-left_near + 5.0 * center + 2.0 * right_near) / 6.0
    guess_right = (2.0 * center + 5.0 * right_near - right_far) / 6.0
    total = weight_left * guess_left + weight_middle * guess_middle + weight_right * guess_right
    return total / (weight_left + weight_middle + weight_right)


def sweep(padded, speeds, axis):
    count = padded.shape[axis] - 6
    plus_flux = jnp.maximum(speeds, 0.0)[:, None, None] * padded
    minus_flux = jnp.minimum(speeds, 0.0)[:, None, None] * padded

    def window(source, offset):
        return lax.slice_in_dim(source, offset, offset + count + 1, axis=axis)

    faces = weno_face(
        window(plus_flux, 0),
        window(plus_flux, 1),
        window(plus_flux, 2),
        window(plus_flux, 3),
        window(plus_flux, 4),
    )
    faces = faces + weno_face(
        window(minus_flux, 5),
        window(minus_flux, 4),
        window(minus_flux, 3),
        window(minus_flux, 2),
        window(minus_flux, 1),
    )
    return lax.slice_in_dim(faces, 1, count + 1, axis=axis) - lax.slice_in_dim(
        faces, 0, count, axis=axis
    )


def crossflow(padded, speed_y, speed_z):
    rows_part = sweep(padded[:, :, 3:-3], speed_y, 1)
    cols_part = sweep(padded[:, 3:-3, :], speed_z, 2)
    return rows_part + cols_part


def streamwise(field, factor):
    return field + factor * field**3 / (1.0 + field**2)


def slope(field, factor):
    return 1.0 + factor * field**2 * (3.0 + field**2) / (1.0 + field**2) ** 2


def correct(padded, current, upstream, diff, blocked, params):
    speed_y, speed_z, vigneron, coupling = params
    factor = vigneron[:, None, None]
    mixed = jnp.einsum("vw,wyz->vyz", coupling, current, precision=lax.Precision.HIGHEST)
    target = (
        streamwise(upstream, factor)
        - STEP_RATIO * crossflow(padded, speed_y, speed_z)
        + STEP_RATIO * mixed
        - (1.0 - factor) * diff
    )
    guess = current
    for newton_index in range(NEWTON):
        guess = guess - (streamwise(guess, factor) - target) / slope(guess, factor)
    return jnp.where(blocked[None], 0.0, guess)


def per_device(inflow, initial, solid, speed_y, speed_z, vigneron, coupling):
    params = (speed_y, speed_z, vigneron, coupling)
    sections = lax.axis_size("sec")
    position = lax.axis_index("sec")
    is_first = position == 0
    start_plane = initial[0]
    guess_above = passed_along(start_plane, "sec", 1)
    guess_above = jnp.where(is_first, inflow, guess_above)
    solid_tile = solid[0] != 0

    def station(upstream, diff):
        current = upstream
        for corrector_index in range(CORRECTORS):
            padded = extended(current, (("gy", 1), ("gz", 2)), 3)
            current = correct(padded, current, upstream, diff, solid_tile, params)
        return current

    def advance(step_index, carry):
        sent, own_prior, upstream_prior = carry
        received = passed_along(sent, "sec", 1)
        received = jnp.where(is_first, inflow, received)
        iterate = step_index - position + 1
        active = (iterate >= 1) & (iterate <= ITERS)
        updated = station(received, own_prior - upstream_prior)
        own_next = jnp.where(active, updated, own_prior)
        upstream_next = jnp.where(active, received, upstream_prior)
        return (own_next, own_next, upstream_next)

    result = lax.fori_loop(
        0, ITERS + sections - 1, advance, (start_plane, start_plane, guess_above)
    )
    return result[1][None]


def solution(mesh):
    return jax.shard_map(
        per_device,
        mesh=mesh,
        in_specs=(
            P(None, "gy", "gz"),
            P("sec", None, "gy", "gz"),
            P("sec", "gy", "gz"),
            P(),
            P(),
            P(),
            P(),
        ),
        out_specs=P("sec", None, "gy", "gz"),
        check_vma=False,
    )
```

profile of v0, /device:TPU:22, one launch (start us, length us, event | category | flops | bytes accessed | tf_op | source)
XLA Modules:
  0.0 320.1 jit_solution(16180668516495175585)
XLA Ops:
  3.0 5.7 %collective-permute-done.13 = f32[5,32,256]{2,1,0:T(8,128)S(1)} collective-permute-done((f32[5,32,256]{2,1,0:T(8,128)S(1)}, f32[5,32,256]{2,1,0:T(8,128)S(1)}, u32[]{:S(2)}, u32[]{:S(2)}) %collective-permute-start.13) | collective-permute-done | bytes 163872 | tf_op jit(solution)/shard_map/ppermute | solution.py:18
  8.8 310.6 %while.17 = (s32[]{:T(128)}, f32[5,32,256]{2,1,0:T(8,128)S(1)}, f32[5,32,256]{2,1,0:T(8,128)S(1)}, f32[5,32,256]{2,1,0:T(8,128)S(1)}, s32[]{:T(128)}, /*index=5*...) while((s32[]{:T(128)}, f32[5,32,256]{2,1,0:T(8,128)S(1)}, ...), condition=%wide.region_1.2_spmd, body=%wide.region_0.1_spmd.sunk | while | flops 46623872 | bytes 23467136 | solution.py:142
  10.2 5.9 %collective-permute-done = f32[5,32,256]{2,1,0:T(8,128)S(1)} collective-permute-done((f32[5,32,256]{2,1,0:T(8,128)S(1)}, f32[5,32,256]{2,1,0:T(8,128)S(1)}, u32[]{:S(2)}, u32[]{:S(2)}) %collective-permute-start) | collective-permute-done | bytes 163872 | tf_op jit(solution)/shard_map/while/body/eval_jaxpr/ppermute | solution.py:18
  18.5 3.5 %collective-permute-start.2 = (f32[5,3,256]{2,1,0:T(4,128)S(1)}, f32[5,3,256]{2,1,0:T(4,128)S(1)}, u32[]{:S(2)}, u32[]{:S(2)}) collective-permute-start(f32[5,3,256]{2,1,0:T(4,128)S(1)} %get-tuple-element.384), channel_id=1, source_target_pairs={{0,4},{4,8},{8,12},{1,5},{5,9},{9,13},{2,6},{6,10},{10,14},{3,7},{... | collective-permute-start | bytes 46088 | tf_op jit(solution)/shard_map/while/body/eval_jaxpr/ppermute | solution.py:26
  36.4 3.5 %collective-permute-start.6 = (f32[5,3,256]{2,1,0:T(4,128)S(1)}, f32[5,3,256]{2,1,0:T(4,128)S(1)}, u32[]{:S(2)}, u32[]{:S(2)}) collective-permute-start(f32[5,3,256]{2,1,0:T(4,128)S(1)} %get-tuple-element.395), channel_id=1, source_target_pairs={{0,4},{4,8},{8,12},{1,5},{5,9},{9,13},{2,6},{6,10},{10,14},{3,7},{... | collective-permute-start | bytes 46088 | tf_op jit(solution)/shard_map/while/body/eval_jaxpr/ppermute | solution.py:26
  52.0 3.5 %collective-permute-start.10 = (f32[5,3,256]{2,1,0:T(4,128)S(1)}, f32[5,3,256]{2,1,0:T(4,128)S(1)}, u32[]{:S(2)}, u32[]{:S(2)}) collective-permute-start(f32[5,3,256]{2,1,0:T(4,128)S(1)} %get-tuple-element.404), channel_id=1, source_target_pairs={{0,4},{4,8},{8,12},{1,5},{5,9},{9,13},{2,6},{6,10},{10,14},{3,7},{... | collective-permute-start | bytes 46088 | tf_op jit(solution)/shard_map/while/body/eval_jaxpr/ppermute | solution.py:26
  72.5 5.9 %collective-permute-done = f32[5,32,256]{2,1,0:T(8,128)S(1)} collective-permute-done((f32[5,32,256]{2,1,0:T(8,128)S(1)}, f32[5,32,256]{2,1,0:T(8,128)S(1)}, u32[]{:S(2)}, u32[]{:S(2)}) %collective-permute-start) | collective-permute-done | bytes 163872 | tf_op jit(solution)/shard_map/while/body/eval_jaxpr/ppermute | solution.py:18
  80.8 3.5 %collective-permute-start.2 = (f32[5,3,256]{2,1,0:T(4,128)S(1)}, f32[5,3,256]{2,1,0:T(4,128)S(1)}, u32[]{:S(2)}, u32[]{:S(2)}) collective-permute-start(f32[5,3,256]{2,1,0:T(4,128)S(1)} %get-tuple-element.384), channel_id=1, source_target_pairs={{0,4},{4,8},{8,12},{1,5},{5,9},{9,13},{2,6},{6,10},{10,14},{3,7},{... | collective-permute-start | bytes 46088 | tf_op jit(solution)/shard_map/while/body/eval_jaxpr/ppermute | solution.py:26
  98.4 3.9 %collective-permute-start.6 = (f32[5,3,256]{2,1,0:T(4,128)S(1)}, f32[5,3,256]{2,1,0:T(4,128)S(1)}, u32[]{:S(2)}, u32[]{:S(2)}) collective-permute-start(f32[5,3,256]{2,1,0:T(4,128)S(1)} %get-tuple-element.395), channel_id=1, source_target_pairs={{0,4},{4,8},{8,12},{1,5},{5,9},{9,13},{2,6},{6,10},{10,14},{3,7},{... | collective-permute-start | bytes 46088 | tf_op jit(solution)/shard_map/while/body/eval_jaxpr/ppermute | solution.py:26
  114.0 3.9 %collective-permute-start.10 = (f32[5,3,256]{2,1,0:T(4,128)S(1)}, f32[5,3,256]{2,1,0:T(4,128)S(1)}, u32[]{:S(2)}, u32[]{:S(2)}) collective-permute-start(f32[5,3,256]{2,1,0:T(4,128)S(1)} %get-tuple-element.404), channel_id=1, source_target_pairs={{0,4},{4,8},{8,12},{1,5},{5,9},{9,13},{2,6},{6,10},{10,14},{3,7},{... | collective-permute-start | bytes 46088 | tf_op jit(solution)/shard_map/while/body/eval_jaxpr/ppermute | solution.py:26
  120.3 3.3 %collective-permute-done.9 = f32[5,3,256]{2,1,0:T(4,128)S(1)} collective-permute-done((f32[5,3,256]{2,1,0:T(4,128)S(1)}, f32[5,3,256]{2,1,0:T(4,128)S(1)}, u32[]{:S(2)}, u32[]{:S(2)}) %collective-permute-start.9) | collective-permute-done | bytes 15392 | tf_op jit(solution)/shard_map/while/body/eval_jaxpr/ppermute | solution.py:29
  134.9 5.9 %collective-permute-done = f32[5,32,256]{2,1,0:T(8,128)S(1)} collective-permute-done((f32[5,32,256]{2,1,0:T(8,128)S(1)}, f32[5,32,256]{2,1,0:T(8,128)S(1)}, u32[]{:S(2)}, u32[]{:S(2)}) %collective-permute-start) | collective-permute-done | bytes 163872 | tf_op jit(solution)/shard_map/while/body/eval_jaxpr/ppermute | solution.py:18
  142.8 3.9 %collective-permute-start.2 = (f32[5,3,256]{2,1,0:T(4,128)S(1)}, f32[5,3,256]{2,1,0:T(4,128)S(1)}, u32[]{:S(2)}, u32[]{:S(2)}) collective-permute-start(f32[5,3,256]{2,1,0:T(4,128)S(1)} %get-tuple-element.384), channel_id=1, source_target_pairs={{0,4},{4,8},{8,12},{1,5},{5,9},{9,13},{2,6},{6,10},{10,14},{3,7},{... | collective-permute-start | bytes 46088 | tf_op jit(solution)/shard_map/while/body/eval_jaxpr/ppermute | solution.py:26
  160.3 3.9 %collective-permute-start.6 = (f32[5,3,256]{2,1,0:T(4,128)S(1)}, f32[5,3,256]{2,1,0:T(4,128)S(1)}, u32[]{:S(2)}, u32[]{:S(2)}) collective-permute-start(f32[5,3,256]{2,1,0:T(4,128)S(1)} %get-tuple-element.395), channel_id=1, source_target_pairs={{0,4},{4,8},{8,12},{1,5},{5,9},{9,13},{2,6},{6,10},{10,14},{3,7},{... | collective-permute-start | bytes 46088 | tf_op jit(solution)/shard_map/while/body/eval_jaxpr/ppermute | solution.py:26
  175.9 3.9 %collective-permute-start.10 = (f32[5,3,256]{2,1,0:T(4,128)S(1)}, f32[5,3,256]{2,1,0:T(4,128)S(1)}, u32[]{:S(2)}, u32[]{:S(2)}) collective-permute-start(f32[5,3,256]{2,1,0:T(4,128)S(1)} %get-tuple-element.404), channel_id=1, source_target_pairs={{0,4},{4,8},{8,12},{1,5},{5,9},{9,13},{2,6},{6,10},{10,14},{3,7},{... | collective-permute-start | bytes 46088 | tf_op jit(solution)/shard_map/while/body/eval_jaxpr/ppermute | solution.py:26
  182.2 3.3 %collective-permute-done.9 = f32[5,3,256]{2,1,0:T(4,128)S(1)} collective-permute-done((f32[5,3,256]{2,1,0:T(4,128)S(1)}, f32[5,3,256]{2,1,0:T(4,128)S(1)}, u32[]{:S(2)}, u32[]{:S(2)}) %collective-permute-start.9) | collective-permute-done | bytes 15392 | tf_op jit(solution)/shard_map/while/body/eval_jaxpr/ppermute | solution.py:29
  196.9 5.9 %collective-permute-done = f32[5,32,256]{2,1,0:T(8,128)S(1)} collective-permute-done((f32[5,32,256]{2,1,0:T(8,128)S(1)}, f32[5,32,256]{2,1,0:T(8,128)S(1)}, u32[]{:S(2)}, u32[]{:S(2)}) %collective-permute-start) | collective-permute-done | bytes 163872 | tf_op jit(solution)/shard_map/while/body/eval_jaxpr/ppermute | solution.py:18
  204.7 3.9 %collective-permute-start.2 = (f32[5,3,256]{2,1,0:T(4,128)S(1)}, f32[5,3,256]{2,1,0:T(4,128)S(1)}, u32[]{:S(2)}, u32[]{:S(2)}) collective-permute-start(f32[5,3,256]{2,1,0:T(4,128)S(1)} %get-tuple-element.384), channel_id=1, source_target_pairs={{0,4},{4,8},{8,12},{1,5},{5,9},{9,13},{2,6},{6,10},{10,14},{3,7},{... | collective-permute-start | bytes 46088 | tf_op jit(solution)/shard_map/while/body/eval_jaxpr/ppermute | solution.py:26
  222.2 3.9 %collective-permute-start.6 = (f32[5,3,256]{2,1,0:T(4,128)S(1)}, f32[5,3,256]{2,1,0:T(4,128)S(1)}, u32[]{:S(2)}, u32[]{:S(2)}) collective-permute-start(f32[5,3,256]{2,1,0:T(4,128)S(1)} %get-tuple-element.395), channel_id=1, source_target_pairs={{0,4},{4,8},{8,12},{1,5},{5,9},{9,13},{2,6},{6,10},{10,14},{3,7},{... | collective-permute-start | bytes 46088 | tf_op jit(solution)/shard_map/while/body/eval_jaxpr/ppermute | solution.py:26
  237.9 3.9 %collective-permute-start.10 = (f32[5,3,256]{2,1,0:T(4,128)S(1)}, f32[5,3,256]{2,1,0:T(4,128)S(1)}, u32[]{:S(2)}, u32[]{:S(2)}) collective-permute-start(f32[5,3,256]{2,1,0:T(4,128)S(1)} %get-tuple-element.404), channel_id=1, source_target_pairs={{0,4},{4,8},{8,12},{1,5},{5,9},{9,13},{2,6},{6,10},{10,14},{3,7},{... | collective-permute-start | bytes 46088 | tf_op jit(solution)/shard_map/while/body/eval_jaxpr/ppermute | solution.py:26
  258.8 5.9 %collective-permute-done = f32[5,32,256]{2,1,0:T(8,128)S(1)} collective-permute-done((f32[5,32,256]{2,1,0:T(8,128)S(1)}, f32[5,32,256]{2,1,0:T(8,128)S(1)}, u32[]{:S(2)}, u32[]{:S(2)}) %collective-permute-start) | collective-permute-done | bytes 163872 | tf_op jit(solution)/shard_map/while/body/eval_jaxpr/ppermute | solution.py:18
  266.7 3.9 %collective-permute-start.2 = (f32[5,3,256]{2,1,0:T(4,128)S(1)}, f32[5,3,256]{2,1,0:T(4,128)S(1)}, u32[]{:S(2)}, u32[]{:S(2)}) collective-permute-start(f32[5,3,256]{2,1,0:T(4,128)S(1)} %get-tuple-element.384), channel_id=1, source_target_pairs={{0,4},{4,8},{8,12},{1,5},{5,9},{9,13},{2,6},{6,10},{10,14},{3,7},{... | collective-permute-start | bytes 46088 | tf_op jit(solution)/shard_map/while/body/eval_jaxpr/ppermute | solution.py:26
  284.2 3.9 %collective-permute-start.6 = (f32[5,3,256]{2,1,0:T(4,128)S(1)}, f32[5,3,256]{2,1,0:T(4,128)S(1)}, u32[]{:S(2)}, u32[]{:S(2)}) collective-permute-start(f32[5,3,256]{2,1,0:T(4,128)S(1)} %get-tuple-element.395), channel_id=1, source_target_pairs={{0,4},{4,8},{8,12},{1,5},{5,9},{9,13},{2,6},{6,10},{10,14},{3,7},{... | collective-permute-start | bytes 46088 | tf_op jit(solution)/shard_map/while/body/eval_jaxpr/ppermute | solution.py:26
  299.8 3.9 %collective-permute-start.10 = (f32[5,3,256]{2,1,0:T(4,128)S(1)}, f32[5,3,256]{2,1,0:T(4,128)S(1)}, u32[]{:S(2)}, u32[]{:S(2)}) collective-permute-start(f32[5,3,256]{2,1,0:T(4,128)S(1)} %get-tuple-element.404), channel_id=1, source_target_pairs={{0,4},{4,8},{8,12},{1,5},{5,9},{9,13},{2,6},{6,10},{10,14},{3,7},{... | collective-permute-start | bytes 46088 | tf_op jit(solution)/shard_map/while/body/eval_jaxpr/ppermute | solution.py:26
  (277 shorter events, 219.6 us)
Async XLA Ops:
  0.9 7.8 %collective-permute-start.13 = (f32[5,32,256]{2,1,0:T(8,128)S(1)}, f32[5,32,256]{2,1,0:T(8,128)S(1)}, u32[]{:S(2)}, u32[]{:S(2)}) collective-permute-start(f32[5,32,256]{2,1,0:T(8,128)S(1)} %bitcast.41), channel_id=1, source_target_pairs={{0,16},{1,17},{2,18},{3,19},{4,20},{5,21},{6,22},{7,23},{8,24},{9,... | collective-permute-start | bytes 491528 | tf_op jit(solution)/shard_map/ppermute | solution.py:18
  8.8 7.2 %collective-permute-start = (f32[5,32,256]{2,1,0:T(8,128)S(1)}, f32[5,32,256]{2,1,0:T(8,128)S(1)}, u32[]{:S(2)}, u32[]{:S(2)}) collective-permute-start(f32[5,32,256]{2,1,0:T(8,128)S(1)} %get-tuple-element.428), channel_id=1, source_target_pairs={{0,16},{1,17},{2,18},{3,19},{4,20},{5,21},{6,22},{7,23},{8,24},{9,... | collective-permute-start | bytes 491528 | tf_op jit(solution)/shard_map/while/body/eval_jaxpr/ppermute | solution.py:18
  16.1 6.3 %collective-permute-start.1 = (f32[5,3,256]{2,1,0:T(4,128)S(1)}, f32[5,3,256]{2,1,0:T(4,128)S(1)}, u32[]{:S(2)}, u32[]{:S(2)}) collective-permute-start(f32[5,3,256]{2,1,0:T(4,128)S(1)} %get-tuple-element.383), channel_id=1, source_target_pairs={{4,0},{8,4},{12,8},{5,1},{9,5},{13,9},{6,2},{10,6},{14,10},{7,3},{... | collective-permute-start | bytes 46088 | tf_op jit(solution)/shard_map/while/body/eval_jaxpr/ppermute | solution.py:29
  34.0 6.3 %collective-permute-start.5 = (f32[5,3,256]{2,1,0:T(4,128)S(1)}, f32[5,3,256]{2,1,0:T(4,128)S(1)}, u32[]{:S(2)}, u32[]{:S(2)}) collective-permute-start(f32[5,3,256]{2,1,0:T(4,128)S(1)} %get-tuple-element.394), channel_id=1, source_target_pairs={{4,0},{8,4},{12,8},{5,1},{9,5},{13,9},{6,2},{10,6},{14,10},{7,3},{... | collective-permute-start | bytes 46088 | tf_op jit(solution)/shard_map/while/body/eval_jaxpr/ppermute | solution.py:29
  52.0 6.3 %collective-permute-start.10 = (f32[5,3,256]{2,1,0:T(4,128)S(1)}, f32[5,3,256]{2,1,0:T(4,128)S(1)}, u32[]{:S(2)}, u32[]{:S(2)}) collective-permute-start(f32[5,3,256]{2,1,0:T(4,128)S(1)} %get-tuple-element.404), channel_id=1, source_target_pairs={{0,4},{4,8},{8,12},{1,5},{5,9},{9,13},{2,6},{6,10},{10,14},{3,7},{... | collective-permute-start | bytes 46088 | tf_op jit(solution)/shard_map/while/body/eval_jaxpr/ppermute | solution.py:26
  63.3 6.0 %collective-permute-start.12 = (f32[5,38,3]{2,1,0:T(8,128)S(1)}, f32[5,38,3]{2,1,0:T(8,128)S(1)}, u32[]{:S(2)}, u32[]{:S(2)}) collective-permute-start(f32[5,38,3]{2,1,0:T(8,128)S(1)} %get-tuple-element.407), channel_id=1, source_target_pairs={{0,1},{1,2},{2,3},{4,5},{5,6},{6,7},{8,9},{9,10},{10,11},{12,13},{... | collective-permute-start | bytes 6848 | tf_op jit(solution)/shard_map/while/body/eval_jaxpr/ppermute | solution.py:26
  71.2 7.2 %collective-permute-start = (f32[5,32,256]{2,1,0:T(8,128)S(1)}, f32[5,32,256]{2,1,0:T(8,128)S(1)}, u32[]{:S(2)}, u32[]{:S(2)}) collective-permute-start(f32[5,32,256]{2,1,0:T(8,128)S(1)} %get-tuple-element.428), channel_id=1, source_target_pairs={{0,16},{1,17},{2,18},{3,19},{4,20},{5,21},{6,22},{7,23},{8,24},{9,... | collective-permute-start | bytes 491528 | tf_op jit(solution)/shard_map/while/body/eval_jaxpr/ppermute | solution.py:18
  78.5 6.3 %collective-permute-start.1 = (f32[5,3,256]{2,1,0:T(4,128)S(1)}, f32[5,3,256]{2,1,0:T(4,128)S(1)}, u32[]{:S(2)}, u32[]{:S(2)}) collective-permute-start(f32[5,3,256]{2,1,0:T(4,128)S(1)} %get-tuple-element.383), channel_id=1, source_target_pairs={{4,0},{8,4},{12,8},{5,1},{9,5},{13,9},{6,2},{10,6},{14,10},{7,3},{... | collective-permute-start | bytes 46088 | tf_op jit(solution)/shard_map/while/body/eval_jaxpr/ppermute | solution.py:29
  88.6 6.0 %collective-permute-start.4 = (f32[5,38,3]{2,1,0:T(8,128)S(1)}, f32[5,38,3]{2,1,0:T(8,128)S(1)}, u32[]{:S(2)}, u32[]{:S(2)}) collective-permute-start(f32[5,38,3]{2,1,0:T(8,128)S(1)} %get-tuple-element.388), channel_id=1, source_target_pairs={{0,1},{1,2},{2,3},{4,5},{5,6},{6,7},{8,9},{9,10},{10,11},{12,13},{... | collective-permute-start | bytes 6848 | tf_op jit(solution)/shard_map/while/body/eval_jaxpr/ppermute | solution.py:26
  96.4 6.3 %collective-permute-start.5 = (f32[5,3,256]{2,1,0:T(4,128)S(1)}, f32[5,3,256]{2,1,0:T(4,128)S(1)}, u32[]{:S(2)}, u32[]{:S(2)}) collective-permute-start(f32[5,3,256]{2,1,0:T(4,128)S(1)} %get-tuple-element.394), channel_id=1, source_target_pairs={{4,0},{8,4},{12,8},{5,1},{9,5},{13,9},{6,2},{10,6},{14,10},{7,3},{... | collective-permute-start | bytes 46088 | tf_op jit(solution)/shard_map/while/body/eval_jaxpr/ppermute | solution.py:29
  114.0 6.3 %collective-permute-start.10 = (f32[5,3,256]{2,1,0:T(4,128)S(1)}, f32[5,3,256]{2,1,0:T(4,128)S(1)}, u32[]{:S(2)}, u32[]{:S(2)}) collective-permute-start(f32[5,3,256]{2,1,0:T(4,128)S(1)} %get-tuple-element.404), channel_id=1, source_target_pairs={{0,4},{4,8},{8,12},{1,5},{5,9},{9,13},{2,6},{6,10},{10,14},{3,7},{... | collective-permute-start | bytes 46088 | tf_op jit(solution)/shard_map/while/body/eval_jaxpr/ppermute | solution.py:26
  133.6 7.2 %collective-permute-start = (f32[5,32,256]{2,1,0:T(8,128)S(1)}, f32[5,32,256]{2,1,0:T(8,128)S(1)}, u32[]{:S(2)}, u32[]{:S(2)}) collective-permute-start(f32[5,32,256]{2,1,0:T(8,128)S(1)} %get-tuple-element.428), channel_id=1, source_target_pairs={{0,16},{1,17},{2,18},{3,19},{4,20},{5,21},{6,22},{7,23},{8,24},{9,... | collective-permute-start | bytes 491528 | tf_op jit(solution)/shard_map/while/body/eval_jaxpr/ppermute | solution.py:18
  140.8 6.3 %collective-permute-start.1 = (f32[5,3,256]{2,1,0:T(4,128)S(1)}, f32[5,3,256]{2,1,0:T(4,128)S(1)}, u32[]{:S(2)}, u32[]{:S(2)}) collective-permute-start(f32[5,3,256]{2,1,0:T(4,128)S(1)} %get-tuple-element.383), channel_id=1, source_target_pairs={{4,0},{8,4},{12,8},{5,1},{9,5},{13,9},{6,2},{10,6},{14,10},{7,3},{... | collective-permute-start | bytes 46088 | tf_op jit(solution)/shard_map/while/body/eval_jaxpr/ppermute | solution.py:29
  150.6 6.0 %collective-permute-start.4 = (f32[5,38,3]{2,1,0:T(8,128)S(1)}, f32[5,38,3]{2,1,0:T(8,128)S(1)}, u32[]{:S(2)}, u32[]{:S(2)}) collective-permute-start(f32[5,38,3]{2,1,0:T(8,128)S(1)} %get-tuple-element.388), channel_id=1, source_target_pairs={{0,1},{1,2},{2,3},{4,5},{5,6},{6,7},{8,9},{9,10},{10,11},{12,13},{... | collective-permute-start | bytes 6848 | tf_op jit(solution)/shard_map/while/body/eval_jaxpr/ppermute | solution.py:26
  158.4 6.3 %collective-permute-start.5 = (f32[5,3,256]{2,1,0:T(4,128)S(1)}, f32[5,3,256]{2,1,0:T(4,128)S(1)}, u32[]{:S(2)}, u32[]{:S(2)}) collective-permute-start(f32[5,3,256]{2,1,0:T(4,128)S(1)} %get-tuple-element.394), channel_id=1, source_target_pairs={{4,0},{8,4},{12,8},{5,1},{9,5},{13,9},{6,2},{10,6},{14,10},{7,3},{... | collective-permute-start | bytes 46088 | tf_op jit(solution)/shard_map/while/body/eval_jaxpr/ppermute | solution.py:29
  175.9 6.3 %collective-permute-start.10 = (f32[5,3,256]{2,1,0:T(4,128)S(1)}, f32[5,3,256]{2,1,0:T(4,128)S(1)}, u32[]{:S(2)}, u32[]{:S(2)}) collective-permute-start(f32[5,3,256]{2,1,0:T(4,128)S(1)} %get-tuple-element.404), channel_id=1, source_target_pairs={{0,4},{4,8},{8,12},{1,5},{5,9},{9,13},{2,6},{6,10},{10,14},{3,7},{... | collective-permute-start | bytes 46088 | tf_op jit(solution)/shard_map/while/body/eval_jaxpr/ppermute | solution.py:26
  195.5 7.2 %collective-permute-start = (f32[5,32,256]{2,1,0:T(8,128)S(1)}, f32[5,32,256]{2,1,0:T(8,128)S(1)}, u32[]{:S(2)}, u32[]{:S(2)}) collective-permute-start(f32[5,32,256]{2,1,0:T(8,128)S(1)} %get-tuple-element.428), channel_id=1, source_target_pairs={{0,16},{1,17},{2,18},{3,19},{4,20},{5,21},{6,22},{7,23},{8,24},{9,... | collective-permute-start | bytes 491528 | tf_op jit(solution)/shard_map/while/body/eval_jaxpr/ppermute | solution.py:18
  202.8 6.3 %collective-permute-start.1 = (f32[5,3,256]{2,1,0:T(4,128)S(1)}, f32[5,3,256]{2,1,0:T(4,128)S(1)}, u32[]{:S(2)}, u32[]{:S(2)}) collective-permute-start(f32[5,3,256]{2,1,0:T(4,128)S(1)} %get-tuple-element.383), channel_id=1, source_target_pairs={{4,0},{8,4},{12,8},{5,1},{9,5},{13,9},{6,2},{10,6},{14,10},{7,3},{... | collective-permute-start | bytes 46088 | tf_op jit(solution)/shard_map/while/body/eval_jaxpr/ppermute | solution.py:29
  220.3 6.3 %collective-permute-start.5 = (f32[5,3,256]{2,1,0:T(4,128)S(1)}, f32[5,3,256]{2,1,0:T(4,128)S(1)}, u32[]{:S(2)}, u32[]{:S(2)}) collective-permute-start(f32[5,3,256]{2,1,0:T(4,128)S(1)} %get-tuple-element.394), channel_id=1, source_target_pairs={{4,0},{8,4},{12,8},{5,1},{9,5},{13,9},{6,2},{10,6},{14,10},{7,3},{... | collective-permute-start | bytes 46088 | tf_op jit(solution)/shard_map/while/body/eval_jaxpr/ppermute | solution.py:29
  237.9 6.3 %collective-permute-start.10 = (f32[5,3,256]{2,1,0:T(4,128)S(1)}, f32[5,3,256]{2,1,0:T(4,128)S(1)}, u32[]{:S(2)}, u32[]{:S(2)}) collective-permute-start(f32[5,3,256]{2,1,0:T(4,128)S(1)} %get-tuple-element.404), channel_id=1, source_target_pairs={{0,4},{4,8},{8,12},{1,5},{5,9},{9,13},{2,6},{6,10},{10,14},{3,7},{... | collective-permute-start | bytes 46088 | tf_op jit(solution)/shard_map/while/body/eval_jaxpr/ppermute | solution.py:26
  257.5 7.2 %collective-permute-start = (f32[5,32,256]{2,1,0:T(8,128)S(1)}, f32[5,32,256]{2,1,0:T(8,128)S(1)}, u32[]{:S(2)}, u32[]{:S(2)}) collective-permute-start(f32[5,32,256]{2,1,0:T(8,128)S(1)} %get-tuple-element.428), channel_id=1, source_target_pairs={{0,16},{1,17},{2,18},{3,19},{4,20},{5,21},{6,22},{7,23},{8,24},{9,... | collective-permute-start | bytes 491528 | tf_op jit(solution)/shard_map/while/body/eval_jaxpr/ppermute | solution.py:18
  264.7 6.3 %collective-permute-start.1 = (f32[5,3,256]{2,1,0:T(4,128)S(1)}, f32[5,3,256]{2,1,0:T(4,128)S(1)}, u32[]{:S(2)}, u32[]{:S(2)}) collective-permute-start(f32[5,3,256]{2,1,0:T(4,128)S(1)} %get-tuple-element.383), channel_id=1, source_target_pairs={{4,0},{8,4},{12,8},{5,1},{9,5},{13,9},{6,2},{10,6},{14,10},{7,3},{... | collective-permute-start | bytes 46088 | tf_op jit(solution)/shard_map/while/body/eval_jaxpr/ppermute | solution.py:29
  282.3 6.3 %collective-permute-start.5 = (f32[5,3,256]{2,1,0:T(4,128)S(1)}, f32[5,3,256]{2,1,0:T(4,128)S(1)}, u32[]{:S(2)}, u32[]{:S(2)}) collective-permute-start(f32[5,3,256]{2,1,0:T(4,128)S(1)} %get-tuple-element.394), channel_id=1, source_target_pairs={{4,0},{8,4},{12,8},{5,1},{9,5},{13,9},{6,2},{10,6},{14,10},{7,3},{... | collective-permute-start | bytes 46088 | tf_op jit(solution)/shard_map/while/body/eval_jaxpr/ppermute | solution.py:29
  299.8 6.3 %collective-permute-start.10 = (f32[5,3,256]{2,1,0:T(4,128)S(1)}, f32[5,3,256]{2,1,0:T(4,128)S(1)}, u32[]{:S(2)}, u32[]{:S(2)}) collective-permute-start(f32[5,3,256]{2,1,0:T(4,128)S(1)} %get-tuple-element.404), channel_id=1, source_target_pairs={{0,4},{4,8},{8,12},{1,5},{5,9},{9,13},{2,6},{6,10},{10,14},{3,7},{... | collective-permute-start | bytes 46088 | tf_op jit(solution)/shard_map/while/body/eval_jaxpr/ppermute | solution.py:26
  (49 other events, 268.7 us)
where the time goes:
time: 322 us; the launch traced here: 320 us
  starting transfers between devices  160 us (50%)
  waiting for transfers between devices  103 us (32%)
  other arithmetic  44.3 us (14%)
  matrix products  6.61 us (2%)
  local copies, waits for them, and re-layouts  3.91 us (1%)
    ppermute x30, starting transfers between devices, extended(): lax.ppermute(lax.slice_in_dim(block, block.shape[dim] - width, None, axis...  93.1 us
    ppermute x30, starting transfers between devices, extended(): lax.ppermute(lax.slice_in_dim(block, 0, width, axis=dim), axis, backward)  59.4 us
    ppermute x30, waiting for transfers between devices, extended(): lax.ppermute(lax.slice_in_dim(block, block.shape[dim] - width, None, axis...  52 us
    ppermute x6, waiting for transfers between devices, passed_along(): lax.ppermute(value, axis, [(source, source + steps) for source in range(i...  35 us
    add x30, other arithmetic, sweep(): faces + weno_face(window(minus_flux, 5), window(minus_flux, 4), window(mi...  34 us
    ppermute x30, waiting for transfers between devices, extended(): lax.ppermute(lax.slice_in_dim(block, 0, width, axis=dim), axis, backward)  16.1 us
    ppermute x6, starting transfers between devices, passed_along(): lax.ppermute(value, axis, [(source, source + steps) for source in range(i...  7.74 us
    dot_general x15, matrix products, correct(): jnp.einsum('vw,wyz->vyz', coupling, current, precision=lax.Precision.HIGH...  6.61 us
  transfers between devices with their start and end apart: 66, of which 36 were waited for; matrix products, arithmetic and copies ran while one was open for 7% of the time, Pallas kernels for 0%

commit v1 on v0

--- a/solution.py
+++ b/solution.py
@@ -1,12 +1,16 @@
+import functools
+
 import jax
 import jax.numpy as jnp
 from jax import lax
+from jax.experimental import pallas as pl
+from jax.experimental.pallas import tpu as pltpu
 from jax.sharding import PartitionSpec as P
 
+NVAR = 5
 ITERS = 4
 CORRECTORS = 3
 NEWTON = 2
-
 
 STEP_RATIO = 0.25
 WENO_EPS = 1e-06
@@ -62,20 +66,8 @@
     def window(source, offset):
         return lax.slice_in_dim(source, offset, offset + count + 1, axis=axis)
 
-    faces = weno_face(
-        window(plus_flux, 0),
-        window(plus_flux, 1),
-        window(plus_flux, 2),
-        window(plus_flux, 3),
-        window(plus_flux, 4),
-    )
-    faces = faces + weno_face(
-        window(minus_flux, 5),
-        window(minus_flux, 4),
-        window(minus_flux, 3),
-        window(minus_flux, 2),
-        window(minus_flux, 1),
-    )
+    faces = weno_face(*(window(plus_flux, i) for i in (0, 1, 2, 3, 4)))
+    faces = faces + weno_face(*(window(minus_flux, i) for i in (5, 4, 3, 2, 1)))
     return lax.slice_in_dim(faces, 1, count + 1, axis=axis) - lax.slice_in_dim(
         faces, 0, count, axis=axis
     )
@@ -145,9 +137,498 @@
     return result[1][None]
 
 
+LANES = 128
+SLAB = 32
+TILE = 256
+MEMBERS = 8
+PIECE = 32
+GUARD = 16
+LEFT = 40
+ROWS = GUARD + LEFT + SLAB + LEFT + GUARD
+CHUNK_IN = 72
+CHUNK_OUT = 40
+NEAR = 24
+EDGE_ONE = 11 * SLAB + 6 * NEAR
+EDGE_TWO = 11 * 8
+CHANNELS = 17
+
+
+def lane_iota():
+    return lax.broadcasted_iota(jnp.int32, (8, LANES), 1)
+
+
+def turned(value, shift):
+    shift = shift % LANES
+    return value if shift == 0 else pltpu.roll(value, shift, 1)
+
+
+def slab_of(member, odd):
+    sec, gy = member // 4, member % 4
+    j = 2 * gy + (sec ^ (gy & 1))
+    return jnp.where(odd, MEMBERS - 1 - j, j)
+
+
+def pack_kernel(place, inflow, initial, solid, out, stacked, turned_ref, solids):
+    sec, odd = place[0], place[1] == 1
+    for group in range(2):
+        for p in range(4):
+            rows = pl.ds(p * PIECE, PIECE)
+            if group == 0:
+                stacked[rows, :] = initial[0, p]
+            elif p == 0:
+                stacked[rows, :] = initial[0, 4]
+            else:
+                stacked[rows, :] = inflow[jnp.minimum(3 * sec + p - 1, NVAR - 1)]
+        for half in range(2):
+            turned_ref[pl.ds(half * LANES, LANES), :] = stacked[:, half * LANES:(half + 1) * LANES].T
+        for member in range(MEMBERS):
+            j = slab_of(member, odd)
+            out[member, pl.ds(group * SLAB, SLAB), :] = turned_ref[
+                pl.ds(pl.multiple_of(j * SLAB, SLAB), SLAB), :
+            ]
+    solids[...] = jnp.zeros_like(solids)
+    for half in range(2):
+        solids[pl.ds(half * PIECE, PIECE), :] = solid[
+            0, :, half * LANES:(half + 1) * LANES
+        ].astype(jnp.float32)
+    turned_ref[pl.ds(0, LANES), :] = solids[...].T
+    quarter = lane_iota() // PIECE
+    for member in range(MEMBERS):
+        j = slab_of(member, odd)
+        half, within = j // 4, j % 4
+        packed = jnp.zeros((8, LANES), jnp.float32)
+        for octet in range(4):
+            piece = turned_ref[pl.ds(pl.multiple_of(within * SLAB + octet * 8, 8), 8), :]
+            piece = pltpu.roll(piece, (PIECE * (octet - half)) % LANES, 1)
+            packed = jnp.where(quarter == octet, piece, packed)
+        out[member, pl.ds(2 * SLAB, 8), :] = packed
+
+
+def assemble_kernel(got, own, right_one, left_one, right_two, left_two):
+    quarter = lane_iota() // PIECE
+
+    def gathered(sec, row, shift):
+        value = None
+        for gy in range(4):
+            piece = turned(got[sec * 4 + gy, pl.ds(row, 8), :], PIECE * gy - shift)
+            value = piece if value is None else jnp.where(quarter == gy, piece, value)
+        return value
+
+    def source(channel, octet):
+        if channel < 3:
+            return gathered(0, SLAB + 8 * octet, PIECE * (channel + 1))
+        if channel < 5:
+            return gathered(1, SLAB + 8 * octet, PIECE * (channel - 2))
+        sec, v = (channel - 5) // 6, (channel - 5) % 6
+        if v < 4:
+            return gathered(sec, 8 * octet, PIECE * v)
+        if v == 4:
+            return gathered(sec, SLAB + 8 * octet, 0)
+        return gathered(sec, 2 * SLAB, PIECE * octet)
+
+    for channel in range(CHANNELS):
+        for octet in range(4):
+            value = source(channel, octet)
+            own[channel, pl.ds(8 * octet, 8), :] = value
+            if channel < 11:
+                rows = pl.ds(channel * SLAB + 8 * octet, 8)
+                right_one[rows, :] = value
+                left_one[rows, :] = value
+                if octet == 3:
+                    right_two[pl.ds(8 * channel, 8), :] = value
+                if octet == 0:
+                    left_two[pl.ds(8 * channel, 8), :] = value
+            else:
+                at = 11 * SLAB + (channel - 11) * NEAR
+                if octet > 0:
+                    right_one[pl.ds(at + 8 * (octet - 1), 8), :] = value
+                if octet < 3:
+                    left_one[pl.ds(at + 8 * octet, 8), :] = value
+
+
+def unpack_kernel(place, got, out, stacked, packed):
+    odd = place[1] == 1
+    quarter = lane_iota() // PIECE
+
+    def member_of(j):
+        j = jnp.where(odd, MEMBERS - 1 - j, j)
+        gy = j // 2
+        sec = (j % 2 + gy % 2) % 2
+        return sec * 4 + gy
+
+    for half in range(2):
+        for within in range(4):
+            member = member_of(4 * half + within)
+            stacked[pl.ds(within * SLAB, SLAB), :] = got[member, pl.ds(0, SLAB), :]
+        block = stacked[...].T
+        for v in range(4):
+            out[0, v, :, half * LANES:(half + 1) * LANES] = block[v * PIECE:(v + 1) * PIECE]
+    for within in range(4):
+        low = got[member_of(within), pl.ds(SLAB, 8), :]
+        high = got[member_of(4 + within), pl.ds(SLAB, 8), :]
+        for octet in range(4):
+            packed[pl.ds(within * SLAB + 8 * octet, 8), :] = jnp.where(
+                quarter == 0, turned(low, -PIECE * octet), turned(high, PIECE - PIECE * octet)
+            )
+    block = packed[...].T
+    for half in range(2):
+        out[0, 4, :, half * LANES:(half + 1) * LANES] = block[half * PIECE:(half + 1) * PIECE]
+
+
+def weighted(d1, d2, d3, d4, t1, t2, t3):
+    a = 3.0 * d2 - d1
+    b = d2 + d3
+    c = 3.0 * d3 - d4
+    y1 = pltpu.reciprocal(t1 + a * a, approx=True)
+    y2 = pltpu.reciprocal(t2 + b * b, approx=True)
+    y3 = pltpu.reciprocal(t3 + c * c, approx=True)
+    g1, g2, g3 = y1 * y1, y2 * y2, y3 * y3
+    p1 = (a + a - d2) * (1.0 / 6.0)
+    p2 = b + d3
+    p3 = (c + d3) * 0.5
+    over = g1 * p1 + g2 * p2 + g3 * p3
+    under = g1 + 6.0 * g2 + 3.0 * g3
+    return over * pltpu.reciprocal(under, approx=True)
+
+
+def main_kernel(
+    place, speed_y, speed_z, vigneron, coupling,
+    own, from_left, from_right, from_left_two, from_right_two,
+    out,
+    inf, still, base, first, second, s0, s1, work_inf, delta, curve, face, blocked, start1,
+):
+    lane = lane_iota()
+    center = GUARD + LEFT
+
+    def fill(ref, index, channel, wide):
+        ref = ref.at[index] if index is not None else ref
+        ref[pl.ds(0, GUARD), :] = jnp.zeros((GUARD, LANES), jnp.float32)
+        ref[pl.ds(ROWS - GUARD, GUARD), :] = jnp.zeros((GUARD, LANES), jnp.float32)
+        ref[pl.ds(center, SLAB), :] = own[channel]
+        if wide:
+            ref[pl.ds(GUARD, 8), :] = from_left_two[pl.ds(8 * channel, 8), :]
+            ref[pl.ds(GUARD + 8, SLAB), :] = from_left[pl.ds(SLAB * channel, SLAB), :]
+            ref[pl.ds(center + SLAB, SLAB), :] = from_right[pl.ds(SLAB * channel, SLAB), :]
+            ref[pl.ds(center + 2 * SLAB, 8), :] = from_right_two[pl.ds(8 * channel, 8), :]
+        else:
+            at = 11 * SLAB + (channel - 11) * NEAR
+            zeros = jnp.zeros((16, LANES), jnp.float32)
+            ref[pl.ds(GUARD, 16), :] = zeros
+            ref[pl.ds(center - NEAR, NEAR), :] = from_left[pl.ds(at, NEAR), :]
+            ref[pl.ds(center + SLAB, NEAR), :] = from_right[pl.ds(at, NEAR), :]
+            ref[pl.ds(center + SLAB + NEAR, 16), :] = zeros
+
+    for v in range(NVAR):
+        fill(inf, v, v, True)
+        fill(s0.at[0], v, 5 + v, True)
+        fill(s1, v, 11 + v, False)
+    fill(blocked, 0, 10, True)
+    fill(blocked, 1, 16, False)
+    slab, last = place[2], place[3]
+    for octet in range(ROWS // 8):
+        rows = pl.ds(8 * octet, 8)
+        column = slab * SLAB + 8 * octet - center + lax.broadcasted_iota(jnp.int32, (8, LANES), 0)
+        outside = (column < 0) | (column >= last)
+        for station in range(2):
+            blocked[station, rows, :] = jnp.where(
+                outside | (blocked[station, rows, :] != 0.0), 0.0, 1.0
+            )
+    for ref in (first, second, s0.at[1]):
+        for v in range(NVAR):
+            ref[v] = jnp.zeros((ROWS, LANES), jnp.float32)
+
+    sy = [speed_y[v] for v in range(NVAR)]
+    sz = [speed_z[v] for v in range(NVAR)]
+    half_y = [0.5 * jnp.maximum(s, -s) for s in sy]
+    half_z = [0.5 * jnp.maximum(s, -s) for s in sz]
+    step_z = [jnp.where(s >= 0.0, 1, -1) for s in sz]
+    turn_y = [jnp.where(s >= 0.0, 1, LANES - 1) for s in sy]
+    back_y = [jnp.where(s >= 0.0, LANES - 1, 1) for s in sy]
+    wind_y = [jnp.where(s >= 0.0, 0, LANES - 1) for s in sy]
+    minus_y = [jnp.where(s >= 0.0, 0, 1) for s in sy]
+    vig = [vigneron[v] for v in range(NVAR)]
+
+    def newton(v, guess, target):
+        for _ in range(NEWTON):
+            r = pltpu.reciprocal(1.0 + guess * guess, approx=True)
+            z = (2.0 * vig[v]) * r
+            over = (z * (1.0 - r)) * guess + target
+            under = z * (0.5 - r) + (1.0 + vig[v])
+            guess = over * pltpu.reciprocal(under, approx=True)
+        return guess
+
+    def energy(v, field):
+        r = pltpu.reciprocal(1.0 + field * field, approx=True)
+        return field * ((1.0 + vig[v]) - vig[v] * r)
+
+    def octet_rows(g):
+        return pl.multiple_of(GUARD + 8 * g, 8)
+
+    def pairs(g0, extra, body, carry):
+        def two(i, c):
+            for k in range(2):
+                c = body(g0 - extra + 2 * i + k, c)
+            return c
+        return lax.fori_loop(0, 7 - g0 + extra, two, carry)
+
+    def fluxes(src, g0):
+        def differ(g, carry):
+            at = octet_rows(g)
+            packed = []
+            for v in range(NVAR):
+                here = src[v, pl.ds(at, 8), :]
+                down = src[v, pl.ds(at + step_z[v], 8), :]
+                up = src[v, pl.ds(at - step_z[v], 8), :]
+                d = (down - here) * half_z[v]
+                t = d - (here - up) * half_z[v]
+                delta[v, pl.ds(at, 8), :] = d
+                curve[v, pl.ds(at, 8), :] = (13.0 / 3.0) * (t * t) + WENO_EPS
+                edge = pltpu.roll(here, (2 * g + 2 * minus_y[v]) & (LANES - 1), 1)
+                packed.append(jnp.where(lane // 2 == g, edge, carry[v]))
+            return tuple(packed)
+
+        zero = jnp.zeros((8, LANES), jnp.float32)
+        edges = pairs(g0, 1, differ, (zero,) * NVAR)
+
+        entry = []
+        for v in range(NVAR):
+            u = edges[v] * half_y[v]
+            d4 = pltpu.roll(u, back_y[v], 1) - u
+            t3 = d4 - u
+            flat = jnp.full((8, LANES), WENO_EPS, jnp.float32)
+            entry.append(weighted(
+                zero, zero, u, d4, flat,
+                (13.0 / 3.0) * (u * u) + WENO_EPS, (13.0 / 3.0) * (t3 * t3) + WENO_EPS,
+            ))
+
+        def across(g, carry):
+            at = octet_rows(g)
+            for v in range(NVAR):
+                s = step_z[v]
+                d3 = delta[v, pl.ds(at, 8), :]
+                d2 = delta[v, pl.ds(at - s, 8), :]
+                d1 = delta[v, pl.ds(at - 2 * s, 8), :]
+                d4 = delta[v, pl.ds(at + s, 8), :]
+                t1 = curve[v, pl.ds(at - s, 8), :]
+                t2 = curve[v, pl.ds(at, 8), :]
+                t3 = curve[v, pl.ds(at + s, 8), :]
+                face[v, pl.ds(at, 8), :] = half_z[v] * src[v, pl.ds(at, 8), :] + weighted(
+                    d1, d2, d3, d4, t1, t2, t3
+                )
+            return carry
+
+        pairs(g0, 0, across, 0)
+        return entry
+
+    def sources(src, g, entry):
+        at = octet_rows(g)
+        field = [src[v, pl.ds(at, 8), :] for v in range(NVAR)]
+        result = []
+        for v in range(NVAR):
+            upwind = lane == wind_y[v]
+            downwind = lane == (LANES - 1) - wind_y[v]
+            u = half_y[v] * field[v]
+            d3 = jnp.where(downwind, 0.0, pltpu.roll(u, back_y[v], 1)) - u
+            d2 = jnp.where(upwind, u, pltpu.roll(d3, turn_y[v], 1))
+            d1 = jnp.where(upwind, 0.0, pltpu.roll(d2, turn_y[v], 1))
+            d4 = jnp.where(downwind, 0.0, pltpu.roll(d3, back_y[v], 1))
+            t = d3 - d2
+            t2 = (13.0 / 3.0) * (t * t) + WENO_EPS
+            end = (13.0 / 3.0) * (u * u) + WENO_EPS
+            t1 = jnp.where(upwind, end, pltpu.roll(t2, turn_y[v], 1))
+            t3 = jnp.where(downwind, end, pltpu.roll(t2, back_y[v], 1))
+            ahead = u + weighted(d1, d2, d3, d4, t1, t2, t3)
+            first_face = pltpu.roll(
+                entry[v], (wind_y[v] - 2 * g - minus_y[v]) & (LANES - 1), 1
+            )
+            behind = jnp.where(upwind, first_face, pltpu.roll(ahead, turn_y[v], 1))
+            columns = face[v, pl.ds(at, 8), :] - face[v, pl.ds(at - step_z[v], 8), :]
+            mixed = coupling[v, 0] * field[0]
+            for w in range(1, NVAR):
+                mixed = mixed + coupling[v, w] * field[w]
+            result.append(STEP_RATIO * mixed - (2.0 * STEP_RATIO) * ((ahead - behind) + columns))
+        return field, result
+
+    def corrector(src, dst, station, g0):
+        entry = fluxes(src, g0)
+
+        def step(g, carry):
+            at = octet_rows(g)
+            field, terms = sources(src, g, entry)
+            fluid = blocked[station, pl.ds(at, 8), :]
+            for v in range(NVAR):
+                value = newton(v, field[v], still[v, pl.ds(at, 8), :] + terms[v])
+                dst[v, pl.ds(at, 8), :] = jnp.where(fluid != 0.0, value, 0.0)
+            return carry
+
+        pairs(g0, 0, step, 0)
+
+    def reach(e):
+        return (LEFT - 1 - e) // 8
+
+    g0 = reach(33)
+    entry = fluxes(inf, g0)
+
+    def prepare(g, carry):
+        at = octet_rows(g)
+        field, terms = sources(inf, g, entry)
+        for v in range(NVAR):
+            base[v, pl.ds(at, 8), :] = energy(v, field[v])
+            work_inf[v, pl.ds(at, 8), :] = terms[v]
+        return carry
+
+    pairs(g0, 0, prepare, 0)
+
+    def iterate(k, carry):
+        old, new = s0.at[k % 2], s0.at[1 - k % 2]
+
+        def first_of_0(g, c):
+            at = octet_rows(g)
+            fluid = blocked[0, pl.ds(at, 8), :]
+            for v in range(NVAR):
+                here = inf[v, pl.ds(at, 8), :]
+                prior = old[v, pl.ds(at, 8), :]
+                fixed = base[v, pl.ds(at, 8), :] - (1.0 - vig[v]) * (prior - here)
+                still[v, pl.ds(at, 8), :] = fixed
+                value = newton(v, here, fixed + work_inf[v, pl.ds(at, 8), :])
+                first[v, pl.ds(at, 8), :] = jnp.where(fluid != 0.0, value, 0.0)
+            return c
+
+        pairs((6 + 6 * k) // 8, 0, first_of_0, 0)
+        corrector(first, second, 0, (9 + 6 * k) // 8)
+        corrector(second, new, 0, (12 + 6 * k) // 8)
+
+        def start_of_1(g, c):
+            at = octet_rows(g)
+            for v in range(NVAR):
+                above = new[v, pl.ds(at, 8), :]
+                prior = s1[v, pl.ds(at, 8), :] - old[v, pl.ds(at, 8), :]
+                still[v, pl.ds(at, 8), :] = energy(v, above) - (1.0 - vig[v]) * prior
+            return c
+
+        pairs((15 + 6 * k) // 8, 0, start_of_1, 0)
+        corrector(new, first, 1, (15 + 6 * k) // 8)
+        corrector(first, second, 1, (18 + 6 * k) // 8)
+        corrector(second, s1, 1, (21 + 6 * k) // 8)
+        return carry
+
+    lax.fori_loop(0, ITERS, iterate, 0)
+
+    quarter = lane // PIECE
+    for station, result in enumerate((s0.at[ITERS % 2], s1)):
+        for octet in range(4):
+            field = [result[v, pl.ds(center + 8 * octet, 8), :] for v in range(NVAR)]
+            for gy in range(4):
+                member = station * 4 + gy
+                value = None
+                for p in range(4):
+                    piece = turned(field[p], PIECE * (p - gy))
+                    value = piece if value is None else jnp.where(quarter == p, piece, value)
+                out[member, pl.ds(8 * octet, 8), :] = value
+                piece = turned(field[4], PIECE * (octet - gy))
+                if octet > 0:
+                    piece = jnp.where(quarter == octet, piece, out[member, pl.ds(SLAB, 8), :])
+                out[member, pl.ds(SLAB, 8), :] = piece
+
+
+def slabs_per_device(inflow, initial, solid, speed_y, speed_z, vigneron, coupling):
+    mesh_axes = ("sec", "gy", "gz")
+    nz_parts = lax.axis_size("gz")
+    sec, gy, gz = (lax.axis_index(a) for a in mesh_axes)
+    path = []
+    for z in range(nz_parts):
+        members = [(s, y) for y in range(4) for s in ((0, 1) if y % 2 == 0 else (1, 0))]
+        path += [(s * 4 + y) * nz_parts + z for s, y in (members if z % 2 == 0 else members[::-1])]
+
+    def along(value, steps):
+        count = len(path)
+        low, high = max(0, -steps), min(count, count - steps)
+        return lax.ppermute(value, mesh_axes, [(path[i], path[i + steps]) for i in range(low, high)])
+
+    odd = gz % 2
+    j = 2 * gy + (sec + gy) % 2
+    slab = gz * MEMBERS + jnp.where(odd == 1, MEMBERS - 1 - j, j)
+    place = jnp.stack(
+        [sec, odd, slab, jnp.asarray(len(path) * SLAB, jnp.int32)]
+    ).astype(jnp.int32)
+
+    smem = pl.BlockSpec(memory_space=pltpu.SMEM)
+    vmem = pl.BlockSpec(memory_space=pltpu.VMEM)
+    f32 = functools.partial(jax.ShapeDtypeStruct, dtype=jnp.float32)
+
+    packed = pl.pallas_call(
+        pack_kernel,
+        out_shape=f32((MEMBERS, CHUNK_IN, LANES)),
+        in_specs=[smem, vmem, vmem, vmem],
+        out_specs=vmem,
+        scratch_shapes=[
+            pltpu.VMEM((LANES, TILE), jnp.float32),
+            pltpu.VMEM((TILE, LANES), jnp.float32),
+            pltpu.VMEM((LANES, LANES), jnp.float32),
+        ],
+        name="pack",
+    )(place, inflow, initial, solid)
+    got = lax.all_to_all(packed, ("sec", "gy"), 0, 0)
+    own, right_one, left_one, right_two, left_two = pl.pallas_call(
+        assemble_kernel,
+        out_shape=[
+            f32((CHANNELS, SLAB, LANES)),
+            f32((EDGE_ONE, LANES)),
+            f32((EDGE_ONE, LANES)),
+            f32((EDGE_TWO, LANES)),
+            f32((EDGE_TWO, LANES)),
+        ],
+        in_specs=[vmem],
+        out_specs=[vmem] * 5,
+        name="assemble",
+    )(got)
+    window = pltpu.VMEM((NVAR, ROWS, LANES), jnp.float32)
+    sent = pl.pallas_call(
+        main_kernel,
+        out_shape=f32((MEMBERS, CHUNK_OUT, LANES)),
+        in_specs=[smem] * 5 + [vmem] * 5,
+        out_specs=vmem,
+        scratch_shapes=[
+            window, window, window, window, window,
+            pltpu.VMEM((2, NVAR, ROWS, LANES), jnp.float32),
+            window, window, window, window, window,
+            pltpu.VMEM((2, ROWS, LANES), jnp.float32),
+            window,
+        ],
+        compiler_params=pltpu.CompilerParams(vmem_limit_bytes=32 * 1024 * 1024),
+        name="march",
+    )(
+        place, speed_y, speed_z, vigneron, coupling,
+        own, along(right_one, 1), along(left_one, -1), along(right_two, 2), along(left_two, -2),
+    )
+    returned = lax.all_to_all(sent, ("sec", "gy"), 0, 0)
+    return pl.pallas_call(
+        unpack_kernel,
+        out_shape=f32((1, NVAR, PIECE, TILE)),
+        in_specs=[smem, vmem],
+        out_specs=vmem,
+        scratch_shapes=[
+            pltpu.VMEM((LANES, LANES), jnp.float32),
+            pltpu.VMEM((LANES, LANES), jnp.float32),
+        ],
+        name="unpack",
+    )(place, returned)
+
+
+def chosen(*args):
+    inflow, initial = args[0], args[1]
+    fits = (
+        lax.axis_size("sec") == 2
+        and lax.axis_size("gy") == 4
+        and inflow.shape == (NVAR, PIECE, TILE)
+        and initial.shape == (1, NVAR, PIECE, TILE)
+    )
+    return slabs_per_device(*args) if fits else per_device(*args)
+
+
 def solution(mesh):
     return jax.shard_map(
-        per_device,
+        chosen,
         mesh=mesh,
         in_specs=(
             P(None, "gy", "gz"),

time: 322 us -> 111 us (0.34)
  the two profiles are of different devices: /device:TPU:22 before, /device:TPU:0 now
where the time goes in v1:
time: 111 us; the launch traced here: 110 us
  Pallas kernels  63.3 us (57%)
  blocking collectives  30.1 us (27%)
  starting transfers between devices  9.63 us (9%)
  waiting for transfers between devices  5.75 us (5%)
    pallas_call x1, Pallas kernels, slabs_per_device(): pl.pallas_call(main_kernel, out_shape=f32((MEMBERS, CHUNK_OUT, LANES)), i...  57.3 us
    all_to_all x1, blocking collectives, slabs_per_device(): got = lax.all_to_all(packed, ('sec', 'gy'), 0, 0)  17.8 us
    all_to_all x1, blocking collectives, slabs_per_device(): returned = lax.all_to_all(sent, ('sec', 'gy'), 0, 0)  12.3 us
    ppermute x4, starting transfers between devices, along(): lax.ppermute(value, mesh_axes, [(path[i], path[i + steps]) for i in range...  9.63 us
    ppermute x4, waiting for transfers between devices, along(): lax.ppermute(value, mesh_axes, [(path[i], path[i + steps]) for i in range...  5.75 us
  transfers between devices with their start and end apart: 4, of which 2 were waited for; matrix products, arithmetic and copies ran while one was open for 0% of the time, Pallas kernels for 0%

profile of v1, /device:TPU:0, one launch (start us, length us, event | category | flops | bytes accessed | tf_op | source)
XLA Modules:
  0.0 110.5 jit_solution(16676998361637382728)
XLA Ops:
  0.0 0.6 pad_add_fusion.place
  0.6 2.1 %pack.1 = f32[8,72,128]{2,1,0:T(8,128)} custom-call(s32[4]{0:T(128)} %pad_add_fusion.place, f32[5,32,256]{2,1,0:T(8,128)} %inflow.1, f32[1,5,32,256]{3,2,1,0:T(8,128)} %initial.1, s32[1,32,256]{2,1,0:T(8,128)} %solid.1), custom_call_target="tpu_custom_call" | custom-call | tf_op jit(solution)/shard_map/pack/pallas_call | solution.py:559
  2.7 17.8 %all_to_all.10.got = f32[8,72,128]{2,1,0:T(8,128)} all-to-all(f32[8,72,128]{2,1,0:T(8,128)} %pack.1), channel_id=1, replica_groups=mesh['sec'=2,'gy'=4,'gz'=4] {'sec','gy'}, dimensions={0} | all-to-all | bytes 589824 | tf_op jit(solution)/shard_map/all_to_all | solution.py:571
  20.5 2.1 %assemble.1 = (f32[17,32,128]{2,1,0:T(8,128)}, f32[496,128]{1,0:T(8,128)}, f32[496,128]{1,0:T(8,128)}, f32[88,128]{1,0:T(8,128)}, f32[88,128]{1,0:T(8,128)}) custom-call(f32[8,72,128]{2,1,0:T(8,128)} %all_to_all.10.got), custom_call_target="tpu_custom_call" | custom-call | tf_op jit(solution)/shard_map/assemble/pallas_call | solution.py:572
  22.6 2.6 %collective-permute-start = (f32[496,128]{1,0:T(8,128)}, f32[496,128]{1,0:T(8,128)S(1)}, u32[]{:S(2)}, u32[]{:S(2)}) collective-permute-start(f32[496,128]{1,0:T(8,128)} %get-tuple-element.11), channel_id=1, source_target_pairs={{0,16},{16,20},{20,4},{4,8},{8,24},{24,28},{28,12},{12,13},{13,29}... | collective-permute-start | bytes 761864 | tf_op jit(solution)/shard_map/ppermute | solution.py:546
  25.2 1.3 %collective-permute-start.1 = (f32[496,128]{1,0:T(8,128)}, f32[496,128]{1,0:T(8,128)S(1)}, u32[]{:S(2)}, u32[]{:S(2)}) collective-permute-start(f32[496,128]{1,0:T(8,128)} %get-tuple-element.12), channel_id=1, source_target_pairs={{16,0},{20,16},{4,20},{8,4},{24,8},{28,24},{12,28},{13,12},{29,13}... | collective-permute-start | bytes 761864 | tf_op jit(solution)/shard_map/ppermute | solution.py:546
  26.5 4.4 %collective-permute-start.2 = (f32[88,128]{1,0:T(8,128)}, f32[88,128]{1,0:T(8,128)S(1)}, u32[]{:S(2)}, u32[]{:S(2)}) collective-permute-start(f32[88,128]{1,0:T(8,128)} %get-tuple-element.13), channel_id=1, source_target_pairs={{0,20},{16,4},{20,8},{4,24},{8,28},{24,12},{28,13},{12,29},{13,25}... | collective-permute-start | bytes 135176 | tf_op jit(solution)/shard_map/ppermute | solution.py:546
  31.0 0.0 copy-start.5
  31.0 0.0 copy-start.1
  31.0 0.0 copy-start.3
  31.0 0.0 copy-start.4
  31.0 1.3 %collective-permute-start.3 = (f32[88,128]{1,0:T(8,128)}, f32[88,128]{1,0:T(8,128)S(1)}, u32[]{:S(2)}, u32[]{:S(2)}) collective-permute-start(f32[88,128]{1,0:T(8,128)} %get-tuple-element.14), channel_id=1, source_target_pairs={{20,0},{4,16},{8,20},{24,4},{28,8},{12,24},{13,28},{29,12},{25,13}... | collective-permute-start | bytes 135176 | tf_op jit(solution)/shard_map/ppermute | solution.py:546
  32.3 0.7 collective-permute-done.2.from_left_two
  33.0 5.1 %collective-permute-done.3.from_right_two = f32[88,128]{1,0:T(8,128)S(1)} collective-permute-done((f32[88,128]{1,0:T(8,128)}, f32[88,128]{1,0:T(8,128)S(1)}, u32[]{:S(2)}, u32[]{:S(2)}) %collective-permute-start.3) | collective-permute-done | bytes 45088 | tf_op jit(solution)/shard_map/ppermute | solution.py:546
  38.1 0.0 collective-permute-done.from_left
  38.1 0.0 collective-permute-done.1.from_right
  38.1 0.0 copy-done.2
  38.1 0.0 copy-done.5
  38.1 0.0 copy-done.1
  38.1 0.0 copy-done.3
  38.1 0.9 copy-done
  39.1 57.3 %march.1 = f32[8,40,128]{2,1,0:T(8,128)S(1)} custom-call(s32[4]{0:T(128)S(1)} %copy-done.1, f32[5]{0:T(128)S(1)} %copy-done.3, f32[5]{0:T(128)S(1)} %copy-done.4, f32[5]{0:T(128)S(1)} %copy-done.5, f32[5,5]{1,0:T(8,128)S(1)} %copy-done.2, f32[17,32,128]{2,1,0:T(8,128)S(1)} %copy-done, f32[496,128]{1,0:T(8,128)S(1)} %collective-permute-done.from_left, ...), custom_call_target="tpu_custom_call" | custom-call | tf_op jit(solution)/shard_map/march/pallas_call | solution.py:586
  96.4 12.3 %all_to_all.11.got = f32[8,40,128]{2,1,0:T(8,128)} all-to-all(f32[8,40,128]{2,1,0:T(8,128)S(1)} %march.1), channel_id=1, replica_groups=mesh['sec'=2,'gy'=4,'gz'=4] {'sec','gy'}, dimensions={0} | all-to-all | bytes 327680 | tf_op jit(solution)/shard_map/all_to_all | solution.py:604
  108.7 1.8 %unpack.1 = f32[1,5,32,256]{3,2,1,0:T(8,128)} custom-call(s32[4]{0:T(128)} %pad_add_fusion.place, f32[8,40,128]{2,1,0:T(8,128)} %all_to_all.11.got), custom_call_target="tpu_custom_call" | custom-call | tf_op jit(solution)/shard_map/unpack/pallas_call | solution.py:605
  (3 shorter events, 0.0 us)
Async XLA Ops:
  22.6 15.5 %copy-start.2 = (f32[5,5]{1,0:T(8,128)S(1)}, f32[5,5]{1,0:T(8,128)}, u32[]{:S(2)}) copy-start(f32[5,5]{1,0:T(8,128)} %coupling.1) | copy-start | bytes 304
  22.6 15.5 %collective-permute-start = (f32[496,128]{1,0:T(8,128)}, f32[496,128]{1,0:T(8,128)S(1)}, u32[]{:S(2)}, u32[]{:S(2)}) collective-permute-start(f32[496,128]{1,0:T(8,128)} %get-tuple-element.11), channel_id=1, source_target_pairs={{0,16},{16,20},{20,4},{4,8},{8,24},{24,28},{28,12},{12,13},{13,29}... | collective-permute-start | bytes 761864 | tf_op jit(solution)/shard_map/ppermute | solution.py:546
  25.2 12.9 %collective-permute-start.1 = (f32[496,128]{1,0:T(8,128)}, f32[496,128]{1,0:T(8,128)S(1)}, u32[]{:S(2)}, u32[]{:S(2)}) collective-permute-start(f32[496,128]{1,0:T(8,128)} %get-tuple-element.12), channel_id=1, source_target_pairs={{16,0},{20,16},{4,20},{8,4},{24,8},{28,24},{12,28},{13,12},{29,13}... | collective-permute-start | bytes 761864 | tf_op jit(solution)/shard_map/ppermute | solution.py:546
  26.5 6.5 %collective-permute-start.2 = (f32[88,128]{1,0:T(8,128)}, f32[88,128]{1,0:T(8,128)S(1)}, u32[]{:S(2)}, u32[]{:S(2)}) collective-permute-start(f32[88,128]{1,0:T(8,128)} %get-tuple-element.13), channel_id=1, source_target_pairs={{0,20},{16,4},{20,8},{4,24},{8,28},{24,12},{28,13},{12,29},{13,25}... | collective-permute-start | bytes 135176 | tf_op jit(solution)/shard_map/ppermute | solution.py:546
  31.0 7.1 %copy-start.5 = (f32[5]{0:T(128)S(1)}, f32[5]{0:T(128)}, u32[]{:S(2)}) copy-start(f32[5]{0:T(128)} %vigneron.1) | copy-start | bytes 64
  31.0 7.1 %copy-start.1 = (s32[4]{0:T(128)S(1)}, s32[4]{0:T(128)}, u32[]{:S(2)}) copy-start(s32[4]{0:T(128)} %pad_add_fusion.place) | copy-start | bytes 52
  31.0 7.1 %copy-start.3 = (f32[5]{0:T(128)S(1)}, f32[5]{0:T(128)}, u32[]{:S(2)}) copy-start(f32[5]{0:T(128)} %speed_y.1) | copy-start | bytes 64
  31.0 7.1 %copy-start.4 = (f32[5]{0:T(128)S(1)}, f32[5]{0:T(128)}, u32[]{:S(2)}) copy-start(f32[5]{0:T(128)} %speed_z.1) | copy-start | bytes 64
  31.0 7.0 %collective-permute-start.3 = (f32[88,128]{1,0:T(8,128)}, f32[88,128]{1,0:T(8,128)S(1)}, u32[]{:S(2)}, u32[]{:S(2)}) collective-permute-start(f32[88,128]{1,0:T(8,128)} %get-tuple-element.14), channel_id=1, source_target_pairs={{20,0},{4,16},{8,20},{24,4},{28,8},{12,24},{13,28},{29,12},{25,13}... | collective-permute-start | bytes 135176 | tf_op jit(solution)/shard_map/ppermute | solution.py:546
  38.1 1.0 copy-start

commit v2 on v1

--- a/solution.py
+++ b/solution.py
@@ -295,13 +295,13 @@
     place, speed_y, speed_z, vigneron, coupling,
     own, from_left, from_right, from_left_two, from_right_two,
     out,
-    inf, still, base, first, second, s0, s1, work_inf, delta, curve, face, blocked, start1,
+    inf, still, base, first, second, s0, s1, work_inf, delta, curve, face, blocked,
+    across, delta_y, curve_y, face_y, rows_part,
 ):
     lane = lane_iota()
     center = GUARD + LEFT
 
-    def fill(ref, index, channel, wide):
-        ref = ref.at[index] if index is not None else ref
+    def fill(ref, channel, wide):
         ref[pl.ds(0, GUARD), :] = jnp.zeros((GUARD, LANES), jnp.float32)
         ref[pl.ds(ROWS - GUARD, GUARD), :] = jnp.zeros((GUARD, LANES), jnp.float32)
         ref[pl.ds(center, SLAB), :] = own[channel]
@@ -319,11 +319,11 @@
             ref[pl.ds(center + SLAB + NEAR, 16), :] = zeros
 
     for v in range(NVAR):
-        fill(inf, v, v, True)
-        fill(s0.at[0], v, 5 + v, True)
-        fill(s1, v, 11 + v, False)
-    fill(blocked, 0, 10, True)
-    fill(blocked, 1, 16, False)
+        fill(inf.at[v], v, True)
+        fill(s0.at[0, v], 5 + v, True)
+        fill(s1.at[v], 11 + v, False)
+    fill(blocked.at[0], 10, True)
+    fill(blocked.at[1], 16, False)
     slab, last = place[2], place[3]
     for octet in range(ROWS // 8):
         rows = pl.ds(8 * octet, 8)
@@ -336,16 +336,16 @@
     for ref in (first, second, s0.at[1]):
         for v in range(NVAR):
             ref[v] = jnp.zeros((ROWS, LANES), jnp.float32)
+    for v in range(NVAR):
+        across[v, pl.ds(0, GUARD), :] = jnp.zeros((GUARD, LANES), jnp.float32)
+        across[v, pl.ds(GUARD + LANES, GUARD), :] = jnp.zeros((GUARD, LANES), jnp.float32)
 
     sy = [speed_y[v] for v in range(NVAR)]
     sz = [speed_z[v] for v in range(NVAR)]
     half_y = [0.5 * jnp.maximum(s, -s) for s in sy]
     half_z = [0.5 * jnp.maximum(s, -s) for s in sz]
+    step_y = [jnp.where(s >= 0.0, 1, -1) for s in sy]
     step_z = [jnp.where(s >= 0.0, 1, -1) for s in sz]
-    turn_y = [jnp.where(s >= 0.0, 1, LANES - 1) for s in sy]
-    back_y = [jnp.where(s >= 0.0, LANES - 1, 1) for s in sy]
-    wind_y = [jnp.where(s >= 0.0, 0, LANES - 1) for s in sy]
-    minus_y = [jnp.where(s >= 0.0, 0, 1) for s in sy]
     vig = [vigneron[v] for v in range(NVAR)]
 
     def newton(v, guess, target):
@@ -364,126 +364,95 @@
     def octet_rows(g):
         return pl.multiple_of(GUARD + 8 * g, 8)
 
-    def pairs(g0, extra, body, carry):
+    def pairs(low, high, body):
         def two(i, c):
             for k in range(2):
-                c = body(g0 - extra + 2 * i + k, c)
+                body(octet_rows(low + 2 * i + k))
             return c
-        return lax.fori_loop(0, 7 - g0 + extra, two, carry)
-
-    def fluxes(src, g0):
-        def differ(g, carry):
-            at = octet_rows(g)
-            packed = []
+        lax.fori_loop(0, (high - low) // 2, two, 0)
+
+    def differences(src, half, step, d_ref, t_ref):
+        def body(at):
             for v in range(NVAR):
                 here = src[v, pl.ds(at, 8), :]
-                down = src[v, pl.ds(at + step_z[v], 8), :]
-                up = src[v, pl.ds(at - step_z[v], 8), :]
-                d = (down - here) * half_z[v]
-                t = d - (here - up) * half_z[v]
-                delta[v, pl.ds(at, 8), :] = d
-                curve[v, pl.ds(at, 8), :] = (13.0 / 3.0) * (t * t) + WENO_EPS
-                edge = pltpu.roll(here, (2 * g + 2 * minus_y[v]) & (LANES - 1), 1)
-                packed.append(jnp.where(lane // 2 == g, edge, carry[v]))
-            return tuple(packed)
-
-        zero = jnp.zeros((8, LANES), jnp.float32)
-        edges = pairs(g0, 1, differ, (zero,) * NVAR)
-
-        entry = []
-        for v in range(NVAR):
-            u = edges[v] * half_y[v]
-            d4 = pltpu.roll(u, back_y[v], 1) - u
-            t3 = d4 - u
-            flat = jnp.full((8, LANES), WENO_EPS, jnp.float32)
-            entry.append(weighted(
-                zero, zero, u, d4, flat,
-                (13.0 / 3.0) * (u * u) + WENO_EPS, (13.0 / 3.0) * (t3 * t3) + WENO_EPS,
-            ))
-
-        def across(g, carry):
-            at = octet_rows(g)
+                down = src[v, pl.ds(at + step[v], 8), :]
+                up = src[v, pl.ds(at - step[v], 8), :]
+                d = (down - here) * half[v]
+                t = d - (here - up) * half[v]
+                d_ref[v, pl.ds(at, 8), :] = d
+                t_ref[v, pl.ds(at, 8), :] = (13.0 / 3.0) * (t * t) + WENO_EPS
+        return body
+
+    def faces(src, half, step, d_ref, t_ref, f_ref, shift=None):
+        def body(at):
             for v in range(NVAR):
-                s = step_z[v]
-                d3 = delta[v, pl.ds(at, 8), :]
-                d2 = delta[v, pl.ds(at - s, 8), :]
-                d1 = delta[v, pl.ds(at - 2 * s, 8), :]
-                d4 = delta[v, pl.ds(at + s, 8), :]
-                t1 = curve[v, pl.ds(at - s, 8), :]
-                t2 = curve[v, pl.ds(at, 8), :]
-                t3 = curve[v, pl.ds(at + s, 8), :]
-                face[v, pl.ds(at, 8), :] = half_z[v] * src[v, pl.ds(at, 8), :] + weighted(
+                s = step[v]
+                rows = at if shift is None else at + shift[v]
+                d3 = d_ref[v, pl.ds(rows, 8), :]
+                d2 = d_ref[v, pl.ds(rows - s, 8), :]
+                d1 = d_ref[v, pl.ds(rows - 2 * s, 8), :]
+                d4 = d_ref[v, pl.ds(rows + s, 8), :]
+                t1 = t_ref[v, pl.ds(rows - s, 8), :]
+                t2 = t_ref[v, pl.ds(rows, 8), :]
+                t3 = t_ref[v, pl.ds(rows + s, 8), :]
+                f_ref[v, pl.ds(rows, 8), :] = half[v] * src[v, pl.ds(rows, 8), :] + weighted(
                     d1, d2, d3, d4, t1, t2, t3
                 )
-            return carry
-
-        pairs(g0, 0, across, 0)
-        return entry
-
-    def sources(src, g, entry):
-        at = octet_rows(g)
+        return body
+
+    def fluxes(src, g0):
+        for v in range(NVAR):
+            across[v, pl.ds(GUARD, LANES), :] = src[v, pl.ds(GUARD - 8, LANES), :].T
+        pairs(-1, 17, differences(across, half_y, step_y, delta_y, curve_y))
+        row_faces = faces(across, half_y, step_y, delta_y, curve_y, face_y)
+        pairs(0, 16, row_faces)
+        faces(across, half_y, step_y, delta_y, curve_y, face_y,
+              [jnp.where(s >= 0.0, -8, LANES) for s in sy])(GUARD)
+        for v in range(NVAR):
+            rows_part[v] = (
+                face_y[v, pl.ds(GUARD, LANES), :] - face_y[v, pl.ds(GUARD - step_y[v], LANES), :]
+            ).T
+        pairs(g0 - 1, 15 - g0, differences(src, half_z, step_z, delta, curve))
+        pairs(g0, 14 - g0, faces(src, half_z, step_z, delta, curve, face))
+
+    def sources(src, at):
         field = [src[v, pl.ds(at, 8), :] for v in range(NVAR)]
         result = []
         for v in range(NVAR):
-            upwind = lane == wind_y[v]
-            downwind = lane == (LANES - 1) - wind_y[v]
-            u = half_y[v] * field[v]
-            d3 = jnp.where(downwind, 0.0, pltpu.roll(u, back_y[v], 1)) - u
-            d2 = jnp.where(upwind, u, pltpu.roll(d3, turn_y[v], 1))
-            d1 = jnp.where(upwind, 0.0, pltpu.roll(d2, turn_y[v], 1))
-            d4 = jnp.where(downwind, 0.0, pltpu.roll(d3, back_y[v], 1))
-            t = d3 - d2
-            t2 = (13.0 / 3.0) * (t * t) + WENO_EPS
-            end = (13.0 / 3.0) * (u * u) + WENO_EPS
-            t1 = jnp.where(upwind, end, pltpu.roll(t2, turn_y[v], 1))
-            t3 = jnp.where(downwind, end, pltpu.roll(t2, back_y[v], 1))
-            ahead = u + weighted(d1, d2, d3, d4, t1, t2, t3)
-            first_face = pltpu.roll(
-                entry[v], (wind_y[v] - 2 * g - minus_y[v]) & (LANES - 1), 1
-            )
-            behind = jnp.where(upwind, first_face, pltpu.roll(ahead, turn_y[v], 1))
             columns = face[v, pl.ds(at, 8), :] - face[v, pl.ds(at - step_z[v], 8), :]
-            mixed = coupling[v, 0] * field[0]
+            rows = rows_part[v, pl.ds(pl.multiple_of(at - (GUARD - 8), 8), 8), :]
+            mixed = (STEP_RATIO * coupling[v, 0]) * field[0]
             for w in range(1, NVAR):
-                mixed = mixed + coupling[v, w] * field[w]
-            result.append(STEP_RATIO * mixed - (2.0 * STEP_RATIO) * ((ahead - behind) + columns))
+                mixed = mixed + (STEP_RATIO * coupling[v, w]) * field[w]
+            result.append(mixed - (2.0 * STEP_RATIO) * (rows + columns))
         return field, result
 
     def corrector(src, dst, station, g0):
-        entry = fluxes(src, g0)
-
-        def step(g, carry):
-            at = octet_rows(g)
-            field, terms = sources(src, g, entry)
+        fluxes(src, g0)
+
+        def step(at):
+            field, terms = sources(src, at)
             fluid = blocked[station, pl.ds(at, 8), :]
             for v in range(NVAR):
                 value = newton(v, field[v], still[v, pl.ds(at, 8), :] + terms[v])
                 dst[v, pl.ds(at, 8), :] = jnp.where(fluid != 0.0, value, 0.0)
-            return carry
-
-        pairs(g0, 0, step, 0)
-
-    def reach(e):
-        return (LEFT - 1 - e) // 8
-
-    g0 = reach(33)
-    entry = fluxes(inf, g0)
-
-    def prepare(g, carry):
-        at = octet_rows(g)
-        field, terms = sources(inf, g, entry)
+
+        pairs(g0, 14 - g0, step)
+
+    fluxes(inf, 0)
+
+    def prepare(at):
+        field, terms = sources(inf, at)
         for v in range(NVAR):
             base[v, pl.ds(at, 8), :] = energy(v, field[v])
             work_inf[v, pl.ds(at, 8), :] = terms[v]
-        return carry
-
-    pairs(g0, 0, prepare, 0)
+
+    pairs(0, 14, prepare)
 
     def iterate(k, carry):
         old, new = s0.at[k % 2], s0.at[1 - k % 2]
 
-        def first_of_0(g, c):
-            at = octet_rows(g)
+        def first_of_0(at):
             fluid = blocked[0, pl.ds(at, 8), :]
             for v in range(NVAR):
                 here = inf[v, pl.ds(at, 8), :]
@@ -492,22 +461,21 @@
                 still[v, pl.ds(at, 8), :] = fixed
                 value = newton(v, here, fixed + work_inf[v, pl.ds(at, 8), :])
                 first[v, pl.ds(at, 8), :] = jnp.where(fluid != 0.0, value, 0.0)
-            return c
-
-        pairs((6 + 6 * k) // 8, 0, first_of_0, 0)
+
+        g0 = (6 + 6 * k) // 8
+        pairs(g0, 14 - g0, first_of_0)
         corrector(first, second, 0, (9 + 6 * k) // 8)
         corrector(second, new, 0, (12 + 6 * k) // 8)
 
-        def start_of_1(g, c):
-            at = octet_rows(g)
+        def start_of_1(at):
             for v in range(NVAR):
                 above = new[v, pl.ds(at, 8), :]
                 prior = s1[v, pl.ds(at, 8), :] - old[v, pl.ds(at, 8), :]
                 still[v, pl.ds(at, 8), :] = energy(v, above) - (1.0 - vig[v]) * prior
-            return c
-
-        pairs((15 + 6 * k) // 8, 0, start_of_1, 0)
-        corrector(new, first, 1, (15 + 6 * k) // 8)
+
+        g0 = (15 + 6 * k) // 8
+        pairs(g0, 14 - g0, start_of_1)
+        corrector(new, first, 1, g0)
         corrector(first, second, 1, (18 + 6 * k) // 8)
         corrector(second, s1, 1, (21 + 6 * k) // 8)
         return carry
@@ -583,6 +551,7 @@
         name="assemble",
     )(got)
     window = pltpu.VMEM((NVAR, ROWS, LANES), jnp.float32)
+    plane = pltpu.VMEM((NVAR, LANES + 2 * GUARD, LANES), jnp.float32)
     sent = pl.pallas_call(
         main_kernel,
         out_shape=f32((MEMBERS, CHUNK_OUT, LANES)),
@@ -593,7 +562,7 @@
             pltpu.VMEM((2, NVAR, ROWS, LANES), jnp.float32),
             window, window, window, window, window,
             pltpu.VMEM((2, ROWS, LANES), jnp.float32),
-            window,
+            plane, plane, plane, plane, pltpu.VMEM((NVAR, LANES, LANES), jnp.float32),
         ],
         compiler_params=pltpu.CompilerParams(vmem_limit_bytes=32 * 1024 * 1024),
         name="march",

time: 111 us -> 97.8 us (0.88)
  Pallas kernels: 63.3 us -> 50.2 us
    pallas_call x1, Pallas kernels: 57.3 us -> 44.2 us  [slabs_per_device(): pl.pallas_call(main_kernel, out_shape=f32((MEMBERS, CHUNK_OUT, LANES)), i...]
where the time goes in v2:
time: 97.8 us; the launch traced here: 97.4 us
  Pallas kernels  50.2 us (51%)
  blocking collectives  30.1 us (31%)
  starting transfers between devices  9.63 us (10%)
  waiting for transfers between devices  5.75 us (6%)
  local copies, waits for them, and re-layouts  0.98 us (1%)
    pallas_call x1, Pallas kernels, slabs_per_device(): pl.pallas_call(main_kernel, out_shape=f32((MEMBERS, CHUNK_OUT, LANES)), i...  44.2 us
    all_to_all x1, blocking collectives, slabs_per_device(): got = lax.all_to_all(packed, ('sec', 'gy'), 0, 0)  17.8 us
    all_to_all x1, blocking collectives, slabs_per_device(): returned = lax.all_to_all(sent, ('sec', 'gy'), 0, 0)  12.3 us
    ppermute x4, starting transfers between devices, along(): lax.ppermute(value, mesh_axes, [(path[i], path[i + steps]) for i in range...  9.63 us
    ppermute x4, waiting for transfers between devices, along(): lax.ppermute(value, mesh_axes, [(path[i], path[i + steps]) for i in range...  5.75 us
    pallas_call x1, Pallas kernels, slabs_per_device(): pl.pallas_call(assemble_kernel, out_shape=[f32((CHANNELS, SLAB, LANES)),...  2.13 us
    pallas_call x1, Pallas kernels, slabs_per_device(): pl.pallas_call(pack_kernel, out_shape=f32((MEMBERS, CHUNK_IN, LANES)), in...  2.06 us
  transfers between devices with their start and end apart: 4, of which 2 were waited for; matrix products, arithmetic and copies ran while one was open for 0% of the time, Pallas kernels for 0%

profile of v2, /device:TPU:0, one launch (start us, length us, event | category | flops | bytes accessed | tf_op | source)
XLA Modules:
  0.0 97.4 jit_solution(1277191362894994214)
XLA Ops:
  0.0 0.6 pad_add_fusion.place
  0.6 2.1 %pack.1 = f32[8,72,128]{2,1,0:T(8,128)} custom-call(s32[4]{0:T(128)} %pad_add_fusion.place, f32[5,32,256]{2,1,0:T(8,128)} %inflow.1, f32[1,5,32,256]{3,2,1,0:T(8,128)} %initial.1, s32[1,32,256]{2,1,0:T(8,128)} %solid.1), custom_call_target="tpu_custom_call" | custom-call | tf_op jit(solution)/shard_map/pack/pallas_call | solution.py:527
  2.7 17.8 %all_to_all.10.got = f32[8,72,128]{2,1,0:T(8,128)} all-to-all(f32[8,72,128]{2,1,0:T(8,128)} %pack.1), channel_id=1, replica_groups=mesh['sec'=2,'gy'=4,'gz'=4] {'sec','gy'}, dimensions={0} | all-to-all | bytes 589824 | tf_op jit(solution)/shard_map/all_to_all | solution.py:539
  20.5 2.1 %assemble.1 = (f32[17,32,128]{2,1,0:T(8,128)}, f32[496,128]{1,0:T(8,128)}, f32[496,128]{1,0:T(8,128)}, f32[88,128]{1,0:T(8,128)}, f32[88,128]{1,0:T(8,128)}) custom-call(f32[8,72,128]{2,1,0:T(8,128)} %all_to_all.10.got), custom_call_target="tpu_custom_call" | custom-call | tf_op jit(solution)/shard_map/assemble/pallas_call | solution.py:540
  22.6 2.6 %collective-permute-start = (f32[496,128]{1,0:T(8,128)}, f32[496,128]{1,0:T(8,128)S(1)}, u32[]{:S(2)}, u32[]{:S(2)}) collective-permute-start(f32[496,128]{1,0:T(8,128)} %get-tuple-element.11), channel_id=1, source_target_pairs={{0,16},{16,20},{20,4},{4,8},{8,24},{24,28},{28,12},{12,13},{13,29}... | collective-permute-start | bytes 761864 | tf_op jit(solution)/shard_map/ppermute | solution.py:514
  25.2 1.3 %collective-permute-start.1 = (f32[496,128]{1,0:T(8,128)}, f32[496,128]{1,0:T(8,128)S(1)}, u32[]{:S(2)}, u32[]{:S(2)}) collective-permute-start(f32[496,128]{1,0:T(8,128)} %get-tuple-element.12), channel_id=1, source_target_pairs={{16,0},{20,16},{4,20},{8,4},{24,8},{28,24},{12,28},{13,12},{29,13}... | collective-permute-start | bytes 761864 | tf_op jit(solution)/shard_map/ppermute | solution.py:514
  26.5 4.4 %collective-permute-start.2 = (f32[88,128]{1,0:T(8,128)}, f32[88,128]{1,0:T(8,128)S(1)}, u32[]{:S(2)}, u32[]{:S(2)}) collective-permute-start(f32[88,128]{1,0:T(8,128)} %get-tuple-element.13), channel_id=1, source_target_pairs={{0,20},{16,4},{20,8},{4,24},{8,28},{24,12},{28,13},{12,29},{13,25}... | collective-permute-start | bytes 135176 | tf_op jit(solution)/shard_map/ppermute | solution.py:514
  31.0 0.0 copy-start.5
  31.0 0.0 copy-start.1
  31.0 0.0 copy-start.3
  31.0 0.0 copy-start.4
  31.0 1.3 %collective-permute-start.3 = (f32[88,128]{1,0:T(8,128)}, f32[88,128]{1,0:T(8,128)S(1)}, u32[]{:S(2)}, u32[]{:S(2)}) collective-permute-start(f32[88,128]{1,0:T(8,128)} %get-tuple-element.14), channel_id=1, source_target_pairs={{20,0},{4,16},{8,20},{24,4},{28,8},{12,24},{13,28},{29,12},{25,13}... | collective-permute-start | bytes 135176 | tf_op jit(solution)/shard_map/ppermute | solution.py:514
  32.3 0.7 collective-permute-done.2.from_left_two
  33.0 5.1 %collective-permute-done.3.from_right_two = f32[88,128]{1,0:T(8,128)S(1)} collective-permute-done((f32[88,128]{1,0:T(8,128)}, f32[88,128]{1,0:T(8,128)S(1)}, u32[]{:S(2)}, u32[]{:S(2)}) %collective-permute-start.3) | collective-permute-done | bytes 45088 | tf_op jit(solution)/shard_map/ppermute | solution.py:514
  38.1 0.0 collective-permute-done.from_left
  38.1 0.0 collective-permute-done.1.from_right
  38.1 0.0 copy-done.2
  38.1 0.0 copy-done.5
  38.1 0.0 copy-done.1
  38.1 0.0 copy-done.3
  38.1 0.9 copy-done
  39.1 44.2 %march.1 = f32[8,40,128]{2,1,0:T(8,128)S(1)} custom-call(s32[4]{0:T(128)S(1)} %copy-done.1, f32[5]{0:T(128)S(1)} %copy-done.3, f32[5]{0:T(128)S(1)} %copy-done.4, f32[5]{0:T(128)S(1)} %copy-done.5, f32[5,5]{1,0:T(8,128)S(1)} %copy-done.2, f32[17,32,128]{2,1,0:T(8,128)S(1)} %copy-done, f32[496,128]{1,0:T(8,128)S(1)} %collective-permute-done.from_left, ...), custom_call_target="tpu_custom_call" | custom-call | tf_op jit(solution)/shard_map/march/pallas_call | solution.py:555
  83.3 12.3 %all_to_all.11.got = f32[8,40,128]{2,1,0:T(8,128)} all-to-all(f32[8,40,128]{2,1,0:T(8,128)S(1)} %march.1), channel_id=1, replica_groups=mesh['sec'=2,'gy'=4,'gz'=4] {'sec','gy'}, dimensions={0} | all-to-all | bytes 327680 | tf_op jit(solution)/shard_map/all_to_all | solution.py:573
  95.6 1.8 %unpack.1 = f32[1,5,32,256]{3,2,1,0:T(8,128)} custom-call(s32[4]{0:T(128)} %pad_add_fusion.place, f32[8,40,128]{2,1,0:T(8,128)} %all_to_all.11.got), custom_call_target="tpu_custom_call" | custom-call | tf_op jit(solution)/shard_map/unpack/pallas_call | solution.py:574
  (3 shorter events, 0.0 us)
Async XLA Ops:
  22.6 15.5 %copy-start.2 = (f32[5,5]{1,0:T(8,128)S(1)}, f32[5,5]{1,0:T(8,128)}, u32[]{:S(2)}) copy-start(f32[5,5]{1,0:T(8,128)} %coupling.1) | copy-start | bytes 304
  22.6 15.5 %collective-permute-start = (f32[496,128]{1,0:T(8,128)}, f32[496,128]{1,0:T(8,128)S(1)}, u32[]{:S(2)}, u32[]{:S(2)}) collective-permute-start(f32[496,128]{1,0:T(8,128)} %get-tuple-element.11), channel_id=1, source_target_pairs={{0,16},{16,20},{20,4},{4,8},{8,24},{24,28},{28,12},{12,13},{13,29}... | collective-permute-start | bytes 761864 | tf_op jit(solution)/shard_map/ppermute | solution.py:514
  25.2 12.9 %collective-permute-start.1 = (f32[496,128]{1,0:T(8,128)}, f32[496,128]{1,0:T(8,128)S(1)}, u32[]{:S(2)}, u32[]{:S(2)}) collective-permute-start(f32[496,128]{1,0:T(8,128)} %get-tuple-element.12), channel_id=1, source_target_pairs={{16,0},{20,16},{4,20},{8,4},{24,8},{28,24},{12,28},{13,12},{29,13}... | collective-permute-start | bytes 761864 | tf_op jit(solution)/shard_map/ppermute | solution.py:514
  26.5 6.5 %collective-permute-start.2 = (f32[88,128]{1,0:T(8,128)}, f32[88,128]{1,0:T(8,128)S(1)}, u32[]{:S(2)}, u32[]{:S(2)}) collective-permute-start(f32[88,128]{1,0:T(8,128)} %get-tuple-element.13), channel_id=1, source_target_pairs={{0,20},{16,4},{20,8},{4,24},{8,28},{24,12},{28,13},{12,29},{13,25}... | collective-permute-start | bytes 135176 | tf_op jit(solution)/shard_map/ppermute | solution.py:514
  31.0 7.1 %copy-start.5 = (f32[5]{0:T(128)S(1)}, f32[5]{0:T(128)}, u32[]{:S(2)}) copy-start(f32[5]{0:T(128)} %vigneron.1) | copy-start | bytes 64
  31.0 7.1 %copy-start.1 = (s32[4]{0:T(128)S(1)}, s32[4]{0:T(128)}, u32[]{:S(2)}) copy-start(s32[4]{0:T(128)} %pad_add_fusion.place) | copy-start | bytes 52
  31.0 7.1 %copy-start.3 = (f32[5]{0:T(128)S(1)}, f32[5]{0:T(128)}, u32[]{:S(2)}) copy-start(f32[5]{0:T(128)} %speed_y.1) | copy-start | bytes 64
  31.0 7.1 %copy-start.4 = (f32[5]{0:T(128)S(1)}, f32[5]{0:T(128)}, u32[]{:S(2)}) copy-start(f32[5]{0:T(128)} %speed_z.1) | copy-start | bytes 64
  31.0 7.0 %collective-permute-start.3 = (f32[88,128]{1,0:T(8,128)}, f32[88,128]{1,0:T(8,128)S(1)}, u32[]{:S(2)}, u32[]{:S(2)}) collective-permute-start(f32[88,128]{1,0:T(8,128)} %get-tuple-element.14), channel_id=1, source_target_pairs={{20,0},{4,16},{8,20},{24,4},{28,8},{12,24},{13,28},{29,12},{25,13}... | collective-permute-start | bytes 135176 | tf_op jit(solution)/shard_map/ppermute | solution.py:514
  38.1 1.0 copy-start

commit v3 on v2

--- a/solution.py
+++ b/solution.py
@@ -282,12 +282,9 @@
     y1 = pltpu.reciprocal(t1 + a * a, approx=True)
     y2 = pltpu.reciprocal(t2 + b * b, approx=True)
     y3 = pltpu.reciprocal(t3 + c * c, approx=True)
-    g1, g2, g3 = y1 * y1, y2 * y2, y3 * y3
-    p1 = (a + a - d2) * (1.0 / 6.0)
-    p2 = b + d3
-    p3 = (c + d3) * 0.5
-    over = g1 * p1 + g2 * p2 + g3 * p3
-    under = g1 + 6.0 * g2 + 3.0 * g3
+    g1, g2, g3 = (1.0 / 6.0) * (y1 * y1), y2 * y2, 0.5 * (y3 * y3)
+    over = g1 * (a + a - d2) + g2 * (b + d3) + g3 * (c + d3)
+    under = g1 + g2 + g3
     return over * pltpu.reciprocal(under, approx=True)
 
 
@@ -295,9 +292,9 @@
     place, speed_y, speed_z, vigneron, coupling,
     own, from_left, from_right, from_left_two, from_right_two,
     out,
-    inf, still, base, first, second, s0, s1, work_inf, delta, curve, face, blocked,
-    across, delta_y, curve_y, face_y, rows_part,
+    inf, still, base, cur, s0, s1, work_inf, delta, curve, face, rows_part, blocked, half_block, *per_block,
 ):
+    across, delta_y, curve_y, face_y = (per_block[NVAR * i:NVAR * (i + 1)] for i in range(4))
     lane = lane_iota()
     center = GUARD + LEFT
 
@@ -320,8 +317,8 @@
 
     for v in range(NVAR):
         fill(inf.at[v], v, True)
-        fill(s0.at[0, v], 5 + v, True)
-        fill(s1.at[v], 11 + v, False)
+        fill(s0.at[v], 5 + v, True)
+        fill(cur.at[v], 11 + v, False)
     fill(blocked.at[0], 10, True)
     fill(blocked.at[1], 16, False)
     slab, last = place[2], place[3]
@@ -333,12 +330,9 @@
             blocked[station, rows, :] = jnp.where(
                 outside | (blocked[station, rows, :] != 0.0), 0.0, 1.0
             )
-    for ref in (first, second, s0.at[1]):
-        for v in range(NVAR):
-            ref[v] = jnp.zeros((ROWS, LANES), jnp.float32)
     for v in range(NVAR):
-        across[v, pl.ds(0, GUARD), :] = jnp.zeros((GUARD, LANES), jnp.float32)
-        across[v, pl.ds(GUARD + LANES, GUARD), :] = jnp.zeros((GUARD, LANES), jnp.float32)
+        across[v][pl.ds(0, GUARD), :] = jnp.zeros((GUARD, LANES), jnp.float32)
+        across[v][pl.ds(GUARD + LANES, GUARD), :] = jnp.zeros((GUARD, LANES), jnp.float32)
 
     sy = [speed_y[v] for v in range(NVAR)]
     sz = [speed_z[v] for v in range(NVAR)]
@@ -347,6 +341,24 @@
     step_y = [jnp.where(s >= 0.0, 1, -1) for s in sy]
     step_z = [jnp.where(s >= 0.0, 1, -1) for s in sz]
     vig = [vigneron[v] for v in range(NVAR)]
+    forward = [(s >= 0.0).astype(jnp.int32) for s in sy]
+    ahead = sum(forward)
+    rank, seen = [], 0
+    for v in range(NVAR):
+        rank.append(jnp.where(forward[v] == 1, seen, ahead + v - seen))
+        seen = seen + forward[v]
+
+    def nth(r):
+        return sum(jnp.where(rank[v] == r, v, 0) for v in range(NVAR))
+
+    lone = jnp.where(ahead % 2 == 0, NVAR - 1, 0)
+    begin = 1 - jnp.minimum(lone, 1)
+    couples = [(nth(begin), nth(begin + 1)), (nth(begin + 2), nth(begin + 3)), (nth(lone), nth(lone))]
+    for b, (va, vb) in enumerate(couples):
+        both = [speed_y[va], speed_y[vb]]
+        both = [0.5 * jnp.maximum(s, -s) for s in both]
+        half_block[b] = jnp.where(lane < LANES // 2, both[0], both[1])
+    mix = [[STEP_RATIO * coupling[v, w] for w in range(NVAR)] for v in range(NVAR)]
 
     def newton(v, guess, target):
         for _ in range(NEWTON):
@@ -371,119 +383,134 @@
             return c
         lax.fori_loop(0, (high - low) // 2, two, 0)
 
-    def differences(src, half, step, d_ref, t_ref):
-        def body(at):
+    def differences(src, half, step, d_ref, t_ref, at):
+        here = src[pl.ds(at, 8), :]
+        down = src[pl.ds(at + step, 8), :]
+        up = src[pl.ds(at - step, 8), :]
+        d = down - here
+        t = d - (here - up)
+        d_ref[pl.ds(at, 8), :] = d * half
+        t_ref[pl.ds(at, 8), :] = ((13.0 / 3.0) * (half * half)) * (t * t) + WENO_EPS
+
+    def faces(src, half, step, d_ref, t_ref, f_ref, at):
+        d3 = d_ref[pl.ds(at, 8), :]
+        d2 = d_ref[pl.ds(at - step, 8), :]
+        d1 = d_ref[pl.ds(at - 2 * step, 8), :]
+        d4 = d_ref[pl.ds(at + step, 8), :]
+        t1 = t_ref[pl.ds(at - step, 8), :]
+        t2 = t_ref[pl.ds(at, 8), :]
+        t3 = t_ref[pl.ds(at + step, 8), :]
+        f_ref[pl.ds(at, 8), :] = (6.0 * half) * src[pl.ds(at, 8), :] + weighted(
+            d1, d2, d3, d4, t1, t2, t3
+        )
+
+    def fluxes(src, n):
+        g0 = 7 - n // 2
+        octets = [GUARD + 8 * g for g in range(g0, g0 + n)]
+        if n <= 8:
+            middle = LANES // 2
+            blocks = []
+            for b, (va, vb) in enumerate(couples):
+                two = [src[v, pl.ds(octets[0] - 8 * (4 - n // 2), middle), :] for v in (va, vb)]
+                across[b][pl.ds(GUARD, LANES), :] = jnp.concatenate(two, axis=0).T
+                blocks.append((half_block[b], jnp.where(speed_y[va] >= 0.0, 1, -1)))
+        else:
             for v in range(NVAR):
-                here = src[v, pl.ds(at, 8), :]
-                down = src[v, pl.ds(at + step[v], 8), :]
-                up = src[v, pl.ds(at - step[v], 8), :]
-                d = (down - here) * half[v]
-                t = d - (here - up) * half[v]
-                d_ref[v, pl.ds(at, 8), :] = d
-                t_ref[v, pl.ds(at, 8), :] = (13.0 / 3.0) * (t * t) + WENO_EPS
-        return body
-
-    def faces(src, half, step, d_ref, t_ref, f_ref, shift=None):
-        def body(at):
+                across[v][pl.ds(GUARD, LANES), :] = src[v, pl.ds(GUARD - 8, LANES), :].T
+            blocks = list(zip(half_y, step_y))
+        for at in [octets[0] - 8] + octets + [octets[-1] + 8]:
             for v in range(NVAR):
-                s = step[v]
-                rows = at if shift is None else at + shift[v]
-                d3 = d_ref[v, pl.ds(rows, 8), :]
-                d2 = d_ref[v, pl.ds(rows - s, 8), :]
-                d1 = d_ref[v, pl.ds(rows - 2 * s, 8), :]
-                d4 = d_ref[v, pl.ds(rows + s, 8), :]
-                t1 = t_ref[v, pl.ds(rows - s, 8), :]
-                t2 = t_ref[v, pl.ds(rows, 8), :]
-                t3 = t_ref[v, pl.ds(rows + s, 8), :]
-                f_ref[v, pl.ds(rows, 8), :] = half[v] * src[v, pl.ds(rows, 8), :] + weighted(
-                    d1, d2, d3, d4, t1, t2, t3
-                )
-        return body
-
-    def fluxes(src, g0):
-        for v in range(NVAR):
-            across[v, pl.ds(GUARD, LANES), :] = src[v, pl.ds(GUARD - 8, LANES), :].T
-        pairs(-1, 17, differences(across, half_y, step_y, delta_y, curve_y))
-        row_faces = faces(across, half_y, step_y, delta_y, curve_y, face_y)
-        pairs(0, 16, row_faces)
-        faces(across, half_y, step_y, delta_y, curve_y, face_y,
-              [jnp.where(s >= 0.0, -8, LANES) for s in sy])(GUARD)
-        for v in range(NVAR):
-            rows_part[v] = (
-                face_y[v, pl.ds(GUARD, LANES), :] - face_y[v, pl.ds(GUARD - step_y[v], LANES), :]
+                differences(src.at[v], half_z[v], step_z[v], delta.at[v], curve.at[v], at)
+        for b, (half, step) in enumerate(blocks):
+            row = (across[b], half, step, delta_y[b], curve_y[b])
+            for i in range(-1, 17):
+                differences(*row, GUARD + 8 * i)
+            for i in range(16):
+                faces(*row, face_y[b], GUARD + 8 * i)
+            faces(*row, face_y[b], GUARD + jnp.where(step > 0, -8, LANES))
+            change = (
+                face_y[b][pl.ds(GUARD, LANES), :] - face_y[b][pl.ds(GUARD - step, LANES), :]
             ).T
-        pairs(g0 - 1, 15 - g0, differences(src, half_z, step_z, delta, curve))
-        pairs(g0, 14 - g0, faces(src, half_z, step_z, delta, curve, face))
+            if n <= 8:
+                rows = pl.ds(octets[0] - 8 * (4 - n // 2) - (GUARD - 8), middle)
+                rows_part[couples[b][0], rows, :] = change[:middle]
+                rows_part[couples[b][1], rows, :] = change[middle:]
+            else:
+                rows_part[b] = change
+        for at in octets:
+            for v in range(NVAR):
+                faces(src.at[v], half_z[v], step_z[v], delta.at[v], curve.at[v], face.at[v], at)
+        return octets
 
     def sources(src, at):
         field = [src[v, pl.ds(at, 8), :] for v in range(NVAR)]
         result = []
         for v in range(NVAR):
             columns = face[v, pl.ds(at, 8), :] - face[v, pl.ds(at - step_z[v], 8), :]
-            rows = rows_part[v, pl.ds(pl.multiple_of(at - (GUARD - 8), 8), 8), :]
-            mixed = (STEP_RATIO * coupling[v, 0]) * field[0]
+            rows = rows_part[v, pl.ds(at - (GUARD - 8), 8), :]
+            mixed = mix[v][0] * field[0]
             for w in range(1, NVAR):
-                mixed = mixed + (STEP_RATIO * coupling[v, w]) * field[w]
-            result.append(mixed - (2.0 * STEP_RATIO) * (rows + columns))
+                mixed = mixed + mix[v][w] * field[w]
+            result.append(mixed - (STEP_RATIO / 3.0) * (rows + columns))
         return field, result
 
-    def corrector(src, dst, station, g0):
-        fluxes(src, g0)
-
-        def step(at):
-            field, terms = sources(src, at)
-            fluid = blocked[station, pl.ds(at, 8), :]
+    def corrector(station, n):
+        for at in fluxes(cur, n):
+            field, terms = sources(cur, at)
+            fluid = blocked[station, pl.ds(at, 8), :] != 0.0
             for v in range(NVAR):
                 value = newton(v, field[v], still[v, pl.ds(at, 8), :] + terms[v])
-                dst[v, pl.ds(at, 8), :] = jnp.where(fluid != 0.0, value, 0.0)
-
-        pairs(g0, 14 - g0, step)
-
-    fluxes(inf, 0)
-
-    def prepare(at):
+                cur[v, pl.ds(at, 8), :] = jnp.where(fluid, value, 0.0)
+
+    for at in fluxes(inf, 14):
         field, terms = sources(inf, at)
         for v in range(NVAR):
             base[v, pl.ds(at, 8), :] = energy(v, field[v])
             work_inf[v, pl.ds(at, 8), :] = terms[v]
 
-    pairs(0, 14, prepare)
-
-    def iterate(k, carry):
-        old, new = s0.at[k % 2], s0.at[1 - k % 2]
-
-        def first_of_0(at):
-            fluid = blocked[0, pl.ds(at, 8), :]
-            for v in range(NVAR):
-                here = inf[v, pl.ds(at, 8), :]
-                prior = old[v, pl.ds(at, 8), :]
-                fixed = base[v, pl.ds(at, 8), :] - (1.0 - vig[v]) * (prior - here)
-                still[v, pl.ds(at, 8), :] = fixed
-                value = newton(v, here, fixed + work_inf[v, pl.ds(at, 8), :])
-                first[v, pl.ds(at, 8), :] = jnp.where(fluid != 0.0, value, 0.0)
-
-        g0 = (6 + 6 * k) // 8
-        pairs(g0, 14 - g0, first_of_0)
-        corrector(first, second, 0, (9 + 6 * k) // 8)
-        corrector(second, new, 0, (12 + 6 * k) // 8)
-
-        def start_of_1(at):
-            for v in range(NVAR):
-                above = new[v, pl.ds(at, 8), :]
-                prior = s1[v, pl.ds(at, 8), :] - old[v, pl.ds(at, 8), :]
-                still[v, pl.ds(at, 8), :] = energy(v, above) - (1.0 - vig[v]) * prior
-
-        g0 = (15 + 6 * k) // 8
-        pairs(g0, 14 - g0, start_of_1)
-        corrector(new, first, 1, g0)
-        corrector(first, second, 1, (18 + 6 * k) // 8)
-        corrector(second, s1, 1, (21 + 6 * k) // 8)
+    def first_of_0(at):
+        fluid = blocked[0, pl.ds(at, 8), :] != 0.0
+        for v in range(NVAR):
+            s1[v, pl.ds(at, 8), :] = cur[v, pl.ds(at, 8), :]
+            here = inf[v, pl.ds(at, 8), :]
+            prior = s0[v, pl.ds(at, 8), :]
+            fixed = base[v, pl.ds(at, 8), :] - (1.0 - vig[v]) * (prior - here)
+            still[v, pl.ds(at, 8), :] = fixed
+            value = newton(v, here, fixed + work_inf[v, pl.ds(at, 8), :])
+            cur[v, pl.ds(at, 8), :] = jnp.where(fluid, value, 0.0)
+
+    def start_of_1(at):
+        for v in range(NVAR):
+            above = cur[v, pl.ds(at, 8), :]
+            prior = s1[v, pl.ds(at, 8), :] - s0[v, pl.ds(at, 8), :]
+            still[v, pl.ds(at, 8), :] = energy(v, above) - (1.0 - vig[v]) * prior
+            s0[v, pl.ds(at, 8), :] = above
+
+    def pass_of(t, carry):
+        k, c = t // 5, t % 5
+
+        @pl.when(c == 0)
+        def _():
+            g0 = (6 + 6 * k) // 8
+            pairs(g0, 14 - g0, first_of_0)
+
+        @pl.when(c == 2)
+        def _():
+            g0 = (12 + 6 * k) // 8
+            pairs(g0, 14 - g0, start_of_1)
+
+        station = (c >= 2).astype(jnp.int32)
+        g0 = (9 + 6 * k + 3 * c) // 8
+        for n in (12, 10, 8, 6):
+            @pl.when(g0 == 7 - n // 2)
+            def _(n=n):
+                corrector(station, n)
         return carry
 
-    lax.fori_loop(0, ITERS, iterate, 0)
+    lax.fori_loop(0, 5 * ITERS, pass_of, 0)
 
     quarter = lane // PIECE
-    for station, result in enumerate((s0.at[ITERS % 2], s1)):
+    for station, result in enumerate((s0, cur)):
         for octet in range(4):
             field = [result[v, pl.ds(center + 8 * octet, 8), :] for v in range(NVAR)]
             for gy in range(4):
@@ -551,19 +578,17 @@
         name="assemble",
     )(got)
     window = pltpu.VMEM((NVAR, ROWS, LANES), jnp.float32)
-    plane = pltpu.VMEM((NVAR, LANES + 2 * GUARD, LANES), jnp.float32)
     sent = pl.pallas_call(
         main_kernel,
         out_shape=f32((MEMBERS, CHUNK_OUT, LANES)),
         in_specs=[smem] * 5 + [vmem] * 5,
         out_specs=vmem,
         scratch_shapes=[
-            window, window, window, window, window,
-            pltpu.VMEM((2, NVAR, ROWS, LANES), jnp.float32),
-            window, window, window, window, window,
+            window, window, window, window, window, window, window, window, window, window,
+            pltpu.VMEM((NVAR, LANES, LANES), jnp.float32),
             pltpu.VMEM((2, ROWS, LANES), jnp.float32),
-            plane, plane, plane, plane, pltpu.VMEM((NVAR, LANES, LANES), jnp.float32),
-        ],
+            pltpu.VMEM((3, 8, LANES), jnp.float32),
+        ] + [pltpu.VMEM((LANES + 2 * GUARD, LANES), jnp.float32)] * (4 * NVAR),
         compiler_params=pltpu.CompilerParams(vmem_limit_bytes=32 * 1024 * 1024),
         name="march",
     )(

time: 97.8 us -> 84.4 us (0.86)
  Pallas kernels: 50.2 us -> 36.7 us
    pallas_call x1, Pallas kernels: 44.2 us -> 30.7 us  [slabs_per_device(): pl.pallas_call(main_kernel, out_shape=f32((MEMBERS, CHUNK_OUT, LANES)), i...]
where the time goes in v3:
time: 84.4 us; the launch traced here: 83.9 us
  Pallas kernels  36.7 us (43%)
  blocking collectives  30.1 us (36%)
  starting transfers between devices  9.63 us (11%)
  waiting for transfers between devices  5.75 us (7%)
  local copies, waits for them, and re-layouts  0.98 us (1%)
    pallas_call x1, Pallas kernels, slabs_per_device(): pl.pallas_call(main_kernel, out_shape=f32((MEMBERS, CHUNK_OUT, LANES)), i...  30.7 us
    all_to_all x1, blocking collectives, slabs_per_device(): got = lax.all_to_all(packed, ('sec', 'gy'), 0, 0)  17.8 us
    all_to_all x1, blocking collectives, slabs_per_device(): returned = lax.all_to_all(sent, ('sec', 'gy'), 0, 0)  12.3 us
    ppermute x4, starting transfers between devices, along(): lax.ppermute(value, mesh_axes, [(path[i], path[i + steps]) for i in range...  9.63 us
    ppermute x4, waiting for transfers between devices, along(): lax.ppermute(value, mesh_axes, [(path[i], path[i + steps]) for i in range...  5.75 us
    pallas_call x1, Pallas kernels, slabs_per_device(): pl.pallas_call(assemble_kernel, out_shape=[f32((CHANNELS, SLAB, LANES)),...  2.13 us
    pallas_call x1, Pallas kernels, slabs_per_device(): pl.pallas_call(pack_kernel, out_shape=f32((MEMBERS, CHUNK_IN, LANES)), in...  2.06 us
    pallas_call x1, Pallas kernels, slabs_per_device(): pl.pallas_call(unpack_kernel, out_shape=f32((1, NVAR, PIECE, TILE)), in_s...  1.8 us
  transfers between devices with their start and end apart: 4, of which 2 were waited for; matrix products, arithmetic and copies ran while one was open for 0% of the time, Pallas kernels for 0%

profile of v3, /device:TPU:0, one launch (start us, length us, event | category | flops | bytes accessed | tf_op | source)
XLA Modules:
  0.0 83.9 jit_solution(1026665975514813761)
XLA Ops:
  0.0 0.6 pad_add_fusion.place
  0.6 2.1 %pack.1 = f32[8,72,128]{2,1,0:T(8,128)} custom-call(s32[4]{0:T(128)} %pad_add_fusion.place, f32[5,32,256]{2,1,0:T(8,128)} %inflow.1, f32[1,5,32,256]{3,2,1,0:T(8,128)} %initial.1, s32[1,32,256]{2,1,0:T(8,128)} %solid.1), custom_call_target="tpu_custom_call" | custom-call | tf_op jit(solution)/shard_map/pack/pallas_call | solution.py:554
  2.7 17.8 %all_to_all.10.got = f32[8,72,128]{2,1,0:T(8,128)} all-to-all(f32[8,72,128]{2,1,0:T(8,128)} %pack.1), channel_id=1, replica_groups=mesh['sec'=2,'gy'=4,'gz'=4] {'sec','gy'}, dimensions={0} | all-to-all | bytes 589824 | tf_op jit(solution)/shard_map/all_to_all | solution.py:566
  20.5 2.1 %assemble.1 = (f32[17,32,128]{2,1,0:T(8,128)}, f32[496,128]{1,0:T(8,128)}, f32[496,128]{1,0:T(8,128)}, f32[88,128]{1,0:T(8,128)}, f32[88,128]{1,0:T(8,128)}) custom-call(f32[8,72,128]{2,1,0:T(8,128)} %all_to_all.10.got), custom_call_target="tpu_custom_call" | custom-call | tf_op jit(solution)/shard_map/assemble/pallas_call | solution.py:567
  22.6 2.6 %collective-permute-start = (f32[496,128]{1,0:T(8,128)}, f32[496,128]{1,0:T(8,128)S(1)}, u32[]{:S(2)}, u32[]{:S(2)}) collective-permute-start(f32[496,128]{1,0:T(8,128)} %get-tuple-element.11), channel_id=1, source_target_pairs={{0,16},{16,20},{20,4},{4,8},{8,24},{24,28},{28,12},{12,13},{13,29}... | collective-permute-start | bytes 761864 | tf_op jit(solution)/shard_map/ppermute | solution.py:541
  25.2 1.3 %collective-permute-start.1 = (f32[496,128]{1,0:T(8,128)}, f32[496,128]{1,0:T(8,128)S(1)}, u32[]{:S(2)}, u32[]{:S(2)}) collective-permute-start(f32[496,128]{1,0:T(8,128)} %get-tuple-element.12), channel_id=1, source_target_pairs={{16,0},{20,16},{4,20},{8,4},{24,8},{28,24},{12,28},{13,12},{29,13}... | collective-permute-start | bytes 761864 | tf_op jit(solution)/shard_map/ppermute | solution.py:541
  26.5 4.4 %collective-permute-start.2 = (f32[88,128]{1,0:T(8,128)}, f32[88,128]{1,0:T(8,128)S(1)}, u32[]{:S(2)}, u32[]{:S(2)}) collective-permute-start(f32[88,128]{1,0:T(8,128)} %get-tuple-element.13), channel_id=1, source_target_pairs={{0,20},{16,4},{20,8},{4,24},{8,28},{24,12},{28,13},{12,29},{13,25}... | collective-permute-start | bytes 135176 | tf_op jit(solution)/shard_map/ppermute | solution.py:541
  31.0 0.0 copy-start.5
  31.0 0.0 copy-start.1
  31.0 0.0 copy-start.3
  31.0 0.0 copy-start.4
  31.0 1.3 %collective-permute-start.3 = (f32[88,128]{1,0:T(8,128)}, f32[88,128]{1,0:T(8,128)S(1)}, u32[]{:S(2)}, u32[]{:S(2)}) collective-permute-start(f32[88,128]{1,0:T(8,128)} %get-tuple-element.14), channel_id=1, source_target_pairs={{20,0},{4,16},{8,20},{24,4},{28,8},{12,24},{13,28},{29,12},{25,13}... | collective-permute-start | bytes 135176 | tf_op jit(solution)/shard_map/ppermute | solution.py:541
  32.3 0.7 collective-permute-done.2.from_left_two
  33.0 5.1 %collective-permute-done.3.from_right_two = f32[88,128]{1,0:T(8,128)S(1)} collective-permute-done((f32[88,128]{1,0:T(8,128)}, f32[88,128]{1,0:T(8,128)S(1)}, u32[]{:S(2)}, u32[]{:S(2)}) %collective-permute-start.3) | collective-permute-done | bytes 45088 | tf_op jit(solution)/shard_map/ppermute | solution.py:541
  38.1 0.0 collective-permute-done.from_left
  38.1 0.0 collective-permute-done.1.from_right
  38.1 0.0 copy-done.2
  38.1 0.0 copy-done.5
  38.1 0.0 copy-done.1
  38.1 0.0 copy-done.3
  38.1 0.9 %copy-done = f32[17,32,128]{2,1,0:T(8,128)S(1)} copy-done((f32[17,32,128]{2,1,0:T(8,128)S(1)}, f32[17,32,128]{2,1,0:T(8,128)}, u32[]{:S(2)}) %copy-start) | copy-done | bytes 278552
  39.1 30.7 %march.1 = f32[8,40,128]{2,1,0:T(8,128)S(1)} custom-call(s32[4]{0:T(128)S(1)} %copy-done.1, f32[5]{0:T(128)S(1)} %copy-done.3, f32[5]{0:T(128)S(1)} %copy-done.4, f32[5]{0:T(128)S(1)} %copy-done.5, f32[5,5]{1,0:T(8,128)S(1)} %copy-done.2, f32[17,32,128]{2,1,0:T(8,128)S(1)} %copy-done, f32[496,128]{1,0:T(8,128)S(1)} %collective-permute-done.from_left, ...), custom_call_target="tpu_custom_call" | custom-call | tf_op jit(solution)/shard_map/march/pallas_call | solution.py:581
  69.8 12.3 %all_to_all.11.got = f32[8,40,128]{2,1,0:T(8,128)} all-to-all(f32[8,40,128]{2,1,0:T(8,128)S(1)} %march.1), channel_id=1, replica_groups=mesh['sec'=2,'gy'=4,'gz'=4] {'sec','gy'}, dimensions={0} | all-to-all | bytes 327680 | tf_op jit(solution)/shard_map/all_to_all | solution.py:598
  82.1 1.8 %unpack.1 = f32[1,5,32,256]{3,2,1,0:T(8,128)} custom-call(s32[4]{0:T(128)} %pad_add_fusion.place, f32[8,40,128]{2,1,0:T(8,128)} %all_to_all.11.got), custom_call_target="tpu_custom_call" | custom-call | tf_op jit(solution)/shard_map/unpack/pallas_call | solution.py:599
  (3 shorter events, 0.0 us)
Async XLA Ops:
  22.6 15.5 %copy-start.2 = (f32[5,5]{1,0:T(8,128)S(1)}, f32[5,5]{1,0:T(8,128)}, u32[]{:S(2)}) copy-start(f32[5,5]{1,0:T(8,128)} %coupling.1) | copy-start | bytes 304
  22.6 15.5 %collective-permute-start = (f32[496,128]{1,0:T(8,128)}, f32[496,128]{1,0:T(8,128)S(1)}, u32[]{:S(2)}, u32[]{:S(2)}) collective-permute-start(f32[496,128]{1,0:T(8,128)} %get-tuple-element.11), channel_id=1, source_target_pairs={{0,16},{16,20},{20,4},{4,8},{8,24},{24,28},{28,12},{12,13},{13,29}... | collective-permute-start | bytes 761864 | tf_op jit(solution)/shard_map/ppermute | solution.py:541
  25.2 12.9 %collective-permute-start.1 = (f32[496,128]{1,0:T(8,128)}, f32[496,128]{1,0:T(8,128)S(1)}, u32[]{:S(2)}, u32[]{:S(2)}) collective-permute-start(f32[496,128]{1,0:T(8,128)} %get-tuple-element.12), channel_id=1, source_target_pairs={{16,0},{20,16},{4,20},{8,4},{24,8},{28,24},{12,28},{13,12},{29,13}... | collective-permute-start | bytes 761864 | tf_op jit(solution)/shard_map/ppermute | solution.py:541
  26.5 6.5 %collective-permute-start.2 = (f32[88,128]{1,0:T(8,128)}, f32[88,128]{1,0:T(8,128)S(1)}, u32[]{:S(2)}, u32[]{:S(2)}) collective-permute-start(f32[88,128]{1,0:T(8,128)} %get-tuple-element.13), channel_id=1, source_target_pairs={{0,20},{16,4},{20,8},{4,24},{8,28},{24,12},{28,13},{12,29},{13,25}... | collective-permute-start | bytes 135176 | tf_op jit(solution)/shard_map/ppermute | solution.py:541
  31.0 7.1 %copy-start.5 = (f32[5]{0:T(128)S(1)}, f32[5]{0:T(128)}, u32[]{:S(2)}) copy-start(f32[5]{0:T(128)} %vigneron.1) | copy-start | bytes 64
  31.0 7.1 %copy-start.1 = (s32[4]{0:T(128)S(1)}, s32[4]{0:T(128)}, u32[]{:S(2)}) copy-start(s32[4]{0:T(128)} %pad_add_fusion.place) | copy-start | bytes 52
  31.0 7.1 %copy-start.3 = (f32[5]{0:T(128)S(1)}, f32[5]{0:T(128)}, u32[]{:S(2)}) copy-start(f32[5]{0:T(128)} %speed_y.1) | copy-start | bytes 64
  31.0 7.1 %copy-start.4 = (f32[5]{0:T(128)S(1)}, f32[5]{0:T(128)}, u32[]{:S(2)}) copy-start(f32[5]{0:T(128)} %speed_z.1) | copy-start | bytes 64
  31.0 7.0 %collective-permute-start.3 = (f32[88,128]{1,0:T(8,128)}, f32[88,128]{1,0:T(8,128)S(1)}, u32[]{:S(2)}, u32[]{:S(2)}) collective-permute-start(f32[88,128]{1,0:T(8,128)} %get-tuple-element.14), channel_id=1, source_target_pairs={{20,0},{4,16},{8,20},{24,4},{28,8},{12,24},{13,28},{29,12},{25,13}... | collective-permute-start | bytes 135176 | tf_op jit(solution)/shard_map/ppermute | solution.py:541
  38.1 1.0 %copy-start = (f32[17,32,128]{2,1,0:T(8,128)S(1)}, f32[17,32,128]{2,1,0:T(8,128)}, u32[]{:S(2)}) copy-start(f32[17,32,128]{2,1,0:T(8,128)} %get-tuple-element.10.own) | copy-start | bytes 835588

commit v4 on v3

--- a/solution.py
+++ b/solution.py
@@ -168,63 +168,77 @@
     return jnp.where(odd, MEMBERS - 1 - j, j)
 
 
-def pack_kernel(place, inflow, initial, solid, out, stacked, turned_ref, solids):
-    sec, odd = place[0], place[1] == 1
+def own_place():
+    return lax.axis_index("sec"), lax.axis_index("gy"), lax.axis_index("gz") % 2 == 1
+
+
+def own_slab():
+    sec, gy, odd = own_place()
+    return lax.axis_index("gz") * MEMBERS + slab_of(sec * 4 + gy, odd)
+
+
+def slot(i, gy):
+    return (i + gy) % 4
+
+
+def pack_kernel(inflow, initial, solid, out, stacked, turned_ref, solids):
+    sec, gy, odd = own_place()
     for group in range(2):
         for p in range(4):
-            rows = pl.ds(p * PIECE, PIECE)
+            rows = pl.ds(pl.multiple_of(slot(p, gy) * PIECE, PIECE), PIECE)
             if group == 0:
-                stacked[rows, :] = initial[0, p]
+                stacked[group, rows, :] = initial[0, p]
             elif p == 0:
-                stacked[rows, :] = initial[0, 4]
+                stacked[group, rows, :] = initial[0, 4]
             else:
-                stacked[rows, :] = inflow[jnp.minimum(3 * sec + p - 1, NVAR - 1)]
-        for half in range(2):
-            turned_ref[pl.ds(half * LANES, LANES), :] = stacked[:, half * LANES:(half + 1) * LANES].T
-        for member in range(MEMBERS):
-            j = slab_of(member, odd)
-            out[member, pl.ds(group * SLAB, SLAB), :] = turned_ref[
-                pl.ds(pl.multiple_of(j * SLAB, SLAB), SLAB), :
-            ]
-    solids[...] = jnp.zeros_like(solids)
+                stacked[group, rows, :] = inflow[jnp.minimum(3 * sec + p - 1, NVAR - 1)]
     for half in range(2):
         solids[pl.ds(half * PIECE, PIECE), :] = solid[
             0, :, half * LANES:(half + 1) * LANES
         ].astype(jnp.float32)
-    turned_ref[pl.ds(0, LANES), :] = solids[...].T
+    solids[pl.ds(2 * PIECE, 2 * PIECE), :] = jnp.zeros((2 * PIECE, LANES), jnp.float32)
+    for group in range(2):
+        for half in range(2):
+            turned_ref[group, pl.ds(half * LANES, LANES), :] = stacked[
+                group, :, half * LANES:(half + 1) * LANES
+            ].T
+    turned_ref[2, pl.ds(0, LANES), :] = solids[...].T
     quarter = lane_iota() // PIECE
     for member in range(MEMBERS):
         j = slab_of(member, odd)
+        rows = pl.ds(pl.multiple_of(j * SLAB, SLAB), SLAB)
+        for group in range(2):
+            out[member, pl.ds(group * SLAB, SLAB), :] = turned_ref[group, rows, :]
         half, within = j // 4, j % 4
         packed = jnp.zeros((8, LANES), jnp.float32)
         for octet in range(4):
-            piece = turned_ref[pl.ds(pl.multiple_of(within * SLAB + octet * 8, 8), 8), :]
-            piece = pltpu.roll(piece, (PIECE * (octet - half)) % LANES, 1)
-            packed = jnp.where(quarter == octet, piece, packed)
+            piece = turned_ref[2, pl.ds(pl.multiple_of(within * SLAB + octet * 8, 8), 8), :]
+            to = slot(octet, gy)
+            piece = pltpu.roll(piece, (PIECE * (to - half)) & (LANES - 1), 1)
+            packed = jnp.where(quarter == to, piece, packed)
         out[member, pl.ds(2 * SLAB, 8), :] = packed
 
 
 def assemble_kernel(got, own, right_one, left_one, right_two, left_two):
     quarter = lane_iota() // PIECE
 
-    def gathered(sec, row, shift):
-        value = None
-        for gy in range(4):
-            piece = turned(got[sec * 4 + gy, pl.ds(row, 8), :], PIECE * gy - shift)
-            value = piece if value is None else jnp.where(quarter == gy, piece, value)
-        return value
+    def gathered(sec, row, i):
+        value = got[sec * 4, pl.ds(row, 8), :]
+        for gy in range(1, 4):
+            value = jnp.where(quarter == slot(i, gy), got[sec * 4 + gy, pl.ds(row, 8), :], value)
+        return turned(value, -PIECE * i)
 
     def source(channel, octet):
         if channel < 3:
-            return gathered(0, SLAB + 8 * octet, PIECE * (channel + 1))
+            return gathered(0, SLAB + 8 * octet, channel + 1)
         if channel < 5:
-            return gathered(1, SLAB + 8 * octet, PIECE * (channel - 2))
+            return gathered(1, SLAB + 8 * octet, channel - 2)
         sec, v = (channel - 5) // 6, (channel - 5) % 6
         if v < 4:
-            return gathered(sec, 8 * octet, PIECE * v)
+            return gathered(sec, 8 * octet, v)
         if v == 4:
             return gathered(sec, SLAB + 8 * octet, 0)
-        return gathered(sec, 2 * SLAB, PIECE * octet)
+        return gathered(sec, 2 * SLAB, octet)
 
     for channel in range(CHANNELS):
         for octet in range(4):
@@ -246,33 +260,38 @@
                     left_one[pl.ds(at + 8 * octet, 8), :] = value
 
 
-def unpack_kernel(place, got, out, stacked, packed):
-    odd = place[1] == 1
+def unpack_kernel(got, out, stacked, packed, turned_ref):
+    _, gy, odd = own_place()
     quarter = lane_iota() // PIECE
 
     def member_of(j):
         j = jnp.where(odd, MEMBERS - 1 - j, j)
-        gy = j // 2
-        sec = (j % 2 + gy % 2) % 2
-        return sec * 4 + gy
+        row_block = j // 2
+        return (j + row_block) % 2 * 4 + row_block
 
     for half in range(2):
         for within in range(4):
             member = member_of(4 * half + within)
-            stacked[pl.ds(within * SLAB, SLAB), :] = got[member, pl.ds(0, SLAB), :]
-        block = stacked[...].T
-        for v in range(4):
-            out[0, v, :, half * LANES:(half + 1) * LANES] = block[v * PIECE:(v + 1) * PIECE]
+            stacked[half, pl.ds(within * SLAB, SLAB), :] = got[member, pl.ds(0, SLAB), :]
     for within in range(4):
         low = got[member_of(within), pl.ds(SLAB, 8), :]
         high = got[member_of(4 + within), pl.ds(SLAB, 8), :]
         for octet in range(4):
+            back = -PIECE * slot(octet, gy)
             packed[pl.ds(within * SLAB + 8 * octet, 8), :] = jnp.where(
-                quarter == 0, turned(low, -PIECE * octet), turned(high, PIECE - PIECE * octet)
+                quarter == 0,
+                pltpu.roll(low, back & (LANES - 1), 1),
+                pltpu.roll(high, (back + PIECE) & (LANES - 1), 1),
             )
+    for half in range(2):
+        turned_ref[half] = stacked[half].T
     block = packed[...].T
     for half in range(2):
-        out[0, 4, :, half * LANES:(half + 1) * LANES] = block[half * PIECE:(half + 1) * PIECE]
+        columns = slice(half * LANES, (half + 1) * LANES)
+        for v in range(4):
+            rows = pl.ds(pl.multiple_of(slot(v, gy) * PIECE, PIECE), PIECE)
+            out[0, v, :, columns] = turned_ref[half, rows, :]
+        out[0, 4, :, columns] = block[half * PIECE:(half + 1) * PIECE]
 
 
 def weighted(d1, d2, d3, d4, t1, t2, t3):
@@ -289,7 +308,7 @@
 
 
 def main_kernel(
-    place, speed_y, speed_z, vigneron, coupling,
+    last, speed_y, speed_z, vigneron, coupling,
     own, from_left, from_right, from_left_two, from_right_two,
     out,
     inf, still, base, cur, s0, s1, work_inf, delta, curve, face, rows_part, blocked, half_block, *per_block,
@@ -321,7 +340,7 @@
         fill(cur.at[v], 11 + v, False)
     fill(blocked.at[0], 10, True)
     fill(blocked.at[1], 16, False)
-    slab, last = place[2], place[3]
+    slab = own_slab()
     for octet in range(ROWS // 8):
         rows = pl.ds(8 * octet, 8)
         column = slab * SLAB + 8 * octet - center + lax.broadcasted_iota(jnp.int32, (8, LANES), 0)
@@ -358,20 +377,24 @@
         both = [speed_y[va], speed_y[vb]]
         both = [0.5 * jnp.maximum(s, -s) for s in both]
         half_block[b] = jnp.where(lane < LANES // 2, both[0], both[1])
-    mix = [[STEP_RATIO * coupling[v, w] for w in range(NVAR)] for v in range(NVAR)]
+    per = [0.5 / vig[v] for v in range(NVAR)]
+    stiff = [(1.0 + vig[v]) * per[v] for v in range(NVAR)]
+    held = [(1.0 - vig[v]) * per[v] for v in range(NVAR)]
+    spread = [(STEP_RATIO / 3.0) * per[v] for v in range(NVAR)]
+    mix = [[STEP_RATIO * coupling[v, w] * per[v] for w in range(NVAR)] for v in range(NVAR)]
 
     def newton(v, guess, target):
         for _ in range(NEWTON):
             r = pltpu.reciprocal(1.0 + guess * guess, approx=True)
-            z = (2.0 * vig[v]) * r
-            over = (z * (1.0 - r)) * guess + target
-            under = z * (0.5 - r) + (1.0 + vig[v])
+            square = r * r
+            over = (r - square) * guess + target
+            under = (0.5 * r - square) + stiff[v]
             guess = over * pltpu.reciprocal(under, approx=True)
         return guess
 
     def energy(v, field):
         r = pltpu.reciprocal(1.0 + field * field, approx=True)
-        return field * ((1.0 + vig[v]) - vig[v] * r)
+        return field * (stiff[v] - 0.5 * r)
 
     def octet_rows(g):
         return pl.multiple_of(GUARD + 8 * g, 8)
@@ -451,7 +474,7 @@
             mixed = mix[v][0] * field[0]
             for w in range(1, NVAR):
                 mixed = mixed + mix[v][w] * field[w]
-            result.append(mixed - (STEP_RATIO / 3.0) * (rows + columns))
+            result.append(mixed - spread[v] * (rows + columns))
         return field, result
 
     def corrector(station, n):
@@ -474,7 +497,7 @@
             s1[v, pl.ds(at, 8), :] = cur[v, pl.ds(at, 8), :]
             here = inf[v, pl.ds(at, 8), :]
             prior = s0[v, pl.ds(at, 8), :]
-            fixed = base[v, pl.ds(at, 8), :] - (1.0 - vig[v]) * (prior - here)
+            fixed = base[v, pl.ds(at, 8), :] - held[v] * (prior - here)
             still[v, pl.ds(at, 8), :] = fixed
             value = newton(v, here, fixed + work_inf[v, pl.ds(at, 8), :])
             cur[v, pl.ds(at, 8), :] = jnp.where(fluid, value, 0.0)
@@ -483,7 +506,7 @@
         for v in range(NVAR):
             above = cur[v, pl.ds(at, 8), :]
             prior = s1[v, pl.ds(at, 8), :] - s0[v, pl.ds(at, 8), :]
-            still[v, pl.ds(at, 8), :] = energy(v, above) - (1.0 - vig[v]) * prior
+            still[v, pl.ds(at, 8), :] = energy(v, above) - held[v] * prior
             s0[v, pl.ds(at, 8), :] = above
 
     def pass_of(t, carry):
@@ -511,25 +534,26 @@
 
     quarter = lane // PIECE
     for station, result in enumerate((s0, cur)):
+        at_last = []
         for octet in range(4):
-            field = [result[v, pl.ds(center + 8 * octet, 8), :] for v in range(NVAR)]
+            rows = pl.ds(center + 8 * octet, 8)
+            field = [turned(result[v, rows, :], PIECE * v) for v in range(4)]
+            at_last.append(turned(result[4, rows, :], PIECE * octet))
             for gy in range(4):
-                member = station * 4 + gy
-                value = None
-                for p in range(4):
-                    piece = turned(field[p], PIECE * (p - gy))
-                    value = piece if value is None else jnp.where(quarter == p, piece, value)
-                out[member, pl.ds(8 * octet, 8), :] = value
-                piece = turned(field[4], PIECE * (octet - gy))
-                if octet > 0:
-                    piece = jnp.where(quarter == octet, piece, out[member, pl.ds(SLAB, 8), :])
-                out[member, pl.ds(SLAB, 8), :] = piece
+                value = field[0]
+                for v in range(1, 4):
+                    value = jnp.where(quarter == slot(v, gy), field[v], value)
+                out[station * 4 + gy, pl.ds(8 * octet, 8), :] = value
+        for gy in range(4):
+            value = at_last[0]
+            for octet in range(1, 4):
+                value = jnp.where(quarter == slot(octet, gy), at_last[octet], value)
+            out[station * 4 + gy, pl.ds(SLAB, 8), :] = value
 
 
 def slabs_per_device(inflow, initial, solid, speed_y, speed_z, vigneron, coupling):
     mesh_axes = ("sec", "gy", "gz")
     nz_parts = lax.axis_size("gz")
-    sec, gy, gz = (lax.axis_index(a) for a in mesh_axes)
     path = []
     for z in range(nz_parts):
         members = [(s, y) for y in range(4) for s in ((0, 1) if y % 2 == 0 else (1, 0))]
@@ -540,38 +564,32 @@
         low, high = max(0, -steps), min(count, count - steps)
         return lax.ppermute(value, mesh_axes, [(path[i], path[i + steps]) for i in range(low, high)])
 
-    odd = gz % 2
-    j = 2 * gy + (sec + gy) % 2
-    slab = gz * MEMBERS + jnp.where(odd == 1, MEMBERS - 1 - j, j)
-    place = jnp.stack(
-        [sec, odd, slab, jnp.asarray(len(path) * SLAB, jnp.int32)]
-    ).astype(jnp.int32)
-
     smem = pl.BlockSpec(memory_space=pltpu.SMEM)
     vmem = pl.BlockSpec(memory_space=pltpu.VMEM)
     f32 = functools.partial(jax.ShapeDtypeStruct, dtype=jnp.float32)
 
     packed = pl.pallas_call(
         pack_kernel,
-        out_shape=f32((MEMBERS, CHUNK_IN, LANES)),
-        in_specs=[smem, vmem, vmem, vmem],
+        out_shape=pltpu.VMEM((MEMBERS, CHUNK_IN, LANES), jnp.float32),
+        in_specs=[vmem, vmem, vmem],
         out_specs=vmem,
         scratch_shapes=[
-            pltpu.VMEM((LANES, TILE), jnp.float32),
-            pltpu.VMEM((TILE, LANES), jnp.float32),
+            pltpu.VMEM((2, LANES, TILE), jnp.float32),
+            pltpu.VMEM((3, TILE, LANES), jnp.float32),
             pltpu.VMEM((LANES, LANES), jnp.float32),
         ],
         name="pack",
-    )(place, inflow, initial, solid)
+    )(inflow, initial, solid)
     got = lax.all_to_all(packed, ("sec", "gy"), 0, 0)
+    got = pltpu.with_memory_space_constraint(got, pltpu.VMEM)
     own, right_one, left_one, right_two, left_two = pl.pallas_call(
         assemble_kernel,
         out_shape=[
-            f32((CHANNELS, SLAB, LANES)),
-            f32((EDGE_ONE, LANES)),
-            f32((EDGE_ONE, LANES)),
-            f32((EDGE_TWO, LANES)),
-            f32((EDGE_TWO, LANES)),
+            pltpu.VMEM((CHANNELS, SLAB, LANES), jnp.float32),
+            pltpu.VMEM((EDGE_ONE, LANES), jnp.float32),
+            pltpu.VMEM((EDGE_ONE, LANES), jnp.float32),
+            pltpu.VMEM((EDGE_TWO, LANES), jnp.float32),
+            pltpu.VMEM((EDGE_TWO, LANES), jnp.float32),
         ],
         in_specs=[vmem],
         out_specs=[vmem] * 5,
@@ -579,9 +597,9 @@
     )(got)
     window = pltpu.VMEM((NVAR, ROWS, LANES), jnp.float32)
     sent = pl.pallas_call(
-        main_kernel,
+        functools.partial(main_kernel, len(path) * SLAB),
         out_shape=f32((MEMBERS, CHUNK_OUT, LANES)),
-        in_specs=[smem] * 5 + [vmem] * 5,
+        in_specs=[smem] * 4 + [vmem] * 5,
         out_specs=vmem,
         scratch_shapes=[
             window, window, window, window, window, window, window, window, window, window,
@@ -592,21 +610,23 @@
         compiler_params=pltpu.CompilerParams(vmem_limit_bytes=32 * 1024 * 1024),
         name="march",
     )(
-        place, speed_y, speed_z, vigneron, coupling,
+        speed_y, speed_z, vigneron, coupling,
         own, along(right_one, 1), along(left_one, -1), along(right_two, 2), along(left_two, -2),
     )
     returned = lax.all_to_all(sent, ("sec", "gy"), 0, 0)
+    returned = pltpu.with_memory_space_constraint(returned, pltpu.VMEM)
     return pl.pallas_call(
         unpack_kernel,
         out_shape=f32((1, NVAR, PIECE, TILE)),
-        in_specs=[smem, vmem],
+        in_specs=[vmem],
         out_specs=vmem,
         scratch_shapes=[
+            pltpu.VMEM((2, LANES, LANES), jnp.float32),
             pltpu.VMEM((LANES, LANES), jnp.float32),
-            pltpu.VMEM((LANES, LANES), jnp.float32),
+            pltpu.VMEM((2, LANES, LANES), jnp.float32),
         ],
         name="unpack",
-    )(place, returned)
+    )(returned)
 
 
 def chosen(*args):

time: 84.4 us -> 77.6 us (0.919)
  Pallas kernels: 36.7 us -> 32.7 us
  blocking collectives: 30.1 us -> 29.1 us
  local copies, waits for them, and re-layouts: 0.98 us -> 0.03 us
    pallas_call x3, Pallas kernels: 34.9 us -> 31.9 us  [the longest x1 30.4 us: slabs_per_device(): pl.pallas_call(functools.partial(main_kernel, len(path) * SLAB), out_shap...]
    unnamed x12 -> x8, local copies, waits for them, and re-layouts: 0.98 us -> 0.03 us
    pallas_call x1, Pallas kernels: 1.8 us -> 0.86 us  [slabs_per_device(): pl.pallas_call(unpack_kernel, out_shape=f32((1, NVAR, PIECE, TILE)), in_s...]
where the time goes in v4:
time: 77.6 us; the launch traced here: 77.2 us
  Pallas kernels  32.7 us (42%)
  blocking collectives  29.1 us (38%)
  starting transfers between devices  9.65 us (12%)
  waiting for transfers between devices  5.54 us (7%)
    pallas_call x1, Pallas kernels, slabs_per_device(): pl.pallas_call(functools.partial(main_kernel, len(path) * SLAB), out_shap...  30.4 us
    all_to_all x1, blocking collectives, slabs_per_device(): got = lax.all_to_all(packed, ('sec', 'gy'), 0, 0)  17.5 us
    all_to_all x1, blocking collectives, slabs_per_device(): returned = lax.all_to_all(sent, ('sec', 'gy'), 0, 0)  11.6 us
    ppermute x4, starting transfers between devices, along(): lax.ppermute(value, mesh_axes, [(path[i], path[i + steps]) for i in range...  9.65 us
    ppermute x4, waiting for transfers between devices, along(): lax.ppermute(value, mesh_axes, [(path[i], path[i + steps]) for i in range...  5.54 us
  transfers between devices with their start and end apart: 4, of which 2 were waited for; matrix products, arithmetic and copies ran while one was open for 0% of the time, Pallas kernels for 0%

profile of v4, /device:TPU:0, one launch (start us, length us, event | category | flops | bytes accessed | tf_op | source)
XLA Modules:
  0.0 77.2 jit_solution(17997972185765779513)
XLA Ops:
  0.0 1.3 %pack.1 = f32[8,72,128]{2,1,0:T(8,128)S(1)} custom-call(f32[5,32,256]{2,1,0:T(8,128)} %inflow.1, f32[1,5,32,256]{3,2,1,0:T(8,128)} %initial.1, s32[1,32,256]{2,1,0:T(8,128)} %solid.1), custom_call_target="tpu_custom_call" | custom-call | tf_op jit(solution)/shard_map/pack/pallas_call | solution.py:571
  1.3 17.5 %all_to_all.10.got = f32[8,72,128]{2,1,0:T(8,128)S(1)} all-to-all(f32[8,72,128]{2,1,0:T(8,128)S(1)} %pack.1), channel_id=1, replica_groups=mesh['sec'=2,'gy'=4,'gz'=4] {'sec','gy'}, dimensions={0} | all-to-all | bytes 589824 | tf_op jit(solution)/shard_map/all_to_all | solution.py:583
  18.9 0.1 assemble.1
  19.0 0.0 copy-start
  19.0 2.5 %collective-permute-start = (f32[496,128]{1,0:T(8,128)S(1)}, f32[496,128]{1,0:T(8,128)S(1)}, u32[]{:S(2)}, u32[]{:S(2)}) collective-permute-start(f32[496,128]{1,0:T(8,128)S(1)} %get-tuple-element.11), channel_id=1, source_target_pairs={{0,16},{16,20},{20,4},{4,8},{8,24},{24,28},{28,12},{12,13},{13,29}... | collective-permute-start | bytes 761864 | tf_op jit(solution)/shard_map/ppermute | solution.py:565
  21.5 1.3 %collective-permute-start.1 = (f32[496,128]{1,0:T(8,128)S(1)}, f32[496,128]{1,0:T(8,128)S(1)}, u32[]{:S(2)}, u32[]{:S(2)}) collective-permute-start(f32[496,128]{1,0:T(8,128)S(1)} %get-tuple-element.12), channel_id=1, source_target_pairs={{16,0},{20,16},{4,20},{8,4},{24,8},{28,24},{12,28},{13,12},{29,13}... | collective-permute-start | bytes 761864 | tf_op jit(solution)/shard_map/ppermute | solution.py:565
  22.8 4.5 %collective-permute-start.2 = (f32[88,128]{1,0:T(8,128)S(1)}, f32[88,128]{1,0:T(8,128)S(1)}, u32[]{:S(2)}, u32[]{:S(2)}) collective-permute-start(f32[88,128]{1,0:T(8,128)S(1)} %get-tuple-element.13), channel_id=1, source_target_pairs={{0,20},{16,4},{20,8},{4,24},{8,28},{24,12},{28,13},{12,29},{13,25}... | collective-permute-start | bytes 135176 | tf_op jit(solution)/shard_map/ppermute | solution.py:565
  27.2 0.0 copy-start.1
  27.3 0.0 copy-start.2
  27.3 0.0 copy-start.3
  27.3 1.4 %collective-permute-start.3 = (f32[88,128]{1,0:T(8,128)S(1)}, f32[88,128]{1,0:T(8,128)S(1)}, u32[]{:S(2)}, u32[]{:S(2)}) collective-permute-start(f32[88,128]{1,0:T(8,128)S(1)} %get-tuple-element.14), channel_id=1, source_target_pairs={{20,0},{4,16},{8,20},{24,4},{28,8},{12,24},{13,28},{29,12},{25,13}... | collective-permute-start | bytes 135176 | tf_op jit(solution)/shard_map/ppermute | solution.py:565
  28.7 0.2 collective-permute-done.2.from_left_two
  28.9 5.3 %collective-permute-done.3.from_right_two = f32[88,128]{1,0:T(8,128)S(1)} collective-permute-done((f32[88,128]{1,0:T(8,128)S(1)}, f32[88,128]{1,0:T(8,128)S(1)}, u32[]{:S(2)}, u32[]{:S(2)}) %collective-permute-start.3) | collective-permute-done | bytes 45088 | tf_op jit(solution)/shard_map/ppermute | solution.py:565
  34.2 0.0 collective-permute-done.from_left
  34.3 0.0 collective-permute-done.1.from_right
  34.3 0.0 copy-done
  34.3 0.0 copy-done.1
  34.3 0.0 copy-done.2
  34.3 0.0 copy-done.3
  34.3 30.4 %march.1 = f32[8,40,128]{2,1,0:T(8,128)S(1)} custom-call(f32[5]{0:T(128)S(1)} %copy-done.1, f32[5]{0:T(128)S(1)} %copy-done.2, f32[5]{0:T(128)S(1)} %copy-done.3, f32[5,5]{1,0:T(8,128)S(1)} %copy-done, f32[17,32,128]{2,1,0:T(8,128)S(1)} %get-tuple-element.10.own, f32[496,128]{1,0:T(8,128)S(1)} %collective-permute-done.from_left, ...), custom_call_target="tpu_custom_call" | custom-call | tf_op jit(solution)/shard_map/march/pallas_call | solution.py:599
  64.7 11.6 %all_to_all.11.got = f32[8,40,128]{2,1,0:T(8,128)S(1)} all-to-all(f32[8,40,128]{2,1,0:T(8,128)S(1)} %march.1), channel_id=1, replica_groups=mesh['sec'=2,'gy'=4,'gz'=4] {'sec','gy'}, dimensions={0} | all-to-all | bytes 327680 | tf_op jit(solution)/shard_map/all_to_all | solution.py:616
  76.3 0.9 %unpack.1 = f32[1,5,32,256]{3,2,1,0:T(8,128)} custom-call(f32[8,40,128]{2,1,0:T(8,128)S(1)} %all_to_all.11.got), custom_call_target="tpu_custom_call" | custom-call | tf_op jit(solution)/shard_map/unpack/pallas_call | solution.py:618
Async XLA Ops:
  19.0 15.3 %copy-start = (f32[5,5]{1,0:T(8,128)S(1)}, f32[5,5]{1,0:T(8,128)}, u32[]{:S(2)}) copy-start(f32[5,5]{1,0:T(8,128)} %coupling.1) | copy-start | bytes 304
  19.0 15.3 %collective-permute-start = (f32[496,128]{1,0:T(8,128)S(1)}, f32[496,128]{1,0:T(8,128)S(1)}, u32[]{:S(2)}, u32[]{:S(2)}) collective-permute-start(f32[496,128]{1,0:T(8,128)S(1)} %get-tuple-element.11), channel_id=1, source_target_pairs={{0,16},{16,20},{20,4},{4,8},{8,24},{24,28},{28,12},{12,13},{13,29}... | collective-permute-start | bytes 761864 | tf_op jit(solution)/shard_map/ppermute | solution.py:565
  21.5 12.8 %collective-permute-start.1 = (f32[496,128]{1,0:T(8,128)S(1)}, f32[496,128]{1,0:T(8,128)S(1)}, u32[]{:S(2)}, u32[]{:S(2)}) collective-permute-start(f32[496,128]{1,0:T(8,128)S(1)} %get-tuple-element.12), channel_id=1, source_target_pairs={{16,0},{20,16},{4,20},{8,4},{24,8},{28,24},{12,28},{13,12},{29,13}... | collective-permute-start | bytes 761864 | tf_op jit(solution)/shard_map/ppermute | solution.py:565
  22.8 6.2 %collective-permute-start.2 = (f32[88,128]{1,0:T(8,128)S(1)}, f32[88,128]{1,0:T(8,128)S(1)}, u32[]{:S(2)}, u32[]{:S(2)}) collective-permute-start(f32[88,128]{1,0:T(8,128)S(1)} %get-tuple-element.13), channel_id=1, source_target_pairs={{0,20},{16,4},{20,8},{4,24},{8,28},{24,12},{28,13},{12,29},{13,25}... | collective-permute-start | bytes 135176 | tf_op jit(solution)/shard_map/ppermute | solution.py:565
  27.2 7.0 %copy-start.1 = (f32[5]{0:T(128)S(1)}, f32[5]{0:T(128)}, u32[]{:S(2)}) copy-start(f32[5]{0:T(128)} %speed_y.1) | copy-start | bytes 64
  27.3 7.0 %copy-start.2 = (f32[5]{0:T(128)S(1)}, f32[5]{0:T(128)}, u32[]{:S(2)}) copy-start(f32[5]{0:T(128)} %speed_z.1) | copy-start | bytes 64
  27.3 7.0 %copy-start.3 = (f32[5]{0:T(128)S(1)}, f32[5]{0:T(128)}, u32[]{:S(2)}) copy-start(f32[5]{0:T(128)} %vigneron.1) | copy-start | bytes 64
  27.3 7.0 %collective-permute-start.3 = (f32[88,128]{1,0:T(8,128)S(1)}, f32[88,128]{1,0:T(8,128)S(1)}, u32[]{:S(2)}, u32[]{:S(2)}) collective-permute-start(f32[88,128]{1,0:T(8,128)S(1)} %get-tuple-element.14), channel_id=1, source_target_pairs={{20,0},{4,16},{8,20},{24,4},{28,8},{12,24},{13,28},{29,12},{25,13}... | collective-permute-start | bytes 135176 | tf_op jit(solution)/shard_map/ppermute | solution.py:565

commit v5 on v4

--- a/solution.py
+++ b/solution.py
@@ -149,7 +149,8 @@
 CHUNK_OUT = 40
 NEAR = 24
 EDGE_ONE = 11 * SLAB + 6 * NEAR
-EDGE_TWO = 11 * 8
+FAR = 4
+EDGE_TWO = 32
 CHANNELS = 17
 
 
@@ -219,6 +220,10 @@
         out[member, pl.ds(2 * SLAB, 8), :] = packed
 
 
+def far_rows(channel):
+    return (FAR * channel, FAR) if channel < NVAR else (FAR * NVAR + channel - NVAR, 1)
+
+
 def assemble_kernel(got, own, right_one, left_one, right_two, left_two):
     quarter = lane_iota() // PIECE
 
@@ -240,6 +245,8 @@
             return gathered(sec, SLAB + 8 * octet, 0)
         return gathered(sec, 2 * SLAB, octet)
 
+    for ref in (right_two, left_two):
+        ref[...] = jnp.zeros((EDGE_TWO, LANES), jnp.float32)
     for channel in range(CHANNELS):
         for octet in range(4):
             value = source(channel, octet)
@@ -248,10 +255,11 @@
                 rows = pl.ds(channel * SLAB + 8 * octet, 8)
                 right_one[rows, :] = value
                 left_one[rows, :] = value
+                at, width = far_rows(channel)
                 if octet == 3:
-                    right_two[pl.ds(8 * channel, 8), :] = value
+                    right_two[pl.ds(at, width), :] = value[8 - width:]
                 if octet == 0:
-                    left_two[pl.ds(8 * channel, 8), :] = value
+                    left_two[pl.ds(at, width), :] = value[:width]
             else:
                 at = 11 * SLAB + (channel - 11) * NEAR
                 if octet > 0:
@@ -322,10 +330,14 @@
         ref[pl.ds(ROWS - GUARD, GUARD), :] = jnp.zeros((GUARD, LANES), jnp.float32)
         ref[pl.ds(center, SLAB), :] = own[channel]
         if wide:
-            ref[pl.ds(GUARD, 8), :] = from_left_two[pl.ds(8 * channel, 8), :]
+            zeros = jnp.zeros((8, LANES), jnp.float32)
+            far, width = far_rows(channel)
+            ref[pl.ds(GUARD, 8), :] = zeros
+            ref[pl.ds(GUARD + 8 - width, width), :] = from_left_two[pl.ds(far, width), :]
             ref[pl.ds(GUARD + 8, SLAB), :] = from_left[pl.ds(SLAB * channel, SLAB), :]
             ref[pl.ds(center + SLAB, SLAB), :] = from_right[pl.ds(SLAB * channel, SLAB), :]
-            ref[pl.ds(center + 2 * SLAB, 8), :] = from_right_two[pl.ds(8 * channel, 8), :]
+            ref[pl.ds(center + 2 * SLAB, 8), :] = zeros
+            ref[pl.ds(center + 2 * SLAB, width), :] = from_right_two[pl.ds(far, width), :]
         else:
             at = 11 * SLAB + (channel - 11) * NEAR
             zeros = jnp.zeros((16, LANES), jnp.float32)
@@ -427,43 +439,61 @@
             d1, d2, d3, d4, t1, t2, t3
         )
 
-    def fluxes(src, n):
+    def octets_of(n):
         g0 = 7 - n // 2
-        octets = [GUARD + 8 * g for g in range(g0, g0 + n)]
-        if n <= 8:
-            middle = LANES // 2
-            blocks = []
-            for b, (va, vb) in enumerate(couples):
-                two = [src[v, pl.ds(octets[0] - 8 * (4 - n // 2), middle), :] for v in (va, vb)]
-                across[b][pl.ds(GUARD, LANES), :] = jnp.concatenate(two, axis=0).T
-                blocks.append((half_block[b], jnp.where(speed_y[va] >= 0.0, 1, -1)))
-        else:
+        return [GUARD + 8 * g for g in range(g0, g0 + n)]
+
+    def blocks_of(n):
+        if n > 8:
+            return list(zip(half_y, step_y))
+        return [
+            (half_block[b], jnp.where(speed_y[va] >= 0.0, 1, -1))
+            for b, (va, _) in enumerate(couples)
+        ]
+
+    middle = LANES // 2
+    narrow = pl.ds(GUARD + 24, middle)
+
+    def turn_in(src, n):
+        if n > 8:
             for v in range(NVAR):
                 across[v][pl.ds(GUARD, LANES), :] = src[v, pl.ds(GUARD - 8, LANES), :].T
-            blocks = list(zip(half_y, step_y))
+        else:
+            for b, couple in enumerate(couples):
+                two = [src[v, narrow, :] for v in couple]
+                across[b][pl.ds(GUARD, LANES), :] = jnp.concatenate(two, axis=0).T
+
+    def column_differences(src, n):
+        octets = octets_of(n)
         for at in [octets[0] - 8] + octets + [octets[-1] + 8]:
             for v in range(NVAR):
                 differences(src.at[v], half_z[v], step_z[v], delta.at[v], curve.at[v], at)
-        for b, (half, step) in enumerate(blocks):
+
+    def column_faces(src, octets):
+        for at in octets:
+            for v in range(NVAR):
+                faces(src.at[v], half_z[v], step_z[v], delta.at[v], curve.at[v], face.at[v], at)
+
+    def row_faces(n):
+        for b, (half, step) in enumerate(blocks_of(n)):
             row = (across[b], half, step, delta_y[b], curve_y[b])
             for i in range(-1, 17):
                 differences(*row, GUARD + 8 * i)
             for i in range(16):
                 faces(*row, face_y[b], GUARD + 8 * i)
             faces(*row, face_y[b], GUARD + jnp.where(step > 0, -8, LANES))
+
+    def turn_out(n):
+        for b, (_, step) in enumerate(blocks_of(n)):
             change = (
                 face_y[b][pl.ds(GUARD, LANES), :] - face_y[b][pl.ds(GUARD - step, LANES), :]
             ).T
-            if n <= 8:
-                rows = pl.ds(octets[0] - 8 * (4 - n // 2) - (GUARD - 8), middle)
+            if n > 8:
+                rows_part[b] = change
+            else:
+                rows = pl.ds(8 + 24, middle)
                 rows_part[couples[b][0], rows, :] = change[:middle]
                 rows_part[couples[b][1], rows, :] = change[middle:]
-            else:
-                rows_part[b] = change
-        for at in octets:
-            for v in range(NVAR):
-                faces(src.at[v], half_z[v], step_z[v], delta.at[v], curve.at[v], face.at[v], at)
-        return octets
 
     def sources(src, at):
         field = [src[v, pl.ds(at, 8), :] for v in range(NVAR)]
@@ -477,15 +507,20 @@
             result.append(mixed - spread[v] * (rows + columns))
         return field, result
 
-    def corrector(station, n):
-        for at in fluxes(cur, n):
+    def steps(station, octets):
+        for at in octets:
             field, terms = sources(cur, at)
             fluid = blocked[station, pl.ds(at, 8), :] != 0.0
             for v in range(NVAR):
                 value = newton(v, field[v], still[v, pl.ds(at, 8), :] + terms[v])
                 cur[v, pl.ds(at, 8), :] = jnp.where(fluid, value, 0.0)
 
-    for at in fluxes(inf, 14):
+    turn_in(inf, 14)
+    column_differences(inf, 14)
+    row_faces(14)
+    turn_out(14)
+    column_faces(inf, octets_of(14))
+    for at in octets_of(14):
         field, terms = sources(inf, at)
         for v in range(NVAR):
             base[v, pl.ds(at, 8), :] = energy(v, field[v])
@@ -525,9 +560,26 @@
         station = (c >= 2).astype(jnp.int32)
         g0 = (9 + 6 * k + 3 * c) // 8
         for n in (12, 10, 8, 6):
-            @pl.when(g0 == 7 - n // 2)
-            def _(n=n):
-                corrector(station, n)
+            times = (g0 == 7 - n // 2).astype(jnp.int32)
+
+            def part(i, c, n=n):
+                turn_in(cur, n)
+                column_differences(cur, n)
+                column_faces(cur, octets_of(n)[:n // 2])
+                return c
+            lax.fori_loop(0, times, part, 0)
+
+            def part(i, c, n=n):
+                row_faces(n)
+                return c
+            lax.fori_loop(0, times, part, 0)
+
+            def part(i, c, n=n):
+                turn_out(n)
+                column_faces(cur, octets_of(n)[n // 2:])
+                steps(station, octets_of(n))
+                return c
+            lax.fori_loop(0, times, part, 0)
         return carry
 
     lax.fori_loop(0, 5 * ITERS, pass_of, 0)

time: 77.6 us -> 75.8 us (0.977)
  Pallas kernels: 32.7 us -> 31.4 us
    pallas_call x1, Pallas kernels: 30.4 us -> 29.1 us  [slabs_per_device(): pl.pallas_call(functools.partial(main_kernel, len(path) * SLAB), out_shap...]
  transfers between devices with their start and end apart: 4 -> 4, of which waited for: 2 -> 1; matrix products, arithmetic and copies ran while one was open for 0% -> 0% of each run, Pallas kernels for 0% -> 0%
where the time goes in v5:
time: 75.8 us; the launch traced here: 75.5 us
  Pallas kernels  31.4 us (41%)
  blocking collectives  29.1 us (38%)
  starting transfers between devices  9.65 us (13%)
  waiting for transfers between devices  5.23 us (7%)
    pallas_call x1, Pallas kernels, slabs_per_device(): pl.pallas_call(functools.partial(main_kernel, len(path) * SLAB), out_shap...  29.1 us
    all_to_all x1, blocking collectives, slabs_per_device(): got = lax.all_to_all(packed, ('sec', 'gy'), 0, 0)  17.5 us
    all_to_all x1, blocking collectives, slabs_per_device(): returned = lax.all_to_all(sent, ('sec', 'gy'), 0, 0)  11.6 us
    ppermute x4, starting transfers between devices, along(): lax.ppermute(value, mesh_axes, [(path[i], path[i + steps]) for i in range...  9.65 us
    ppermute x4, waiting for transfers between devices, along(): lax.ppermute(value, mesh_axes, [(path[i], path[i + steps]) for i in range...  5.23 us
  transfers between devices with their start and end apart: 4, of which 1 were waited for; matrix products, arithmetic and copies ran while one was open for 0% of the time, Pallas kernels for 0%

profile of v5, /device:TPU:0, one launch (start us, length us, event | category | flops | bytes accessed | tf_op | source)
XLA Modules:
  0.0 75.5 jit_solution(7076091740507853841)
XLA Ops:
  0.0 1.3 %pack.1 = f32[8,72,128]{2,1,0:T(8,128)S(1)} custom-call(f32[5,32,256]{2,1,0:T(8,128)} %inflow.1, f32[1,5,32,256]{3,2,1,0:T(8,128)} %initial.1, s32[1,32,256]{2,1,0:T(8,128)} %solid.1), custom_call_target="tpu_custom_call" | custom-call | tf_op jit(solution)/shard_map/pack/pallas_call | solution.py:623
  1.3 17.5 %all_to_all.10.got = f32[8,72,128]{2,1,0:T(8,128)S(1)} all-to-all(f32[8,72,128]{2,1,0:T(8,128)S(1)} %pack.1), channel_id=1, replica_groups=mesh['sec'=2,'gy'=4,'gz'=4] {'sec','gy'}, dimensions={0} | all-to-all | bytes 589824 | tf_op jit(solution)/shard_map/all_to_all | solution.py:635
  18.9 0.1 assemble.1
  19.0 0.0 copy-start
  19.0 2.5 %collective-permute-start = (f32[496,128]{1,0:T(8,128)S(1)}, f32[496,128]{1,0:T(8,128)S(1)}, u32[]{:S(2)}, u32[]{:S(2)}) collective-permute-start(f32[496,128]{1,0:T(8,128)S(1)} %get-tuple-element.11), channel_id=1, source_target_pairs={{0,16},{16,20},{20,4},{4,8},{8,24},{24,28},{28,12},{12,13},{13,29}... | collective-permute-start | bytes 761864 | tf_op jit(solution)/shard_map/ppermute | solution.py:617
  21.5 1.3 %collective-permute-start.1 = (f32[496,128]{1,0:T(8,128)S(1)}, f32[496,128]{1,0:T(8,128)S(1)}, u32[]{:S(2)}, u32[]{:S(2)}) collective-permute-start(f32[496,128]{1,0:T(8,128)S(1)} %get-tuple-element.12), channel_id=1, source_target_pairs={{16,0},{20,16},{4,20},{8,4},{24,8},{28,24},{12,28},{13,12},{29,13}... | collective-permute-start | bytes 761864 | tf_op jit(solution)/shard_map/ppermute | solution.py:617
  22.8 4.4 %collective-permute-start.2 = (f32[32,128]{1,0:T(8,128)S(1)}, f32[32,128]{1,0:T(8,128)S(1)}, u32[]{:S(2)}, u32[]{:S(2)}) collective-permute-start(f32[32,128]{1,0:T(8,128)S(1)} %get-tuple-element.13), channel_id=1, source_target_pairs={{0,20},{16,4},{20,8},{4,24},{8,28},{24,12},{28,13},{12,29},{13,25}... | collective-permute-start | bytes 49160 | tf_op jit(solution)/shard_map/ppermute | solution.py:617
  27.2 0.0 copy-start.1
  27.3 0.0 copy-start.2
  27.3 0.0 copy-start.3
  27.3 1.4 %collective-permute-start.3 = (f32[32,128]{1,0:T(8,128)S(1)}, f32[32,128]{1,0:T(8,128)S(1)}, u32[]{:S(2)}, u32[]{:S(2)}) collective-permute-start(f32[32,128]{1,0:T(8,128)S(1)} %get-tuple-element.14), channel_id=1, source_target_pairs={{20,0},{4,16},{8,20},{24,4},{28,8},{12,24},{13,28},{29,12},{25,13}... | collective-permute-start | bytes 49160 | tf_op jit(solution)/shard_map/ppermute | solution.py:617
  28.7 0.0 collective-permute-done.2.from_left_two
  28.7 5.2 %collective-permute-done.3.from_right_two = f32[32,128]{1,0:T(8,128)S(1)} collective-permute-done((f32[32,128]{1,0:T(8,128)S(1)}, f32[32,128]{1,0:T(8,128)S(1)}, u32[]{:S(2)}, u32[]{:S(2)}) %collective-permute-start.3) | collective-permute-done | bytes 16416 | tf_op jit(solution)/shard_map/ppermute | solution.py:617
  33.9 0.0 collective-permute-done.from_left
  33.9 0.0 collective-permute-done.1.from_right
  33.9 0.0 copy-done
  34.0 0.0 copy-done.1
  34.0 0.0 copy-done.2
  34.0 0.0 copy-done.3
  34.0 29.1 %march.1 = f32[8,40,128]{2,1,0:T(8,128)S(1)} custom-call(f32[5]{0:T(128)S(1)} %copy-done.1, f32[5]{0:T(128)S(1)} %copy-done.2, f32[5]{0:T(128)S(1)} %copy-done.3, f32[5,5]{1,0:T(8,128)S(1)} %copy-done, f32[17,32,128]{2,1,0:T(8,128)S(1)} %get-tuple-element.10.own, f32[496,128]{1,0:T(8,128)S(1)} %collective-permute-done.from_left, ...), custom_call_target="tpu_custom_call" | custom-call | tf_op jit(solution)/shard_map/march/pallas_call | solution.py:651
  63.1 11.6 %all_to_all.11.got = f32[8,40,128]{2,1,0:T(8,128)S(1)} all-to-all(f32[8,40,128]{2,1,0:T(8,128)S(1)} %march.1), channel_id=1, replica_groups=mesh['sec'=2,'gy'=4,'gz'=4] {'sec','gy'}, dimensions={0} | all-to-all | bytes 327680 | tf_op jit(solution)/shard_map/all_to_all | solution.py:668
  74.7 0.9 %unpack.1 = f32[1,5,32,256]{3,2,1,0:T(8,128)} custom-call(f32[8,40,128]{2,1,0:T(8,128)S(1)} %all_to_all.11.got), custom_call_target="tpu_custom_call" | custom-call | tf_op jit(solution)/shard_map/unpack/pallas_call | solution.py:670
Async XLA Ops:
  19.0 15.0 %copy-start = (f32[5,5]{1,0:T(8,128)S(1)}, f32[5,5]{1,0:T(8,128)}, u32[]{:S(2)}) copy-start(f32[5,5]{1,0:T(8,128)} %coupling.1) | copy-start | bytes 304
  19.0 14.9 %collective-permute-start = (f32[496,128]{1,0:T(8,128)S(1)}, f32[496,128]{1,0:T(8,128)S(1)}, u32[]{:S(2)}, u32[]{:S(2)}) collective-permute-start(f32[496,128]{1,0:T(8,128)S(1)} %get-tuple-element.11), channel_id=1, source_target_pairs={{0,16},{16,20},{20,4},{4,8},{8,24},{24,28},{28,12},{12,13},{13,29}... | collective-permute-start | bytes 761864 | tf_op jit(solution)/shard_map/ppermute | solution.py:617
  21.5 12.5 %collective-permute-start.1 = (f32[496,128]{1,0:T(8,128)S(1)}, f32[496,128]{1,0:T(8,128)S(1)}, u32[]{:S(2)}, u32[]{:S(2)}) collective-permute-start(f32[496,128]{1,0:T(8,128)S(1)} %get-tuple-element.12), channel_id=1, source_target_pairs={{16,0},{20,16},{4,20},{8,4},{24,8},{28,24},{12,28},{13,12},{29,13}... | collective-permute-start | bytes 761864 | tf_op jit(solution)/shard_map/ppermute | solution.py:617
  22.8 5.9 %collective-permute-start.2 = (f32[32,128]{1,0:T(8,128)S(1)}, f32[32,128]{1,0:T(8,128)S(1)}, u32[]{:S(2)}, u32[]{:S(2)}) collective-permute-start(f32[32,128]{1,0:T(8,128)S(1)} %get-tuple-element.13), channel_id=1, source_target_pairs={{0,20},{16,4},{20,8},{4,24},{8,28},{24,12},{28,13},{12,29},{13,25}... | collective-permute-start | bytes 49160 | tf_op jit(solution)/shard_map/ppermute | solution.py:617
  27.2 6.7 %copy-start.1 = (f32[5]{0:T(128)S(1)}, f32[5]{0:T(128)}, u32[]{:S(2)}) copy-start(f32[5]{0:T(128)} %speed_y.1) | copy-start | bytes 64
  27.3 6.7 %copy-start.2 = (f32[5]{0:T(128)S(1)}, f32[5]{0:T(128)}, u32[]{:S(2)}) copy-start(f32[5]{0:T(128)} %speed_z.1) | copy-start | bytes 64
  27.3 6.7 %copy-start.3 = (f32[5]{0:T(128)S(1)}, f32[5]{0:T(128)}, u32[]{:S(2)}) copy-start(f32[5]{0:T(128)} %vigneron.1) | copy-start | bytes 64
  27.3 6.7 %collective-permute-start.3 = (f32[32,128]{1,0:T(8,128)S(1)}, f32[32,128]{1,0:T(8,128)S(1)}, u32[]{:S(2)}, u32[]{:S(2)}) collective-permute-start(f32[32,128]{1,0:T(8,128)S(1)} %get-tuple-element.14), channel_id=1, source_target_pairs={{20,0},{4,16},{8,20},{24,4},{28,8},{12,24},{13,28},{29,12},{25,13}... | collective-permute-start | bytes 49160 | tf_op jit(solution)/shard_map/ppermute | solution.py:617

commit v6 on v5

--- a/solution.py
+++ b/solution.py
@@ -143,6 +143,7 @@
 MEMBERS = 8
 PIECE = 32
 GUARD = 16
+STRIP = 80
 LEFT = 40
 ROWS = GUARD + LEFT + SLAB + LEFT + GUARD
 CHUNK_IN = 72
@@ -319,7 +320,7 @@
     last, speed_y, speed_z, vigneron, coupling,
     own, from_left, from_right, from_left_two, from_right_two,
     out,
-    inf, still, base, cur, s0, s1, work_inf, delta, curve, face, rows_part, blocked, half_block, *per_block,
+    inf, still, base, cur, s0, s1, work_inf, delta, curve, face, rows_part, blocked, half_block, half_strip, strips, *per_block,
 ):
     across, delta_y, curve_y, face_y = (per_block[NVAR * i:NVAR * (i + 1)] for i in range(4))
     lane = lane_iota()
@@ -382,6 +383,20 @@
     def nth(r):
         return sum(jnp.where(rank[v] == r, v, 0) for v in range(NVAR))
 
+    turning = (STRIP * ahead + LANES - 1) // LANES * LANES
+    place_of = [
+        pl.multiple_of(
+            jnp.where(forward[v] == 1, STRIP * rank[v], turning + STRIP * (rank[v] - ahead)), 16
+        )
+        for v in range(NVAR)
+    ]
+    for b in range(4):
+        value = jnp.zeros((8, LANES), jnp.float32)
+        for v in range(NVAR):
+            at = lane + LANES * b - place_of[v]
+            value = jnp.where((at >= 0) & (at < STRIP), half_y[v], value)
+        half_strip[b] = value
+    strips[...] = jnp.zeros((4 * LANES, LANES), jnp.float32)
     lone = jnp.where(ahead % 2 == 0, NVAR - 1, 0)
     begin = 1 - jnp.minimum(lone, 1)
     couples = [(nth(begin), nth(begin + 1)), (nth(begin + 2), nth(begin + 3)), (nth(lone), nth(lone))]
@@ -445,6 +460,10 @@
 
     def blocks_of(n):
         if n > 8:
+            if n == STRIP // 8:
+                return [
+                    (half_strip[b], jnp.where(LANES * b < turning, 1, -1)) for b in range(4)
+                ]
             return list(zip(half_y, step_y))
         return [
             (half_block[b], jnp.where(speed_y[va] >= 0.0, 1, -1))
@@ -454,8 +473,15 @@
     middle = LANES // 2
     narrow = pl.ds(GUARD + 24, middle)
 
+    strip = pl.ds(GUARD + LEFT + SLAB // 2 - STRIP // 2, STRIP)
+
     def turn_in(src, n):
-        if n > 8:
+        if n == STRIP // 8:
+            for v in range(NVAR):
+                strips[pl.ds(place_of[v], STRIP), :] = src[v, strip, :]
+            for b in range(4):
+                across[b][pl.ds(GUARD, LANES), :] = strips[pl.ds(LANES * b, LANES), :].T
+        elif n > 8:
             for v in range(NVAR):
                 across[v][pl.ds(GUARD, LANES), :] = src[v, pl.ds(GUARD - 8, LANES), :].T
         else:
@@ -488,12 +514,18 @@
             change = (
                 face_y[b][pl.ds(GUARD, LANES), :] - face_y[b][pl.ds(GUARD - step, LANES), :]
             ).T
-            if n > 8:
+            if n == STRIP // 8:
+                strips[pl.ds(LANES * b, LANES), :] = change
+            elif n > 8:
                 rows_part[b] = change
             else:
                 rows = pl.ds(8 + 24, middle)
                 rows_part[couples[b][0], rows, :] = change[:middle]
                 rows_part[couples[b][1], rows, :] = change[middle:]
+        if n == STRIP // 8:
+            rows = pl.ds(8 + LEFT + SLAB // 2 - STRIP // 2, STRIP)
+            for v in range(NVAR):
+                rows_part[v, rows, :] = strips[pl.ds(place_of[v], STRIP), :]
 
     def sources(src, at):
         field = [src[v, pl.ds(at, 8), :] for v in range(NVAR)]
@@ -565,7 +597,7 @@
             def part(i, c, n=n):
                 turn_in(cur, n)
                 column_differences(cur, n)
-                column_faces(cur, octets_of(n)[:n // 2])
+                column_faces(cur, octets_of(n)[:n // 3])
                 return c
             lax.fori_loop(0, times, part, 0)
 
@@ -576,7 +608,7 @@
 
             def part(i, c, n=n):
                 turn_out(n)
-                column_faces(cur, octets_of(n)[n // 2:])
+                column_faces(cur, octets_of(n)[n // 3:])
                 steps(station, octets_of(n))
                 return c
             lax.fori_loop(0, times, part, 0)
@@ -658,6 +690,8 @@
             pltpu.VMEM((NVAR, LANES, LANES), jnp.float32),
             pltpu.VMEM((2, ROWS, LANES), jnp.float32),
             pltpu.VMEM((3, 8, LANES), jnp.float32),
+            pltpu.VMEM((4, 8, LANES), jnp.float32),
+            pltpu.VMEM((4 * LANES, LANES), jnp.float32),
         ] + [pltpu.VMEM((LANES + 2 * GUARD, LANES), jnp.float32)] * (4 * NVAR),
         compiler_params=pltpu.CompilerParams(vmem_limit_bytes=32 * 1024 * 1024),
         name="march",

time: 75.8 us -> 75.2 us (level)
  no operation moved by 1% of the time
where the time goes in v6:
time: 75.2 us; the launch traced here: 74.9 us
  Pallas kernels  30.8 us (41%)
  blocking collectives  29.1 us (39%)
  starting transfers between devices  9.65 us (13%)
  waiting for transfers between devices  5.23 us (7%)
    pallas_call x1, Pallas kernels, slabs_per_device(): pl.pallas_call(functools.partial(main_kernel, len(path) * SLAB), out_shap...  28.5 us
    all_to_all x1, blocking collectives, slabs_per_device(): got = lax.all_to_all(packed, ('sec', 'gy'), 0, 0)  17.5 us
    all_to_all x1, blocking collectives, slabs_per_device(): returned = lax.all_to_all(sent, ('sec', 'gy'), 0, 0)  11.6 us
    ppermute x4, starting transfers between devices, along(): lax.ppermute(value, mesh_axes, [(path[i], path[i + steps]) for i in range...  9.65 us
    ppermute x4, waiting for transfers between devices, along(): lax.ppermute(value, mesh_axes, [(path[i], path[i + steps]) for i in range...  5.23 us
  transfers between devices with their start and end apart: 4, of which 1 were waited for; matrix products, arithmetic and copies ran while one was open for 0% of the time, Pallas kernels for 0%

profile of v6, /device:TPU:0, one launch (start us, length us, event | category | flops | bytes accessed | tf_op | source)
XLA Modules:
  0.0 74.9 jit_solution(2802538025240537643)
XLA Ops:
  0.0 1.3 %pack.1 = f32[8,72,128]{2,1,0:T(8,128)S(1)} custom-call(f32[5,32,256]{2,1,0:T(8,128)} %inflow.1, f32[1,5,32,256]{3,2,1,0:T(8,128)} %initial.1, s32[1,32,256]{2,1,0:T(8,128)} %solid.1), custom_call_target="tpu_custom_call" | custom-call | tf_op jit(solution)/shard_map/pack/pallas_call | solution.py:655
  1.3 17.5 %all_to_all.10.got = f32[8,72,128]{2,1,0:T(8,128)S(1)} all-to-all(f32[8,72,128]{2,1,0:T(8,128)S(1)} %pack.1), channel_id=1, replica_groups=mesh['sec'=2,'gy'=4,'gz'=4] {'sec','gy'}, dimensions={0} | all-to-all | bytes 589824 | tf_op jit(solution)/shard_map/all_to_all | solution.py:667
  18.9 0.1 assemble.1
  19.0 0.0 copy-start
  19.0 2.5 %collective-permute-start = (f32[496,128]{1,0:T(8,128)S(1)}, f32[496,128]{1,0:T(8,128)S(1)}, u32[]{:S(2)}, u32[]{:S(2)}) collective-permute-start(f32[496,128]{1,0:T(8,128)S(1)} %get-tuple-element.11), channel_id=1, source_target_pairs={{0,16},{16,20},{20,4},{4,8},{8,24},{24,28},{28,12},{12,13},{13,29}... | collective-permute-start | bytes 761864 | tf_op jit(solution)/shard_map/ppermute | solution.py:649
  21.5 1.3 %collective-permute-start.1 = (f32[496,128]{1,0:T(8,128)S(1)}, f32[496,128]{1,0:T(8,128)S(1)}, u32[]{:S(2)}, u32[]{:S(2)}) collective-permute-start(f32[496,128]{1,0:T(8,128)S(1)} %get-tuple-element.12), channel_id=1, source_target_pairs={{16,0},{20,16},{4,20},{8,4},{24,8},{28,24},{12,28},{13,12},{29,13}... | collective-permute-start | bytes 761864 | tf_op jit(solution)/shard_map/ppermute | solution.py:649
  22.8 4.4 %collective-permute-start.2 = (f32[32,128]{1,0:T(8,128)S(1)}, f32[32,128]{1,0:T(8,128)S(1)}, u32[]{:S(2)}, u32[]{:S(2)}) collective-permute-start(f32[32,128]{1,0:T(8,128)S(1)} %get-tuple-element.13), channel_id=1, source_target_pairs={{0,20},{16,4},{20,8},{4,24},{8,28},{24,12},{28,13},{12,29},{13,25}... | collective-permute-start | bytes 49160 | tf_op jit(solution)/shard_map/ppermute | solution.py:649
  27.2 0.0 copy-start.1
  27.3 0.0 copy-start.2
  27.3 0.0 copy-start.3
  27.3 1.4 %collective-permute-start.3 = (f32[32,128]{1,0:T(8,128)S(1)}, f32[32,128]{1,0:T(8,128)S(1)}, u32[]{:S(2)}, u32[]{:S(2)}) collective-permute-start(f32[32,128]{1,0:T(8,128)S(1)} %get-tuple-element.14), channel_id=1, source_target_pairs={{20,0},{4,16},{8,20},{24,4},{28,8},{12,24},{13,28},{29,12},{25,13}... | collective-permute-start | bytes 49160 | tf_op jit(solution)/shard_map/ppermute | solution.py:649
  28.7 0.0 collective-permute-done.2.from_left_two
  28.7 5.2 %collective-permute-done.3.from_right_two = f32[32,128]{1,0:T(8,128)S(1)} collective-permute-done((f32[32,128]{1,0:T(8,128)S(1)}, f32[32,128]{1,0:T(8,128)S(1)}, u32[]{:S(2)}, u32[]{:S(2)}) %collective-permute-start.3) | collective-permute-done | bytes 16416 | tf_op jit(solution)/shard_map/ppermute | solution.py:649
  33.9 0.0 collective-permute-done.from_left
  33.9 0.0 collective-permute-done.1.from_right
  33.9 0.0 copy-done
  34.0 0.0 copy-done.1
  34.0 0.0 copy-done.2
  34.0 0.0 copy-done.3
  34.0 28.5 %march.1 = f32[8,40,128]{2,1,0:T(8,128)S(1)} custom-call(f32[5]{0:T(128)S(1)} %copy-done.1, f32[5]{0:T(128)S(1)} %copy-done.2, f32[5]{0:T(128)S(1)} %copy-done.3, f32[5,5]{1,0:T(8,128)S(1)} %copy-done, f32[17,32,128]{2,1,0:T(8,128)S(1)} %get-tuple-element.10.own, f32[496,128]{1,0:T(8,128)S(1)} %collective-permute-done.from_left, ...), custom_call_target="tpu_custom_call" | custom-call | tf_op jit(solution)/shard_map/march/pallas_call | solution.py:683
  62.5 11.6 %all_to_all.11.got = f32[8,40,128]{2,1,0:T(8,128)S(1)} all-to-all(f32[8,40,128]{2,1,0:T(8,128)S(1)} %march.1), channel_id=1, replica_groups=mesh['sec'=2,'gy'=4,'gz'=4] {'sec','gy'}, dimensions={0} | all-to-all | bytes 327680 | tf_op jit(solution)/shard_map/all_to_all | solution.py:702
  74.1 0.9 %unpack.1 = f32[1,5,32,256]{3,2,1,0:T(8,128)} custom-call(f32[8,40,128]{2,1,0:T(8,128)S(1)} %all_to_all.11.got), custom_call_target="tpu_custom_call" | custom-call | tf_op jit(solution)/shard_map/unpack/pallas_call | solution.py:704
Async XLA Ops:
  19.0 15.0 %copy-start = (f32[5,5]{1,0:T(8,128)S(1)}, f32[5,5]{1,0:T(8,128)}, u32[]{:S(2)}) copy-start(f32[5,5]{1,0:T(8,128)} %coupling.1) | copy-start | bytes 304
  19.0 14.9 %collective-permute-start = (f32[496,128]{1,0:T(8,128)S(1)}, f32[496,128]{1,0:T(8,128)S(1)}, u32[]{:S(2)}, u32[]{:S(2)}) collective-permute-start(f32[496,128]{1,0:T(8,128)S(1)} %get-tuple-element.11), channel_id=1, source_target_pairs={{0,16},{16,20},{20,4},{4,8},{8,24},{24,28},{28,12},{12,13},{13,29}... | collective-permute-start | bytes 761864 | tf_op jit(solution)/shard_map/ppermute | solution.py:649
  21.5 12.5 %collective-permute-start.1 = (f32[496,128]{1,0:T(8,128)S(1)}, f32[496,128]{1,0:T(8,128)S(1)}, u32[]{:S(2)}, u32[]{:S(2)}) collective-permute-start(f32[496,128]{1,0:T(8,128)S(1)} %get-tuple-element.12), channel_id=1, source_target_pairs={{16,0},{20,16},{4,20},{8,4},{24,8},{28,24},{12,28},{13,12},{29,13}... | collective-permute-start | bytes 761864 | tf_op jit(solution)/shard_map/ppermute | solution.py:649
  22.8 5.9 %collective-permute-start.2 = (f32[32,128]{1,0:T(8,128)S(1)}, f32[32,128]{1,0:T(8,128)S(1)}, u32[]{:S(2)}, u32[]{:S(2)}) collective-permute-start(f32[32,128]{1,0:T(8,128)S(1)} %get-tuple-element.13), channel_id=1, source_target_pairs={{0,20},{16,4},{20,8},{4,24},{8,28},{24,12},{28,13},{12,29},{13,25}... | collective-permute-start | bytes 49160 | tf_op jit(solution)/shard_map/ppermute | solution.py:649
  27.2 6.7 %copy-start.1 = (f32[5]{0:T(128)S(1)}, f32[5]{0:T(128)}, u32[]{:S(2)}) copy-start(f32[5]{0:T(128)} %speed_y.1) | copy-start | bytes 64
  27.3 6.7 %copy-start.2 = (f32[5]{0:T(128)S(1)}, f32[5]{0:T(128)}, u32[]{:S(2)}) copy-start(f32[5]{0:T(128)} %speed_z.1) | copy-start | bytes 64
  27.3 6.7 %copy-start.3 = (f32[5]{0:T(128)S(1)}, f32[5]{0:T(128)}, u32[]{:S(2)}) copy-start(f32[5]{0:T(128)} %vigneron.1) | copy-start | bytes 64
  27.3 6.7 %collective-permute-start.3 = (f32[32,128]{1,0:T(8,128)S(1)}, f32[32,128]{1,0:T(8,128)S(1)}, u32[]{:S(2)}, u32[]{:S(2)}) collective-permute-start(f32[32,128]{1,0:T(8,128)S(1)} %get-tuple-element.14), channel_id=1, source_target_pairs={{20,0},{4,16},{8,20},{24,4},{28,8},{12,24},{13,28},{29,12},{25,13}... | collective-permute-start | bytes 49160 | tf_op jit(solution)/shard_map/ppermute | solution.py:649

commit v7 on v6

--- a/solution.py
+++ b/solution.py
@@ -500,6 +500,12 @@
             for v in range(NVAR):
                 faces(src.at[v], half_z[v], step_z[v], delta.at[v], curve.at[v], face.at[v], at)
 
+    def entry_faces(src, n):
+        octets = octets_of(n)
+        for v in range(NVAR):
+            at = jnp.where(step_z[v] > 0, octets[0] - 8, octets[-1] + 8)
+            faces(src.at[v], half_z[v], step_z[v], delta.at[v], curve.at[v], face.at[v], at)
+
     def row_faces(n):
         for b, (half, step) in enumerate(blocks_of(n)):
             row = (across[b], half, step, delta_y[b], curve_y[b])
@@ -590,7 +596,7 @@
             pairs(g0, 14 - g0, start_of_1)
 
         station = (c >= 2).astype(jnp.int32)
-        g0 = (9 + 6 * k + 3 * c) // 8
+        g0 = jnp.minimum((10 + 6 * k + 3 * c) // 8, 4)
         for n in (12, 10, 8, 6):
             times = (g0 == 7 - n // 2).astype(jnp.int32)
 
@@ -609,6 +615,8 @@
             def part(i, c, n=n):
                 turn_out(n)
                 column_faces(cur, octets_of(n)[n // 3:])
+                if n == STRIP // 8:
+                    entry_faces(cur, n)
                 steps(station, octets_of(n))
                 return c
             lax.fori_loop(0, times, part, 0)

time: 75.2 us -> 75 us (level)
  no operation moved by 1% of the time
where the time goes in v7:
time: 75 us; the launch traced here: 74.6 us
  Pallas kernels  30.5 us (41%)
  blocking collectives  29.1 us (39%)
  starting transfers between devices  9.65 us (13%)
  waiting for transfers between devices  5.23 us (7%)
    pallas_call x1, Pallas kernels, slabs_per_device(): pl.pallas_call(functools.partial(main_kernel, len(path) * SLAB), out_shap...  28.2 us
    all_to_all x1, blocking collectives, slabs_per_device(): got = lax.all_to_all(packed, ('sec', 'gy'), 0, 0)  17.5 us
    all_to_all x1, blocking collectives, slabs_per_device(): returned = lax.all_to_all(sent, ('sec', 'gy'), 0, 0)  11.6 us
    ppermute x4, starting transfers between devices, along(): lax.ppermute(value, mesh_axes, [(path[i], path[i + steps]) for i in range...  9.65 us
    ppermute x4, waiting for transfers between devices, along(): lax.ppermute(value, mesh_axes, [(path[i], path[i + steps]) for i in range...  5.23 us
  transfers between devices with their start and end apart: 4, of which 1 were waited for; matrix products, arithmetic and copies ran while one was open for 0% of the time, Pallas kernels for 0%

profile of v7, /device:TPU:0, one launch (start us, length us, event | category | flops | bytes accessed | tf_op | source)
XLA Modules:
  0.0 74.6 jit_solution(2582874435314124446)
XLA Ops:
  0.0 1.3 %pack.1 = f32[8,72,128]{2,1,0:T(8,128)S(1)} custom-call(f32[5,32,256]{2,1,0:T(8,128)} %inflow.1, f32[1,5,32,256]{3,2,1,0:T(8,128)} %initial.1, s32[1,32,256]{2,1,0:T(8,128)} %solid.1), custom_call_target="tpu_custom_call" | custom-call | tf_op jit(solution)/shard_map/pack/pallas_call | solution.py:663
  1.3 17.5 %all_to_all.10.got = f32[8,72,128]{2,1,0:T(8,128)S(1)} all-to-all(f32[8,72,128]{2,1,0:T(8,128)S(1)} %pack.1), channel_id=1, replica_groups=mesh['sec'=2,'gy'=4,'gz'=4] {'sec','gy'}, dimensions={0} | all-to-all | bytes 589824 | tf_op jit(solution)/shard_map/all_to_all | solution.py:675
  18.9 0.1 assemble.1
  19.0 0.0 copy-start
  19.0 2.5 %collective-permute-start = (f32[496,128]{1,0:T(8,128)S(1)}, f32[496,128]{1,0:T(8,128)S(1)}, u32[]{:S(2)}, u32[]{:S(2)}) collective-permute-start(f32[496,128]{1,0:T(8,128)S(1)} %get-tuple-element.11), channel_id=1, source_target_pairs={{0,16},{16,20},{20,4},{4,8},{8,24},{24,28},{28,12},{12,13},{13,29}... | collective-permute-start | bytes 761864 | tf_op jit(solution)/shard_map/ppermute | solution.py:657
  21.5 1.3 %collective-permute-start.1 = (f32[496,128]{1,0:T(8,128)S(1)}, f32[496,128]{1,0:T(8,128)S(1)}, u32[]{:S(2)}, u32[]{:S(2)}) collective-permute-start(f32[496,128]{1,0:T(8,128)S(1)} %get-tuple-element.12), channel_id=1, source_target_pairs={{16,0},{20,16},{4,20},{8,4},{24,8},{28,24},{12,28},{13,12},{29,13}... | collective-permute-start | bytes 761864 | tf_op jit(solution)/shard_map/ppermute | solution.py:657
  22.8 4.4 %collective-permute-start.2 = (f32[32,128]{1,0:T(8,128)S(1)}, f32[32,128]{1,0:T(8,128)S(1)}, u32[]{:S(2)}, u32[]{:S(2)}) collective-permute-start(f32[32,128]{1,0:T(8,128)S(1)} %get-tuple-element.13), channel_id=1, source_target_pairs={{0,20},{16,4},{20,8},{4,24},{8,28},{24,12},{28,13},{12,29},{13,25}... | collective-permute-start | bytes 49160 | tf_op jit(solution)/shard_map/ppermute | solution.py:657
  27.2 0.0 copy-start.1
  27.3 0.0 copy-start.2
  27.3 0.0 copy-start.3
  27.3 1.4 %collective-permute-start.3 = (f32[32,128]{1,0:T(8,128)S(1)}, f32[32,128]{1,0:T(8,128)S(1)}, u32[]{:S(2)}, u32[]{:S(2)}) collective-permute-start(f32[32,128]{1,0:T(8,128)S(1)} %get-tuple-element.14), channel_id=1, source_target_pairs={{20,0},{4,16},{8,20},{24,4},{28,8},{12,24},{13,28},{29,12},{25,13}... | collective-permute-start | bytes 49160 | tf_op jit(solution)/shard_map/ppermute | solution.py:657
  28.7 0.0 collective-permute-done.2.from_left_two
  28.7 5.2 %collective-permute-done.3.from_right_two = f32[32,128]{1,0:T(8,128)S(1)} collective-permute-done((f32[32,128]{1,0:T(8,128)S(1)}, f32[32,128]{1,0:T(8,128)S(1)}, u32[]{:S(2)}, u32[]{:S(2)}) %collective-permute-start.3) | collective-permute-done | bytes 16416 | tf_op jit(solution)/shard_map/ppermute | solution.py:657
  33.9 0.0 collective-permute-done.from_left
  33.9 0.0 collective-permute-done.1.from_right
  33.9 0.0 copy-done
  34.0 0.0 copy-done.1
  34.0 0.0 copy-done.2
  34.0 0.0 copy-done.3
  34.0 28.2 %march.1 = f32[8,40,128]{2,1,0:T(8,128)S(1)} custom-call(f32[5]{0:T(128)S(1)} %copy-done.1, f32[5]{0:T(128)S(1)} %copy-done.2, f32[5]{0:T(128)S(1)} %copy-done.3, f32[5,5]{1,0:T(8,128)S(1)} %copy-done, f32[17,32,128]{2,1,0:T(8,128)S(1)} %get-tuple-element.10.own, f32[496,128]{1,0:T(8,128)S(1)} %collective-permute-done.from_left, ...), custom_call_target="tpu_custom_call" | custom-call | tf_op jit(solution)/shard_map/march/pallas_call | solution.py:691
  62.2 11.6 %all_to_all.11.got = f32[8,40,128]{2,1,0:T(8,128)S(1)} all-to-all(f32[8,40,128]{2,1,0:T(8,128)S(1)} %march.1), channel_id=1, replica_groups=mesh['sec'=2,'gy'=4,'gz'=4] {'sec','gy'}, dimensions={0} | all-to-all | bytes 327680 | tf_op jit(solution)/shard_map/all_to_all | solution.py:710
  73.8 0.9 %unpack.1 = f32[1,5,32,256]{3,2,1,0:T(8,128)} custom-call(f32[8,40,128]{2,1,0:T(8,128)S(1)} %all_to_all.11.got), custom_call_target="tpu_custom_call" | custom-call | tf_op jit(solution)/shard_map/unpack/pallas_call | solution.py:712
Async XLA Ops:
  19.0 15.0 %copy-start = (f32[5,5]{1,0:T(8,128)S(1)}, f32[5,5]{1,0:T(8,128)}, u32[]{:S(2)}) copy-start(f32[5,5]{1,0:T(8,128)} %coupling.1) | copy-start | bytes 304
  19.0 14.9 %collective-permute-start = (f32[496,128]{1,0:T(8,128)S(1)}, f32[496,128]{1,0:T(8,128)S(1)}, u32[]{:S(2)}, u32[]{:S(2)}) collective-permute-start(f32[496,128]{1,0:T(8,128)S(1)} %get-tuple-element.11), channel_id=1, source_target_pairs={{0,16},{16,20},{20,4},{4,8},{8,24},{24,28},{28,12},{12,13},{13,29}... | collective-permute-start | bytes 761864 | tf_op jit(solution)/shard_map/ppermute | solution.py:657
  21.5 12.5 %collective-permute-start.1 = (f32[496,128]{1,0:T(8,128)S(1)}, f32[496,128]{1,0:T(8,128)S(1)}, u32[]{:S(2)}, u32[]{:S(2)}) collective-permute-start(f32[496,128]{1,0:T(8,128)S(1)} %get-tuple-element.12), channel_id=1, source_target_pairs={{16,0},{20,16},{4,20},{8,4},{24,8},{28,24},{12,28},{13,12},{29,13}... | collective-permute-start | bytes 761864 | tf_op jit(solution)/shard_map/ppermute | solution.py:657
  22.8 5.9 %collective-permute-start.2 = (f32[32,128]{1,0:T(8,128)S(1)}, f32[32,128]{1,0:T(8,128)S(1)}, u32[]{:S(2)}, u32[]{:S(2)}) collective-permute-start(f32[32,128]{1,0:T(8,128)S(1)} %get-tuple-element.13), channel_id=1, source_target_pairs={{0,20},{16,4},{20,8},{4,24},{8,28},{24,12},{28,13},{12,29},{13,25}... | collective-permute-start | bytes 49160 | tf_op jit(solution)/shard_map/ppermute | solution.py:657
  27.2 6.7 %copy-start.1 = (f32[5]{0:T(128)S(1)}, f32[5]{0:T(128)}, u32[]{:S(2)}) copy-start(f32[5]{0:T(128)} %speed_y.1) | copy-start | bytes 64
  27.3 6.7 %copy-start.2 = (f32[5]{0:T(128)S(1)}, f32[5]{0:T(128)}, u32[]{:S(2)}) copy-start(f32[5]{0:T(128)} %speed_z.1) | copy-start | bytes 64
  27.3 6.7 %copy-start.3 = (f32[5]{0:T(128)S(1)}, f32[5]{0:T(128)}, u32[]{:S(2)}) copy-start(f32[5]{0:T(128)} %vigneron.1) | copy-start | bytes 64
  27.3 6.7 %collective-permute-start.3 = (f32[32,128]{1,0:T(8,128)S(1)}, f32[32,128]{1,0:T(8,128)S(1)}, u32[]{:S(2)}, u32[]{:S(2)}) collective-permute-start(f32[32,128]{1,0:T(8,128)S(1)} %get-tuple-element.14), channel_id=1, source_target_pairs={{20,0},{4,16},{8,20},{24,4},{28,8},{12,24},{13,28},{29,12},{25,13}... | collective-permute-start | bytes 49160 | tf_op jit(solution)/shard_map/ppermute | solution.py:657

commit v8 on v7

--- a/solution.py
+++ b/solution.py
@@ -596,8 +596,8 @@
             pairs(g0, 14 - g0, start_of_1)
 
         station = (c >= 2).astype(jnp.int32)
-        g0 = jnp.minimum((10 + 6 * k + 3 * c) // 8, 4)
-        for n in (12, 10, 8, 6):
+        g0 = (10 + 6 * k + 3 * c) // 8
+        for n in (12, 10, 8, 6, 4):
             times = (g0 == 7 - n // 2).astype(jnp.int32)
 
             def part(i, c, n=n):
@@ -615,7 +615,7 @@
             def part(i, c, n=n):
                 turn_out(n)
                 column_faces(cur, octets_of(n)[n // 3:])
-                if n == STRIP // 8:
+                if n in (STRIP // 8, SLAB // 8):
                     entry_faces(cur, n)
                 steps(station, octets_of(n))
                 return c

time: 75 us -> 75.2 us (level)
  no operation moved by 1% of the time
where the time goes in v8:
time: 75.2 us; the launch traced here: 74.9 us
  Pallas kernels  30.8 us (41%)
  blocking collectives  29.1 us (39%)
  starting transfers between devices  9.65 us (13%)
  waiting for transfers between devices  5.23 us (7%)
    pallas_call x1, Pallas kernels, slabs_per_device(): pl.pallas_call(functools.partial(main_kernel, len(path) * SLAB), out_shap...  28.5 us
    all_to_all x1, blocking collectives, slabs_per_device(): got = lax.all_to_all(packed, ('sec', 'gy'), 0, 0)  17.5 us
    all_to_all x1, blocking collectives, slabs_per_device(): returned = lax.all_to_all(sent, ('sec', 'gy'), 0, 0)  11.6 us
    ppermute x4, starting transfers between devices, along(): lax.ppermute(value, mesh_axes, [(path[i], path[i + steps]) for i in range...  9.65 us
    ppermute x4, waiting for transfers between devices, along(): lax.ppermute(value, mesh_axes, [(path[i], path[i + steps]) for i in range...  5.23 us
  transfers between devices with their start and end apart: 4, of which 1 were waited for; matrix products, arithmetic and copies ran while one was open for 0% of the time, Pallas kernels for 0%

profile of v8, /device:TPU:0, one launch (start us, length us, event | category | flops | bytes accessed | tf_op | source)
XLA Modules:
  0.0 74.9 jit_solution(7824901146351416039)
XLA Ops:
  0.0 1.3 %pack.1 = f32[8,72,128]{2,1,0:T(8,128)S(1)} custom-call(f32[5,32,256]{2,1,0:T(8,128)} %inflow.1, f32[1,5,32,256]{3,2,1,0:T(8,128)} %initial.1, s32[1,32,256]{2,1,0:T(8,128)} %solid.1), custom_call_target="tpu_custom_call" | custom-call | tf_op jit(solution)/shard_map/pack/pallas_call | solution.py:663
  1.3 17.5 %all_to_all.10.got = f32[8,72,128]{2,1,0:T(8,128)S(1)} all-to-all(f32[8,72,128]{2,1,0:T(8,128)S(1)} %pack.1), channel_id=1, replica_groups=mesh['sec'=2,'gy'=4,'gz'=4] {'sec','gy'}, dimensions={0} | all-to-all | bytes 589824 | tf_op jit(solution)/shard_map/all_to_all | solution.py:675
  18.9 0.1 assemble.1
  19.0 0.0 copy-start
  19.0 2.5 %collective-permute-start = (f32[496,128]{1,0:T(8,128)S(1)}, f32[496,128]{1,0:T(8,128)S(1)}, u32[]{:S(2)}, u32[]{:S(2)}) collective-permute-start(f32[496,128]{1,0:T(8,128)S(1)} %get-tuple-element.11), channel_id=1, source_target_pairs={{0,16},{16,20},{20,4},{4,8},{8,24},{24,28},{28,12},{12,13},{13,29}... | collective-permute-start | bytes 761864 | tf_op jit(solution)/shard_map/ppermute | solution.py:657
  21.5 1.3 %collective-permute-start.1 = (f32[496,128]{1,0:T(8,128)S(1)}, f32[496,128]{1,0:T(8,128)S(1)}, u32[]{:S(2)}, u32[]{:S(2)}) collective-permute-start(f32[496,128]{1,0:T(8,128)S(1)} %get-tuple-element.12), channel_id=1, source_target_pairs={{16,0},{20,16},{4,20},{8,4},{24,8},{28,24},{12,28},{13,12},{29,13}... | collective-permute-start | bytes 761864 | tf_op jit(solution)/shard_map/ppermute | solution.py:657
  22.8 4.4 %collective-permute-start.2 = (f32[32,128]{1,0:T(8,128)S(1)}, f32[32,128]{1,0:T(8,128)S(1)}, u32[]{:S(2)}, u32[]{:S(2)}) collective-permute-start(f32[32,128]{1,0:T(8,128)S(1)} %get-tuple-element.13), channel_id=1, source_target_pairs={{0,20},{16,4},{20,8},{4,24},{8,28},{24,12},{28,13},{12,29},{13,25}... | collective-permute-start | bytes 49160 | tf_op jit(solution)/shard_map/ppermute | solution.py:657
  27.2 0.0 copy-start.1
  27.3 0.0 copy-start.2
  27.3 0.0 copy-start.3
  27.3 1.4 %collective-permute-start.3 = (f32[32,128]{1,0:T(8,128)S(1)}, f32[32,128]{1,0:T(8,128)S(1)}, u32[]{:S(2)}, u32[]{:S(2)}) collective-permute-start(f32[32,128]{1,0:T(8,128)S(1)} %get-tuple-element.14), channel_id=1, source_target_pairs={{20,0},{4,16},{8,20},{24,4},{28,8},{12,24},{13,28},{29,12},{25,13}... | collective-permute-start | bytes 49160 | tf_op jit(solution)/shard_map/ppermute | solution.py:657
  28.7 0.0 collective-permute-done.2.from_left_two
  28.7 5.2 %collective-permute-done.3.from_right_two = f32[32,128]{1,0:T(8,128)S(1)} collective-permute-done((f32[32,128]{1,0:T(8,128)S(1)}, f32[32,128]{1,0:T(8,128)S(1)}, u32[]{:S(2)}, u32[]{:S(2)}) %collective-permute-start.3) | collective-permute-done | bytes 16416 | tf_op jit(solution)/shard_map/ppermute | solution.py:657
  33.9 0.0 collective-permute-done.from_left
  33.9 0.0 collective-permute-done.1.from_right
  33.9 0.0 copy-done
  34.0 0.0 copy-done.1
  34.0 0.0 copy-done.2
  34.0 0.0 copy-done.3
  34.0 28.5 %march.1 = f32[8,40,128]{2,1,0:T(8,128)S(1)} custom-call(f32[5]{0:T(128)S(1)} %copy-done.1, f32[5]{0:T(128)S(1)} %copy-done.2, f32[5]{0:T(128)S(1)} %copy-done.3, f32[5,5]{1,0:T(8,128)S(1)} %copy-done, f32[17,32,128]{2,1,0:T(8,128)S(1)} %get-tuple-element.10.own, f32[496,128]{1,0:T(8,128)S(1)} %collective-permute-done.from_left, ...), custom_call_target="tpu_custom_call" | custom-call | tf_op jit(solution)/shard_map/march/pallas_call | solution.py:691
  62.5 11.6 %all_to_all.11.got = f32[8,40,128]{2,1,0:T(8,128)S(1)} all-to-all(f32[8,40,128]{2,1,0:T(8,128)S(1)} %march.1), channel_id=1, replica_groups=mesh['sec'=2,'gy'=4,'gz'=4] {'sec','gy'}, dimensions={0} | all-to-all | bytes 327680 | tf_op jit(solution)/shard_map/all_to_all | solution.py:710
  74.0 0.9 %unpack.1 = f32[1,5,32,256]{3,2,1,0:T(8,128)} custom-call(f32[8,40,128]{2,1,0:T(8,128)S(1)} %all_to_all.11.got), custom_call_target="tpu_custom_call" | custom-call | tf_op jit(solution)/shard_map/unpack/pallas_call | solution.py:712
Async XLA Ops:
  19.0 15.0 %copy-start = (f32[5,5]{1,0:T(8,128)S(1)}, f32[5,5]{1,0:T(8,128)}, u32[]{:S(2)}) copy-start(f32[5,5]{1,0:T(8,128)} %coupling.1) | copy-start | bytes 304
  19.0 14.9 %collective-permute-start = (f32[496,128]{1,0:T(8,128)S(1)}, f32[496,128]{1,0:T(8,128)S(1)}, u32[]{:S(2)}, u32[]{:S(2)}) collective-permute-start(f32[496,128]{1,0:T(8,128)S(1)} %get-tuple-element.11), channel_id=1, source_target_pairs={{0,16},{16,20},{20,4},{4,8},{8,24},{24,28},{28,12},{12,13},{13,29}... | collective-permute-start | bytes 761864 | tf_op jit(solution)/shard_map/ppermute | solution.py:657
  21.5 12.5 %collective-permute-start.1 = (f32[496,128]{1,0:T(8,128)S(1)}, f32[496,128]{1,0:T(8,128)S(1)}, u32[]{:S(2)}, u32[]{:S(2)}) collective-permute-start(f32[496,128]{1,0:T(8,128)S(1)} %get-tuple-element.12), channel_id=1, source_target_pairs={{16,0},{20,16},{4,20},{8,4},{24,8},{28,24},{12,28},{13,12},{29,13}... | collective-permute-start | bytes 761864 | tf_op jit(solution)/shard_map/ppermute | solution.py:657
  22.8 5.9 %collective-permute-start.2 = (f32[32,128]{1,0:T(8,128)S(1)}, f32[32,128]{1,0:T(8,128)S(1)}, u32[]{:S(2)}, u32[]{:S(2)}) collective-permute-start(f32[32,128]{1,0:T(8,128)S(1)} %get-tuple-element.13), channel_id=1, source_target_pairs={{0,20},{16,4},{20,8},{4,24},{8,28},{24,12},{28,13},{12,29},{13,25}... | collective-permute-start | bytes 49160 | tf_op jit(solution)/shard_map/ppermute | solution.py:657
  27.2 6.7 %copy-start.1 = (f32[5]{0:T(128)S(1)}, f32[5]{0:T(128)}, u32[]{:S(2)}) copy-start(f32[5]{0:T(128)} %speed_y.1) | copy-start | bytes 64
  27.3 6.7 %copy-start.2 = (f32[5]{0:T(128)S(1)}, f32[5]{0:T(128)}, u32[]{:S(2)}) copy-start(f32[5]{0:T(128)} %speed_z.1) | copy-start | bytes 64
  27.3 6.7 %copy-start.3 = (f32[5]{0:T(128)S(1)}, f32[5]{0:T(128)}, u32[]{:S(2)}) copy-start(f32[5]{0:T(128)} %vigneron.1) | copy-start | bytes 64
  27.3 6.7 %collective-permute-start.3 = (f32[32,128]{1,0:T(8,128)S(1)}, f32[32,128]{1,0:T(8,128)S(1)}, u32[]{:S(2)}, u32[]{:S(2)}) collective-permute-start(f32[32,128]{1,0:T(8,128)S(1)} %get-tuple-element.14), channel_id=1, source_target_pairs={{20,0},{4,16},{8,20},{24,4},{28,8},{12,24},{13,28},{29,12},{25,13}... | collective-permute-start | bytes 49160 | tf_op jit(solution)/shard_map/ppermute | solution.py:657
